TPU v7x, 256 devices: a whole 4x4x8 slice. The times are simulated.
256 devices in a mesh: section: 16 (over x, y), tile: 16 (over z, core).
Axes of the slice: x: 4, y: 4, z: 8, core: 2. Of those that a mesh axis runs over, the one named last changes fastest.
Arguments:
- checkpoint: float32 [16, 128, 32768], P('section', None, 'tile'), may hold values from -5 to 5
- prior_llr: float32 [32768], P('tile'), may hold values from 0.5 to 3
- retention: float32 [32768], P('tile'), may hold values from 0 to 1
- syndrome: int32 [128, 32768], P(None, 'tile'), may hold values 0 or 1
- labels: int32 [128, 32768], P(None, 'tile'), may hold values 0 or 1
- tile_cols: int32 [768], P('tile'), may hold values from 0 to 17, as said below
- tile_count: int32 [16], P('tile'), may hold values from 24 to 48, as said below
- pattern: int32 [768, 128, 128], P('tile'), may hold values 0 or 1
- gate_weight: float32 [768], P('tile'), may hold values from 0.1 to 0.4
- msg_weight: float32 [768], P('tile'), may hold values from 0.5 to 1.5
Outputs:
- input_grads: float32 [16, 128, 32768], P('section', None, 'tile')
- gate_grads: float32 [768], P('tile')
- msg_grads: float32 [768], P('tile')
- prior_grads: float32 [32768], P('tile')
Inputs may be any that keep to these rules, and one draw needn't show every extreme that they name: `tile_cols`: entries name a block of the shard's extended variable range: 0 is the last block of the shard before, 17 the first block of the shard after. Live slots of a shard are its first tile_count slots.
All inputs are finite; a program needn't handle non-finite values. No bound on the sum of `syndrome` or of `labels` or of `pattern` on one device may be relied on, other than what follows from the above.
Results may differ from a plain program's by a relative error of at most 0.0075.
Values may be sent and summed in bfloat16 or wider, within the bound.
No kernel may reach another device: no remote copies, remote signals or barrier semaphores. Data moves between devices by JAX's collectives and lax.ppermute only.
A program may use at most 64 MiB of HBM per device.

v0:
```python
import functools

import jax
import jax.numpy as jnp
from jax import lax
from jax.experimental import pallas as pl
from jax.experimental.pallas import tpu as pltpu
from jax.sharding import PartitionSpec as P

BLK = 128
NB = 16
EXT = NB + 2
TPC = 3
TILES = NB * TPC
SEC = 16
SH = 8
GRAD_LANES = 640
LANES = NB * BLK
VMEM_LIMIT = 8 * 1024 * 1024
PREP_ROWS = 4
F32 = jnp.float32
BF16 = jnp.bfloat16
VSPEC = pl.BlockSpec(memory_space=pltpu.VMEM)
SSPEC = pl.BlockSpec(memory_space=pltpu.SMEM)

CORE_PAIRS = [(i, i ^ 1) for i in range(16)]
Z_PAIRS = [(i, (i + 1) % 16 if i % 2 else (i - 1) % 16) for i in range(16)]


def nn(a, b):
    return lax.dot_general(a, b, (((1,), (0,)), ((), ())), preferred_element_type=F32)


def call(body, outs, args, n_smem, scratch=(), flops=0, bytes_accessed=0):
    return pl.pallas_call(
        body,
        out_shape=outs,
        in_specs=[SSPEC] * n_smem + [VSPEC] * (len(args) - n_smem),
        out_specs=[VSPEC] * len(outs),
        scratch_shapes=list(scratch),
        compiler_params=pltpu.CompilerParams(vmem_limit_bytes=VMEM_LIMIT),
        cost_estimate=pl.CostEstimate(flops=flops, bytes_accessed=bytes_accessed, transcendentals=0),
    )(*args)


def send_edges(acc_ref, ints, sendc, sendz):
    sendc[0] = acc_ref[NB]
    sendc[1] = acc_ref[ints[TILES]]
    sendz[0] = acc_ref[NB + 1]
    sendz[1] = acc_ref[ints[TILES + 1]]


def received(acc_ref, block, recvc, recvz, floats):
    own = acc_ref[block]
    even = floats[2 * TILES]
    zmask = floats[2 * TILES + 1]
    if block == 0:
        return own + (recvz[0] * (zmask * even) + recvc[0] * (1.0 - even))
    if block == NB - 1:
        return own + (recvz[0] * (zmask * (1.0 - even)) + recvc[0] * even)
    if block == NB:
        return own + recvc[1]
    if block == NB + 1:
        return (own + recvz[1]) * zmask
    return own


def forward_body(ints, floats, marg, by_check, by_var, signs, th_out, u_out, gv_out, sendc, sendz, tb):
    zmask = floats[2 * TILES + 1]
    for block in range(EXT):
        th = jnp.tanh(0.5 * marg[:, block * BLK : (block + 1) * BLK])
        if block == NB + 1:
            th = th * zmask
        th_out[block] = th
        tb[block] = th.astype(BF16)
    gv_out[...] = jnp.zeros_like(gv_out)
    for row in range(NB):
        total = None
        for slot in range(TPC):
            tile = slot * NB + row
            part = nn(tb[ints[tile]], by_var[row, slot * BLK : (slot + 1) * BLK, :]) * floats[tile]
            total = part if total is None else total + part
        sign = signs[:, row * BLK : (row + 1) * BLK]
        soft = jnp.tanh(total).reshape(SEC, SH, BLK) * sign[None]
        u_out[row] = soft.reshape(SEC * SH, BLK)
    for row in range(NB):
        parts = nn(u_out[row, (SEC - 1) * SH :, :].astype(BF16), by_check[row])
        for slot in range(TPC):
            tile = slot * NB + row
            gv_out[ints[tile]] += parts[:, slot * BLK : (slot + 1) * BLK] * floats[TILES + tile]
    send_edges(gv_out, ints, sendc, sendz)


def backward_rows(ints, floats, section, u_ref, signs, by_check, by_var, qs, dz_out, acc_out):
    acc_out[...] = jnp.zeros_like(acc_out)
    for row in range(NB):
        tiles = [slot * NB + row for slot in range(TPC)]
        scaled = [(qs[ints[tile]] * floats[TILES + tile]).astype(BF16) for tile in tiles]
        total = nn(jnp.concatenate(scaled, axis=1), by_var[row])
        u = u_ref[row, section * SH : (section + 1) * SH, :]
        sign = signs[:, row * BLK : (row + 1) * BLK]
        dz_out[row] = (total * sign * (1.0 - u * u)).astype(BF16).astype(F32)
    for row in range(NB):
        parts = nn(dz_out[row].astype(BF16), by_check[row])
        for slot in range(TPC):
            tile = slot * NB + row
            acc_out[ints[tile]] += parts[:, slot * BLK : (slot + 1) * BLK] * floats[tile]


def first_body(ints, floats, marg, gv, recvc, recvz, ret, prior, labels, u_ref, signs, by_check,
               by_var, g_out, q_out, dz_out, acc_out, sendc, sendz):
    zmask = floats[2 * TILES + 1]
    for block in range(EXT):
        lanes = slice(block * BLK, (block + 1) * BLK)
        r = ret[0:1, lanes]
        message = received(gv, block, recvc, recvz, floats)
        level = marg[(SEC - 1) * SH :, lanes]
        f = r * level + (1.0 - r) * (prior[0:1, lanes] + message)
        y = labels[:, lanes]
        g = y * jax.nn.sigmoid(f) - (1.0 - y) * jax.nn.sigmoid(-f)
        if block == NB + 1:
            g = g * zmask
        g_out[block] = g
        q_out[block] = (1.0 - r) * g
    backward_rows(ints, floats, SEC - 1, u_ref, signs, by_check, by_var, q_out, dz_out, acc_out)
    send_edges(acc_out, ints, sendc, sendz)


def next_gradient(section, g_in, acc_in, recvc, recvz, th_ref, ret, floats, block):
    r = ret[0:1, block * BLK : (block + 1) * BLK]
    th = th_ref[block, section * SH : (section + 1) * SH, :]
    down = received(acc_in, block, recvc, recvz, floats)
    return r * g_in[block] + 0.5 * down * (1.0 - th * th)


def step_body(section, ints, floats, g_in, acc_in, recvc, recvz, ret, th_ref, u_ref, signs, by_check,
              by_var, g_out, q_out, dz_out, acc_out, sendc, sendz):
    for block in range(EXT):
        g = next_gradient(section + 1, g_in, acc_in, recvc, recvz, th_ref, ret, floats, block)
        g_out[block] = g
        r = ret[0:1, block * BLK : (block + 1) * BLK]
        q_out[block] = (1.0 - r) * g
    backward_rows(ints, floats, section, u_ref, signs, by_check, by_var, q_out, dz_out, acc_out)
    send_edges(acc_out, ints, sendc, sendz)


def weights_body(section_high, count, ints, *refs):
    th_ref, u_ref, by_check, gate_in, msg_in = refs[:5]
    q_refs = refs[5 : 5 + count]
    dz_refs = refs[5 + count : 5 + 2 * count]
    gate_out, msg_out = refs[5 + 2 * count :]
    first = (section_high - count + 1) * SH
    rows = slice(first, first + count * SH)
    for row in range(NB):
        dz = jnp.concatenate([ref[row] for ref in dz_refs], axis=0).astype(BF16)
        gates = nn(dz, by_check[row])
        msgs = nn(u_ref[row, rows, :].astype(BF16), by_check[row])
        for slot in range(TPC):
            tile = slot * NB + row
            lanes = slice(slot * BLK, (slot + 1) * BLK)
            column = ints[tile]
            gate = gates[:, lanes] * th_ref[column, rows, :].astype(BF16).astype(F32)
            gate_out[tile] = gate_in[tile] + jnp.sum(gate.reshape(count, SH, BLK), axis=0)
            q = jnp.concatenate([ref[column] for ref in q_refs], axis=0).astype(BF16).astype(F32)
            msg = msgs[:, lanes] * q
            msg_out[tile] = msg_in[tile] + jnp.sum(msg.reshape(count, SH, BLK), axis=0)


def prepare_body(pattern, by_check, by_var):
    for row in range(PREP_ROWS):
        for slot in range(TPC):
            lanes = slice(slot * BLK, (slot + 1) * BLK)
            tile = pattern[slot, row].astype(F32)
            by_check[row, :, lanes] = tile.astype(BF16)
            by_var[row, lanes, :] = tile.T.astype(BF16)


def prepare(pattern):
    return pl.pallas_call(
        prepare_body,
        grid=(NB // PREP_ROWS,),
        in_specs=[pl.BlockSpec((TPC, PREP_ROWS, BLK, BLK), lambda i: (0, i, 0, 0))],
        out_specs=[
            pl.BlockSpec((PREP_ROWS, BLK, TPC * BLK), lambda i: (i, 0, 0)),
            pl.BlockSpec((PREP_ROWS, TPC * BLK, BLK), lambda i: (i, 0, 0)),
        ],
        out_shape=[
            jax.ShapeDtypeStruct((NB, BLK, TPC * BLK), BF16),
            jax.ShapeDtypeStruct((NB, TPC * BLK, BLK), BF16),
        ],
        compiler_params=pltpu.CompilerParams(vmem_limit_bytes=VMEM_LIMIT),
        cost_estimate=pl.CostEstimate(flops=10**9, bytes_accessed=6 * 2**20, transcendentals=0),
    )(pattern.reshape(TPC, NB, BLK, BLK))


def split(value):
    high = value.astype(BF16).astype(F32)
    return high, value - high


def pack_body(floats, acc_in, recvc, recvz, ret, th_ref, gate, msg, *refs):
    g_refs = refs[:SEC]
    out = refs[SEC]
    for block in range(NB):
        lanes = slice(block * BLK, (block + 1) * BLK)
        entering = [next_gradient(0, g_refs[0], acc_in, recvc, recvz, th_ref, ret, floats, block)]
        entering += [g_refs[section][block] for section in range(SEC - 1)]
        for pair in range(SEC // 2):
            both = jnp.concatenate(entering[2 * pair : 2 * pair + 2], axis=0)
            out[pair * 2 * SH : (pair + 1) * 2 * SH, lanes] = both.astype(BF16)
    priors = []
    for block in range(NB):
        total = g_refs[0][block]
        for section in range(1, SEC):
            total = total + g_refs[section][block]
        r = ret[0:1, block * BLK : (block + 1) * BLK]
        priors.append((1.0 - r) * jnp.sum(total, axis=0, keepdims=True))
    prior_high, prior_low = [], []
    for half in range(2):
        high, low = split(jnp.concatenate(priors[half * SH : (half + 1) * SH], axis=0))
        prior_high.append(high)
        prior_low.append(low)
    gate_rows = jnp.sum(gate[...], axis=1)
    msg_rows = jnp.sum(msg[...], axis=1)
    gate_sum = jnp.sum(gate_rows, axis=1, keepdims=True)
    msg_sum = jnp.sum(msg_rows, axis=1, keepdims=True)
    tile_index = lax.broadcasted_iota(jnp.int32, (TILES, BLK), 0)
    lane_index = lax.broadcasted_iota(jnp.int32, (TILES, BLK), 1)
    merged = jnp.where(tile_index == lane_index, gate_sum, 0.0) + jnp.where(
        tile_index + TILES == lane_index, msg_sum, 0.0
    )
    high, low = split(jnp.sum(merged, axis=0, keepdims=True))
    weights = jnp.concatenate([high, low, jnp.zeros((SH - 2, BLK), F32)], axis=0)
    for index, value in enumerate(prior_high + prior_low + [weights]):
        doubled = jnp.concatenate([value, value], axis=0).astype(BF16)
        lanes = slice(LANES + index * BLK, LANES + (index + 1) * BLK)
        for pair in range(SEC // 2):
            out[pair * 2 * SH : (pair + 1) * 2 * SH, lanes] = doubled


def on_device(
    checkpoint,
    prior_llr,
    retention,
    syndrome,
    labels,
    tile_cols,
    tile_count,
    pattern,
    gate_weight,
    msg_weight,
):
    shard = lax.axis_index("tile")
    group = lax.axis_index("section")
    even = shard % 2 == 0
    has_z = jnp.logical_and(shard != 0, shard != SEC - 1)

    def own_edges(x):
        first, last = x[..., :BLK], x[..., -BLK:]
        return jnp.where(even, last, first), jnp.where(even, first, last)

    def exchange(core, z):
        return lax.ppermute(core, "tile", CORE_PAIRS), lax.ppermute(z, "tile", Z_PAIRS)

    levels = checkpoint[0]
    my_labels = lax.dynamic_slice_in_dim(labels, group * SH, SH, 0).astype(F32)
    my_signs = 1.0 - 2.0 * lax.dynamic_slice_in_dim(syndrome, group * SH, SH, 0).astype(F32)
    fixed = jnp.stack([prior_llr, retention])
    edges = [own_edges(x) for x in (levels, my_labels, fixed)]
    pad = jnp.zeros((SH - 2, BLK), F32)
    halo_core, halo_z = exchange(
        jnp.concatenate([e[0] for e in edges] + [pad], axis=0),
        jnp.concatenate([e[1] for e in edges] + [pad], axis=0),
    )

    slots = jnp.arange(TILES, dtype=jnp.int32)
    live = (slots < tile_count[0]).astype(F32)
    low_slot = jnp.where(even, NB + 1, NB)
    high_slot = jnp.where(even, NB, NB + 1)
    columns = jnp.where(
        tile_cols == 0, low_slot, jnp.where(tile_cols == NB + 1, high_slot, tile_cols - 1)
    )
    core_side = jnp.where(even, NB - 1, 0)
    z_side = jnp.where(even, 0, NB - 1)
    ints = jnp.concatenate([columns, core_side[None], z_side[None]]).astype(jnp.int32)
    floats = jnp.concatenate(
        [gate_weight * live, msg_weight * live, jnp.stack([even, has_z]).astype(F32)]
    )
    shots = SEC * SH
    halo = jnp.concatenate([halo_core, halo_z], axis=1)
    labels_ext = jnp.concatenate([my_labels, halo[shots : shots + SH]], axis=1)
    fixed_ext = jnp.concatenate([fixed, halo[shots + SH : shots + SH + 2]], axis=1)
    prior_ext, ret_ext = fixed_ext[0:1], fixed_ext[1:2]
    sent = jnp.concatenate([levels, halo[:shots]], axis=1).astype(jnp.float16)
    sent = sent.reshape(SEC, SH, EXT * BLK)
    patterns = prepare(pattern)
    marg = lax.all_to_all(sent, "section", 0, 0, tiled=True)
    marg = marg.reshape(SEC * SH, EXT * BLK).astype(F32)

    def shape(*dims, dtype=F32):
        return jax.ShapeDtypeStruct(dims, dtype)

    edge = shape(2, SH, BLK)
    field = shape(EXT, SH, BLK)
    rows = shape(NB, SH, BLK)
    th, u, gv, core, z = call(
        forward_body,
        [shape(EXT, SEC * SH, BLK), shape(NB, SEC * SH, BLK), field, edge, edge],
        [ints, floats, marg, *patterns, my_signs],
        2,
        scratch=[pltpu.VMEM((EXT, SEC * SH, BLK), BF16)],
    )
    core, z = exchange(core, z)
    g, q, dz, acc, core, z = call(
        first_body,
        [field, field, rows, field, edge, edge],
        [ints, floats, marg, gv, core, z, ret_ext, prior_ext, labels_ext, u, my_signs, *patterns],
        2,
    )
    leaving = {SEC - 1: g}
    saved = [(q, dz)]
    gate = jnp.zeros((TILES, SH, BLK), F32)
    msg = jnp.zeros((TILES, SH, BLK), F32)
    group_size = 4
    for section in reversed(range(SEC - 1)):
        core, z = exchange(core, z)
        if not saved:
            core, z, gate, msg = lax.optimization_barrier((core, z, gate, msg))
        g, q, dz, acc, core, z = call(
            functools.partial(step_body, section),
            [field, field, rows, field, edge, edge],
            [ints, floats, g, acc, core, z, ret_ext, th, u, my_signs, *patterns],
            2,
        )
        leaving[section] = g
        saved.append((q, dz))
        if len(saved) == group_size:
            saved = saved[::-1]
            gate, msg = call(
                functools.partial(weights_body, section + group_size - 1, group_size),
                [shape(TILES, SH, BLK)] * 2,
                [ints, th, u, patterns[0], gate, msg] + [s[0] for s in saved] + [s[1] for s in saved],
                1,
                flops=2 * 2 * group_size * SH * TILES * BLK * BLK,
                bytes_accessed=4 * 2**20,
            )
            saved = []
    core, z = exchange(core, z)
    (packed,) = call(
        pack_body,
        [shape(SEC * SH, LANES + GRAD_LANES, dtype=BF16)],
        [floats, acc, core, z, ret_ext, th, gate, msg] + [leaving[s] for s in range(SEC)],
        1,
    )
    got = lax.all_to_all(packed.reshape(SEC, SH, LANES + GRAD_LANES), "section", 0, 0, tiled=True)
    grads = jnp.sum(got[:, :, LANES:].astype(F32), axis=0)
    prior = (grads[:, : 2 * BLK] + grads[:, 2 * BLK : 4 * BLK]).reshape(SH, 2, BLK)
    prior = prior.transpose(1, 0, 2).reshape(LANES)
    weights = grads[0, 4 * BLK :] + grads[1, 4 * BLK :]
    input_grads = got[:, :, :LANES].astype(F32).reshape(1, SEC * SH, LANES)
    return input_grads, weights[:TILES] * live, weights[TILES : 2 * TILES] * live, prior


def solution(mesh):
    placed = (
        P("section", None, "tile"),
        P("tile"),
        P("tile"),
        P(None, "tile"),
        P(None, "tile"),
        P("tile"),
        P("tile"),
        P("tile", None, None),
        P("tile"),
        P("tile"),
    )
    return jax.shard_map(
        on_device,
        mesh=mesh,
        in_specs=placed,
        out_specs=(P("section", None, "tile"), P("tile"), P("tile"), P("tile")),
        check_vma=False,
    )
```

profile of v0, /device:TPU:1, one launch (start us, length us, event | category | flops | bytes accessed | tf_op | source)
XLA Modules:
  0.0 152.5 jit_solution(15696134275893845822)
XLA Ops:
  3.3 3.3 %collective-permute-start = (f32[144,128]{1,0:T(8,128)S(1)}, f32[144,128]{1,0:T(8,128)}, u32[]{:S(2)}, u32[]{:S(2)}) collective-permute-start(f32[144,128]{1,0:T(8,128)S(1)} %get-tuple-element.260), channel_id=1, source_target_pairs={{0,1},{1,0},{2,3},{3,2},{4,5},{5,4},{6,7},{7,6},{8,9},{9,8},{10,11... | collective-permute-start | bytes 221192 | tf_op jit(solution)/shard_map/ppermute | solution.py:263
  6.6 2.1 %convert_bitcast_fusion = f16[16,8,2048]{2,1,0:T(8,128)(2,1)} fusion(f32[1,128,2048]{2,1,0:T(8,128)} %param.10), kind=kLoop, calls=%fused_computation.4 | loop fusion | flops 262144 | bytes 1572864 | tf_op jit(solution)/shard_map/concatenate | solution.py:294
  10.5 1.9 %copy-done = s32[48,128,128]{2,1,0:T(8,128)S(1)} copy-done((s32[48,128,128]{2,1,0:T(8,128)S(1)}, s32[48,128,128]{2,1,0:T(8,128)}, u32[]{:S(2)}) %copy-start) | copy-done | bytes 3145752
  12.4 1.0 shard_map.129
  15.3 6.7 %all-to-all-start = ((f16[16,8,2304]{2,1,0:T(8,128)(2,1)}), f16[16,8,2304]{2,1,0:T(8,128)(2,1)}, u32[]{:S(2)}, u32[]{:S(2)}) async-start(f16[16,8,2304]{2,1,0:T(8,128)(2,1)} %pad_maximum_fusion), calls=%async_computation | async-start | bytes 1179648 | tf_op jit(solution)/shard_map/all_to_all | solution.py:297
  22.1 9.3 %all-to-all-done = f16[16,8,2304]{2,1,0:T(8,128)(2,1)} async-done(((f16[16,8,2304]{2,1,0:T(8,128)(2,1)}), f16[16,8,2304]{2,1,0:T(8,128)(2,1)}, u32[]{:S(2)}, u32[]{:S(2)}) %all-to-all-start) | async-done | bytes 589856 | tf_op jit(solution)/shard_map/all_to_all | solution.py:297
  31.4 1.1 bitcast_convert_fusion.marg
  32.5 1.5 %shard_map.130 = (f32[18,128,128]{2,1,0:T(8,128)S(1)}, f32[16,128,128]{2,1,0:T(8,128)S(1)}, f32[18,8,128]{2,1,0:T(8,128)S(1)}, f32[2,8,128]{2,1,0:T(8,128)S(1)}, f32[2,8,128]{2,1,0:T(8,128)S(1)}) custom-call(s32[50]{0:T(128)S(1)} %pad_add_fusion.ints, f32[98]{0:T(128)S(1)} %pad_maximum_fusion.5.floats, f32[128,2304]{1,0:T(8,128)S(1)} %bitcast_convert_fusion.marg, ...), custom_call_target="tpu_custom_call" | custom-call | tf_op jit(solution)/shard_map/pallas_call | solution.py:35
  34.1 5.8 %collective-permute-start.2 = (f32[2,8,128]{2,1,0:T(8,128)S(1)}, f32[2,8,128]{2,1,0:T(8,128)S(1)}, u32[]{:S(2)}, u32[]{:S(2)}) collective-permute-start(f32[2,8,128]{2,1,0:T(8,128)S(1)} %get-tuple-element.130), channel_id=1, source_target_pairs={{0,1},{1,0},{2,3},{3,2},{4,5},{5,4},{6,7},{7,6},{8,9},{9,8},{10,11... | collective-permute-start | bytes 24584 | tf_op jit(solution)/shard_map/ppermute | solution.py:263
  40.7 2.2 %collective-permute-done.3.recvz = f32[2,8,128]{2,1,0:T(8,128)S(1)} collective-permute-done((f32[2,8,128]{2,1,0:T(8,128)S(1)}, f32[2,8,128]{2,1,0:T(8,128)S(1)}, u32[]{:S(2)}, u32[]{:S(2)}) %collective-permute-start.3) | collective-permute-done | bytes 8224 | tf_op jit(solution)/shard_map/ppermute | solution.py:263
  43.0 1.3 shard_map.131
  44.3 1.4 collective-permute-start.4
  46.5 2.2 %collective-permute-done.5.recvz = f32[2,8,128]{2,1,0:T(8,128)S(1)} collective-permute-done((f32[2,8,128]{2,1,0:T(8,128)S(1)}, f32[2,8,128]{2,1,0:T(8,128)S(1)}, u32[]{:S(2)}, u32[]{:S(2)}) %collective-permute-start.5) | collective-permute-done | bytes 8224 | tf_op jit(solution)/shard_map/ppermute | solution.py:263
  48.7 1.3 shard_map.132
  50.0 1.4 collective-permute-start.6
  52.2 2.2 %collective-permute-done.7.recvz = f32[2,8,128]{2,1,0:T(8,128)S(1)} collective-permute-done((f32[2,8,128]{2,1,0:T(8,128)S(1)}, f32[2,8,128]{2,1,0:T(8,128)S(1)}, u32[]{:S(2)}, u32[]{:S(2)}) %collective-permute-start.7) | collective-permute-done | bytes 8224 | tf_op jit(solution)/shard_map/ppermute | solution.py:263
  54.5 1.3 shard_map.133
  55.7 1.4 collective-permute-start.8
  58.0 2.2 %collective-permute-done.9.recvz = f32[2,8,128]{2,1,0:T(8,128)S(1)} collective-permute-done((f32[2,8,128]{2,1,0:T(8,128)S(1)}, f32[2,8,128]{2,1,0:T(8,128)S(1)}, u32[]{:S(2)}, u32[]{:S(2)}) %collective-permute-start.9) | collective-permute-done | bytes 8224 | tf_op jit(solution)/shard_map/ppermute | solution.py:263
  60.2 1.2 shard_map.134
  61.5 1.4 collective-permute-start.10
  62.9 1.2 shard_map.135
  64.2 1.8 %collective-permute-done.11.recvz = f32[2,8,128]{2,1,0:T(8,128)S(1)} collective-permute-done((f32[2,8,128]{2,1,0:T(8,128)S(1)}, f32[2,8,128]{2,1,0:T(8,128)S(1)}, u32[]{:S(2)}, u32[]{:S(2)}) %collective-permute-start.11) | collective-permute-done | bytes 8224 | tf_op jit(solution)/shard_map/ppermute | solution.py:263
  65.9 1.2 shard_map.136
  67.2 1.6 %collective-permute-start.12 = (f32[2,8,128]{2,1,0:T(8,128)S(1)}, f32[2,8,128]{2,1,0:T(8,128)S(1)}, u32[]{:S(2)}, u32[]{:S(2)}) collective-permute-start(f32[2,8,128]{2,1,0:T(8,128)S(1)} %get-tuple-element.164), channel_id=1, source_target_pairs={{0,1},{1,0},{2,3},{3,2},{4,5},{5,4},{6,7},{7,6},{8,9},{9,8},{10,11... | collective-permute-start | bytes 24584 | tf_op jit(solution)/shard_map/ppermute | solution.py:263
  69.6 2.2 %collective-permute-done.13.recvz = f32[2,8,128]{2,1,0:T(8,128)S(1)} collective-permute-done((f32[2,8,128]{2,1,0:T(8,128)S(1)}, f32[2,8,128]{2,1,0:T(8,128)S(1)}, u32[]{:S(2)}, u32[]{:S(2)}) %collective-permute-start.13) | collective-permute-done | bytes 8224 | tf_op jit(solution)/shard_map/ppermute | solution.py:263
  71.9 1.2 shard_map.137
  73.1 1.4 collective-permute-start.14
  75.3 2.2 %collective-permute-done.15.recvz = f32[2,8,128]{2,1,0:T(8,128)S(1)} collective-permute-done((f32[2,8,128]{2,1,0:T(8,128)S(1)}, f32[2,8,128]{2,1,0:T(8,128)S(1)}, u32[]{:S(2)}, u32[]{:S(2)}) %collective-permute-start.15) | collective-permute-done | bytes 8224 | tf_op jit(solution)/shard_map/ppermute | solution.py:263
  77.6 1.3 shard_map.138
  78.8 1.4 collective-permute-start.16
  81.1 2.2 %collective-permute-done.17.recvz = f32[2,8,128]{2,1,0:T(8,128)S(1)} collective-permute-done((f32[2,8,128]{2,1,0:T(8,128)S(1)}, f32[2,8,128]{2,1,0:T(8,128)S(1)}, u32[]{:S(2)}, u32[]{:S(2)}) %collective-permute-start.17) | collective-permute-done | bytes 8224 | tf_op jit(solution)/shard_map/ppermute | solution.py:263
  83.3 1.3 shard_map.139
  84.6 1.4 collective-permute-start.18
  86.0 1.2 shard_map.140
  87.2 1.8 %collective-permute-done.19.recvz = f32[2,8,128]{2,1,0:T(8,128)S(1)} collective-permute-done((f32[2,8,128]{2,1,0:T(8,128)S(1)}, f32[2,8,128]{2,1,0:T(8,128)S(1)}, u32[]{:S(2)}, u32[]{:S(2)}) %collective-permute-start.19) | collective-permute-done | bytes 8224 | tf_op jit(solution)/shard_map/ppermute | solution.py:263
  89.1 1.2 shard_map.141
  90.3 1.4 collective-permute-start.20
  92.5 2.2 %collective-permute-done.21.recvz = f32[2,8,128]{2,1,0:T(8,128)S(1)} collective-permute-done((f32[2,8,128]{2,1,0:T(8,128)S(1)}, f32[2,8,128]{2,1,0:T(8,128)S(1)}, u32[]{:S(2)}, u32[]{:S(2)}) %collective-permute-start.21) | collective-permute-done | bytes 8224 | tf_op jit(solution)/shard_map/ppermute | solution.py:263
  94.8 1.2 shard_map.142
  96.0 1.4 collective-permute-start.22
  98.3 2.2 %collective-permute-done.23.recvz = f32[2,8,128]{2,1,0:T(8,128)S(1)} collective-permute-done((f32[2,8,128]{2,1,0:T(8,128)S(1)}, f32[2,8,128]{2,1,0:T(8,128)S(1)}, u32[]{:S(2)}, u32[]{:S(2)}) %collective-permute-start.23) | collective-permute-done | bytes 8224 | tf_op jit(solution)/shard_map/ppermute | solution.py:263
  100.5 1.3 shard_map.143
  101.8 1.6 %collective-permute-start.24 = (f32[2,8,128]{2,1,0:T(8,128)S(1)}, f32[2,8,128]{2,1,0:T(8,128)S(1)}, u32[]{:S(2)}, u32[]{:S(2)}) collective-permute-start(f32[2,8,128]{2,1,0:T(8,128)S(1)} %get-tuple-element.202), channel_id=1, source_target_pairs={{0,1},{1,0},{2,3},{3,2},{4,5},{5,4},{6,7},{7,6},{8,9},{9,8},{10,11... | collective-permute-start | bytes 24584 | tf_op jit(solution)/shard_map/ppermute | solution.py:263
  104.2 2.2 %collective-permute-done.25.recvz = f32[2,8,128]{2,1,0:T(8,128)S(1)} collective-permute-done((f32[2,8,128]{2,1,0:T(8,128)S(1)}, f32[2,8,128]{2,1,0:T(8,128)S(1)}, u32[]{:S(2)}, u32[]{:S(2)}) %collective-permute-start.25) | collective-permute-done | bytes 8224 | tf_op jit(solution)/shard_map/ppermute | solution.py:263
  106.5 1.3 shard_map.144
  107.7 1.4 collective-permute-start.26
  109.1 1.2 shard_map.145
  110.4 1.8 %collective-permute-done.27.recvz = f32[2,8,128]{2,1,0:T(8,128)S(1)} collective-permute-done((f32[2,8,128]{2,1,0:T(8,128)S(1)}, f32[2,8,128]{2,1,0:T(8,128)S(1)}, u32[]{:S(2)}, u32[]{:S(2)}) %collective-permute-start.27) | collective-permute-done | bytes 8224 | tf_op jit(solution)/shard_map/ppermute | solution.py:263
  112.2 1.3 shard_map.146
  113.5 1.4 collective-permute-start.28
  115.7 2.2 %collective-permute-done.29.recvz = f32[2,8,128]{2,1,0:T(8,128)S(1)} collective-permute-done((f32[2,8,128]{2,1,0:T(8,128)S(1)}, f32[2,8,128]{2,1,0:T(8,128)S(1)}, u32[]{:S(2)}, u32[]{:S(2)}) %collective-permute-start.29) | collective-permute-done | bytes 8224 | tf_op jit(solution)/shard_map/ppermute | solution.py:263
  117.9 1.2 shard_map.147
  119.2 1.4 collective-permute-start.30
  121.4 2.2 %collective-permute-done.31.recvz = f32[2,8,128]{2,1,0:T(8,128)S(1)} collective-permute-done((f32[2,8,128]{2,1,0:T(8,128)S(1)}, f32[2,8,128]{2,1,0:T(8,128)S(1)}, u32[]{:S(2)}, u32[]{:S(2)}) %collective-permute-start.31) | collective-permute-done | bytes 8224 | tf_op jit(solution)/shard_map/ppermute | solution.py:263
  123.7 1.3 shard_map.148
  124.9 1.4 collective-permute-start.32
  127.2 2.2 %collective-permute-done.33.recvz = f32[2,8,128]{2,1,0:T(8,128)S(1)} collective-permute-done((f32[2,8,128]{2,1,0:T(8,128)S(1)}, f32[2,8,128]{2,1,0:T(8,128)S(1)}, u32[]{:S(2)}, u32[]{:S(2)}) %collective-permute-start.33) | collective-permute-done | bytes 8224 | tf_op jit(solution)/shard_map/ppermute | solution.py:263
  129.4 1.3 shard_map.149
  130.7 1.4 collective-permute-start.34
  132.1 1.2 shard_map.150
  133.3 1.8 %collective-permute-done.35.recvz = f32[2,8,128]{2,1,0:T(8,128)S(1)} collective-permute-done((f32[2,8,128]{2,1,0:T(8,128)S(1)}, f32[2,8,128]{2,1,0:T(8,128)S(1)}, u32[]{:S(2)}, u32[]{:S(2)}) %collective-permute-start.35) | collective-permute-done | bytes 8224 | tf_op jit(solution)/shard_map/ppermute | solution.py:263
  136.0 14.2 %all_to_all.10 = bf16[16,8,2688]{2,1,0:T(8,128)(2,1)S(1)} all-to-all(bf16[16,8,2688]{2,1,0:T(8,128)(2,1)S(1)} %bitcast.34), channel_id=1, replica_groups=mesh['section'=16,'tile'=16] {'section'}, dimensions={0} | all-to-all | bytes 1376256 | tf_op jit(solution)/shard_map/all_to_all | solution.py:355
  151.4 1.1 fusion
  (79 shorter events, 18.5 us)
Async XLA Ops:
  0.6 9.7 %copy-start.4 = (f32[48]{0:T(128)S(1)}, f32[48]{0:T(128)}, u32[]{:S(2)}) copy-start(f32[48]{0:T(128)} %param.19) | copy-start | bytes 580
  0.6 9.7 %copy-start.5 = (f32[48]{0:T(128)S(1)}, f32[48]{0:T(128)}, u32[]{:S(2)}) copy-start(f32[48]{0:T(128)} %param.18) | copy-start | bytes 580
  0.7 9.8 %copy-start.6 = (s32[48]{0:T(128)S(1)}, s32[48]{0:T(128)}, u32[]{:S(2)}) copy-start(s32[48]{0:T(128)} %param.15) | copy-start | bytes 580
  3.3 10.1 %collective-permute-start = (f32[144,128]{1,0:T(8,128)S(1)}, f32[144,128]{1,0:T(8,128)}, u32[]{:S(2)}, u32[]{:S(2)}) collective-permute-start(f32[144,128]{1,0:T(8,128)S(1)} %get-tuple-element.260), channel_id=1, source_target_pairs={{0,1},{1,0},{2,3},{3,2},{4,5},{5,4},{6,7},{7,6},{8,9},{9,8},{10,11... | collective-permute-start | bytes 221192 | tf_op jit(solution)/shard_map/ppermute | solution.py:263
  6.6 7.7 %collective-permute-start.1 = (f32[144,128]{1,0:T(8,128)S(1)}, f32[144,128]{1,0:T(8,128)S(1)}, u32[]{:S(2)}, u32[]{:S(2)}) collective-permute-start(f32[144,128]{1,0:T(8,128)S(1)} %get-tuple-element.259), channel_id=1, source_target_pairs={{0,15},{1,2},{2,1},{3,4},{4,3},{5,6},{6,5},{7,8},{8,7},{9,10},{10,... | collective-permute-start | bytes 221192 | tf_op jit(solution)/shard_map/ppermute | solution.py:263
  10.5 1.9 %copy-start = (s32[48,128,128]{2,1,0:T(8,128)S(1)}, s32[48,128,128]{2,1,0:T(8,128)}, u32[]{:S(2)}) copy-start(s32[48,128,128]{2,1,0:T(8,128)} %param.17) | copy-start | bytes 9437188
  12.4 2.0 %copy-start.1 = (f16[16,8,2048]{2,1,0:T(8,128)(2,1)S(1)}, f16[16,8,2048]{2,1,0:T(8,128)(2,1)}, u32[]{:S(2)}) copy-start(f16[16,8,2048]{2,1,0:T(8,128)(2,1)} %convert_bitcast_fusion) | copy-start | bytes 1572868
  13.4 8.6 %copy-start.2 = (f32[2048]{0:T(1024)S(1)}, f32[2048]{0:T(1024)}, u32[]{:S(2)}) copy-start(f32[2048]{0:T(1024)} %param.12) | copy-start | bytes 24580
  13.4 8.6 %copy-start.3 = (f32[2048]{0:T(1024)S(1)}, f32[2048]{0:T(1024)}, u32[]{:S(2)}) copy-start(f32[2048]{0:T(1024)} %param.11) | copy-start | bytes 24580
  15.3 16.1 %all-to-all-start = ((f16[16,8,2304]{2,1,0:T(8,128)(2,1)}), f16[16,8,2304]{2,1,0:T(8,128)(2,1)}, u32[]{:S(2)}, u32[]{:S(2)}) async-start(f16[16,8,2304]{2,1,0:T(8,128)(2,1)} %pad_maximum_fusion), calls=%async_computation | async-start | bytes 1179648 | tf_op jit(solution)/shard_map/all_to_all | solution.py:297
  34.1 6.7 %collective-permute-start.2 = (f32[2,8,128]{2,1,0:T(8,128)S(1)}, f32[2,8,128]{2,1,0:T(8,128)S(1)}, u32[]{:S(2)}, u32[]{:S(2)}) collective-permute-start(f32[2,8,128]{2,1,0:T(8,128)S(1)} %get-tuple-element.130), channel_id=1, source_target_pairs={{0,1},{1,0},{2,3},{3,2},{4,5},{5,4},{6,7},{7,6},{8,9},{9,8},{10,11... | collective-permute-start | bytes 24584 | tf_op jit(solution)/shard_map/ppermute | solution.py:263
  39.9 3.1 %collective-permute-start.3 = (f32[2,8,128]{2,1,0:T(8,128)S(1)}, f32[2,8,128]{2,1,0:T(8,128)S(1)}, u32[]{:S(2)}, u32[]{:S(2)}) collective-permute-start(f32[2,8,128]{2,1,0:T(8,128)S(1)} %get-tuple-element.131), channel_id=1, source_target_pairs={{0,15},{1,2},{2,1},{3,4},{4,3},{5,6},{6,5},{7,8},{8,7},{9,10},{10,... | collective-permute-start | bytes 24584 | tf_op jit(solution)/shard_map/ppermute | solution.py:263
  44.3 2.2 %collective-permute-start.4 = (f32[2,8,128]{2,1,0:T(8,128)S(1)}, f32[2,8,128]{2,1,0:T(8,128)S(1)}, u32[]{:S(2)}, u32[]{:S(2)}) collective-permute-start(f32[2,8,128]{2,1,0:T(8,128)S(1)} %get-tuple-element.135), channel_id=1, source_target_pairs={{0,1},{1,0},{2,3},{3,2},{4,5},{5,4},{6,7},{7,6},{8,9},{9,8},{10,11... | collective-permute-start | bytes 24584 | tf_op jit(solution)/shard_map/ppermute | solution.py:263
  45.7 3.1 %collective-permute-start.5 = (f32[2,8,128]{2,1,0:T(8,128)S(1)}, f32[2,8,128]{2,1,0:T(8,128)S(1)}, u32[]{:S(2)}, u32[]{:S(2)}) collective-permute-start(f32[2,8,128]{2,1,0:T(8,128)S(1)} %get-tuple-element.136), channel_id=1, source_target_pairs={{0,15},{1,2},{2,1},{3,4},{4,3},{5,6},{6,5},{7,8},{8,7},{9,10},{10,... | collective-permute-start | bytes 24584 | tf_op jit(solution)/shard_map/ppermute | solution.py:263
  50.0 2.2 %collective-permute-start.6 = (f32[2,8,128]{2,1,0:T(8,128)S(1)}, f32[2,8,128]{2,1,0:T(8,128)S(1)}, u32[]{:S(2)}, u32[]{:S(2)}) collective-permute-start(f32[2,8,128]{2,1,0:T(8,128)S(1)} %get-tuple-element.140), channel_id=1, source_target_pairs={{0,1},{1,0},{2,3},{3,2},{4,5},{5,4},{6,7},{7,6},{8,9},{9,8},{10,11... | collective-permute-start | bytes 24584 | tf_op jit(solution)/shard_map/ppermute | solution.py:263
  51.4 3.1 %collective-permute-start.7 = (f32[2,8,128]{2,1,0:T(8,128)S(1)}, f32[2,8,128]{2,1,0:T(8,128)S(1)}, u32[]{:S(2)}, u32[]{:S(2)}) collective-permute-start(f32[2,8,128]{2,1,0:T(8,128)S(1)} %get-tuple-element.141), channel_id=1, source_target_pairs={{0,15},{1,2},{2,1},{3,4},{4,3},{5,6},{6,5},{7,8},{8,7},{9,10},{10,... | collective-permute-start | bytes 24584 | tf_op jit(solution)/shard_map/ppermute | solution.py:263
  55.7 2.2 %collective-permute-start.8 = (f32[2,8,128]{2,1,0:T(8,128)S(1)}, f32[2,8,128]{2,1,0:T(8,128)S(1)}, u32[]{:S(2)}, u32[]{:S(2)}) collective-permute-start(f32[2,8,128]{2,1,0:T(8,128)S(1)} %get-tuple-element.144), channel_id=1, source_target_pairs={{0,1},{1,0},{2,3},{3,2},{4,5},{5,4},{6,7},{7,6},{8,9},{9,8},{10,11... | collective-permute-start | bytes 24584 | tf_op jit(solution)/shard_map/ppermute | solution.py:263
  57.1 3.1 %collective-permute-start.9 = (f32[2,8,128]{2,1,0:T(8,128)S(1)}, f32[2,8,128]{2,1,0:T(8,128)S(1)}, u32[]{:S(2)}, u32[]{:S(2)}) collective-permute-start(f32[2,8,128]{2,1,0:T(8,128)S(1)} %get-tuple-element.145), channel_id=1, source_target_pairs={{0,15},{1,2},{2,1},{3,4},{4,3},{5,6},{6,5},{7,8},{8,7},{9,10},{10,... | collective-permute-start | bytes 24584 | tf_op jit(solution)/shard_map/ppermute | solution.py:263
  61.5 2.7 %collective-permute-start.10 = (f32[2,8,128]{2,1,0:T(8,128)S(1)}, f32[2,8,128]{2,1,0:T(8,128)S(1)}, u32[]{:S(2)}, u32[]{:S(2)}) collective-permute-start(f32[2,8,128]{2,1,0:T(8,128)S(1)} %get-tuple-element.148), channel_id=1, source_target_pairs={{0,1},{1,0},{2,3},{3,2},{4,5},{5,4},{6,7},{7,6},{8,9},{9,8},{10,11... | collective-permute-start | bytes 24584 | tf_op jit(solution)/shard_map/ppermute | solution.py:263
  62.9 3.1 %collective-permute-start.11 = (f32[2,8,128]{2,1,0:T(8,128)S(1)}, f32[2,8,128]{2,1,0:T(8,128)S(1)}, u32[]{:S(2)}, u32[]{:S(2)}) collective-permute-start(f32[2,8,128]{2,1,0:T(8,128)S(1)} %get-tuple-element.149), channel_id=1, source_target_pairs={{0,15},{1,2},{2,1},{3,4},{4,3},{5,6},{6,5},{7,8},{8,7},{9,10},{10,... | collective-permute-start | bytes 24584 | tf_op jit(solution)/shard_map/ppermute | solution.py:263
  67.2 2.4 %collective-permute-start.12 = (f32[2,8,128]{2,1,0:T(8,128)S(1)}, f32[2,8,128]{2,1,0:T(8,128)S(1)}, u32[]{:S(2)}, u32[]{:S(2)}) collective-permute-start(f32[2,8,128]{2,1,0:T(8,128)S(1)} %get-tuple-element.164), channel_id=1, source_target_pairs={{0,1},{1,0},{2,3},{3,2},{4,5},{5,4},{6,7},{7,6},{8,9},{9,8},{10,11... | collective-permute-start | bytes 24584 | tf_op jit(solution)/shard_map/ppermute | solution.py:263
  68.8 3.1 %collective-permute-start.13 = (f32[2,8,128]{2,1,0:T(8,128)S(1)}, f32[2,8,128]{2,1,0:T(8,128)S(1)}, u32[]{:S(2)}, u32[]{:S(2)}) collective-permute-start(f32[2,8,128]{2,1,0:T(8,128)S(1)} %get-tuple-element.165), channel_id=1, source_target_pairs={{0,15},{1,2},{2,1},{3,4},{4,3},{5,6},{6,5},{7,8},{8,7},{9,10},{10,... | collective-permute-start | bytes 24584 | tf_op jit(solution)/shard_map/ppermute | solution.py:263
  73.1 2.2 %collective-permute-start.14 = (f32[2,8,128]{2,1,0:T(8,128)S(1)}, f32[2,8,128]{2,1,0:T(8,128)S(1)}, u32[]{:S(2)}, u32[]{:S(2)}) collective-permute-start(f32[2,8,128]{2,1,0:T(8,128)S(1)} %get-tuple-element.168), channel_id=1, source_target_pairs={{0,1},{1,0},{2,3},{3,2},{4,5},{5,4},{6,7},{7,6},{8,9},{9,8},{10,11... | collective-permute-start | bytes 24584 | tf_op jit(solution)/shard_map/ppermute | solution.py:263
  74.5 3.1 %collective-permute-start.15 = (f32[2,8,128]{2,1,0:T(8,128)S(1)}, f32[2,8,128]{2,1,0:T(8,128)S(1)}, u32[]{:S(2)}, u32[]{:S(2)}) collective-permute-start(f32[2,8,128]{2,1,0:T(8,128)S(1)} %get-tuple-element.169), channel_id=1, source_target_pairs={{0,15},{1,2},{2,1},{3,4},{4,3},{5,6},{6,5},{7,8},{8,7},{9,10},{10,... | collective-permute-start | bytes 24584 | tf_op jit(solution)/shard_map/ppermute | solution.py:263
  78.8 2.2 %collective-permute-start.16 = (f32[2,8,128]{2,1,0:T(8,128)S(1)}, f32[2,8,128]{2,1,0:T(8,128)S(1)}, u32[]{:S(2)}, u32[]{:S(2)}) collective-permute-start(f32[2,8,128]{2,1,0:T(8,128)S(1)} %get-tuple-element.172), channel_id=1, source_target_pairs={{0,1},{1,0},{2,3},{3,2},{4,5},{5,4},{6,7},{7,6},{8,9},{9,8},{10,11... | collective-permute-start | bytes 24584 | tf_op jit(solution)/shard_map/ppermute | solution.py:263
  80.2 3.1 %collective-permute-start.17 = (f32[2,8,128]{2,1,0:T(8,128)S(1)}, f32[2,8,128]{2,1,0:T(8,128)S(1)}, u32[]{:S(2)}, u32[]{:S(2)}) collective-permute-start(f32[2,8,128]{2,1,0:T(8,128)S(1)} %get-tuple-element.173), channel_id=1, source_target_pairs={{0,15},{1,2},{2,1},{3,4},{4,3},{5,6},{6,5},{7,8},{8,7},{9,10},{10,... | collective-permute-start | bytes 24584 | tf_op jit(solution)/shard_map/ppermute | solution.py:263
  84.6 2.7 %collective-permute-start.18 = (f32[2,8,128]{2,1,0:T(8,128)S(1)}, f32[2,8,128]{2,1,0:T(8,128)S(1)}, u32[]{:S(2)}, u32[]{:S(2)}) collective-permute-start(f32[2,8,128]{2,1,0:T(8,128)S(1)} %get-tuple-element.176), channel_id=1, source_target_pairs={{0,1},{1,0},{2,3},{3,2},{4,5},{5,4},{6,7},{7,6},{8,9},{9,8},{10,11... | collective-permute-start | bytes 24584 | tf_op jit(solution)/shard_map/ppermute | solution.py:263
  86.0 3.1 %collective-permute-start.19 = (f32[2,8,128]{2,1,0:T(8,128)S(1)}, f32[2,8,128]{2,1,0:T(8,128)S(1)}, u32[]{:S(2)}, u32[]{:S(2)}) collective-permute-start(f32[2,8,128]{2,1,0:T(8,128)S(1)} %get-tuple-element.177), channel_id=1, source_target_pairs={{0,15},{1,2},{2,1},{3,4},{4,3},{5,6},{6,5},{7,8},{8,7},{9,10},{10,... | collective-permute-start | bytes 24584 | tf_op jit(solution)/shard_map/ppermute | solution.py:263
  90.3 2.2 %collective-permute-start.20 = (f32[2,8,128]{2,1,0:T(8,128)S(1)}, f32[2,8,128]{2,1,0:T(8,128)S(1)}, u32[]{:S(2)}, u32[]{:S(2)}) collective-permute-start(f32[2,8,128]{2,1,0:T(8,128)S(1)} %get-tuple-element.194), channel_id=1, source_target_pairs={{0,1},{1,0},{2,3},{3,2},{4,5},{5,4},{6,7},{7,6},{8,9},{9,8},{10,11... | collective-permute-start | bytes 24584 | tf_op jit(solution)/shard_map/ppermute | solution.py:263
  91.7 3.1 %collective-permute-start.21 = (f32[2,8,128]{2,1,0:T(8,128)S(1)}, f32[2,8,128]{2,1,0:T(8,128)S(1)}, u32[]{:S(2)}, u32[]{:S(2)}) collective-permute-start(f32[2,8,128]{2,1,0:T(8,128)S(1)} %get-tuple-element.195), channel_id=1, source_target_pairs={{0,15},{1,2},{2,1},{3,4},{4,3},{5,6},{6,5},{7,8},{8,7},{9,10},{10,... | collective-permute-start | bytes 24584 | tf_op jit(solution)/shard_map/ppermute | solution.py:263
  96.0 2.2 %collective-permute-start.22 = (f32[2,8,128]{2,1,0:T(8,128)S(1)}, f32[2,8,128]{2,1,0:T(8,128)S(1)}, u32[]{:S(2)}, u32[]{:S(2)}) collective-permute-start(f32[2,8,128]{2,1,0:T(8,128)S(1)} %get-tuple-element.198), channel_id=1, source_target_pairs={{0,1},{1,0},{2,3},{3,2},{4,5},{5,4},{6,7},{7,6},{8,9},{9,8},{10,11... | collective-permute-start | bytes 24584 | tf_op jit(solution)/shard_map/ppermute | solution.py:263
  97.4 3.1 %collective-permute-start.23 = (f32[2,8,128]{2,1,0:T(8,128)S(1)}, f32[2,8,128]{2,1,0:T(8,128)S(1)}, u32[]{:S(2)}, u32[]{:S(2)}) collective-permute-start(f32[2,8,128]{2,1,0:T(8,128)S(1)} %get-tuple-element.199), channel_id=1, source_target_pairs={{0,15},{1,2},{2,1},{3,4},{4,3},{5,6},{6,5},{7,8},{8,7},{9,10},{10,... | collective-permute-start | bytes 24584 | tf_op jit(solution)/shard_map/ppermute | solution.py:263
  101.8 2.5 %collective-permute-start.24 = (f32[2,8,128]{2,1,0:T(8,128)S(1)}, f32[2,8,128]{2,1,0:T(8,128)S(1)}, u32[]{:S(2)}, u32[]{:S(2)}) collective-permute-start(f32[2,8,128]{2,1,0:T(8,128)S(1)} %get-tuple-element.202), channel_id=1, source_target_pairs={{0,1},{1,0},{2,3},{3,2},{4,5},{5,4},{6,7},{7,6},{8,9},{9,8},{10,11... | collective-permute-start | bytes 24584 | tf_op jit(solution)/shard_map/ppermute | solution.py:263
  103.4 3.1 %collective-permute-start.25 = (f32[2,8,128]{2,1,0:T(8,128)S(1)}, f32[2,8,128]{2,1,0:T(8,128)S(1)}, u32[]{:S(2)}, u32[]{:S(2)}) collective-permute-start(f32[2,8,128]{2,1,0:T(8,128)S(1)} %get-tuple-element.203), channel_id=1, source_target_pairs={{0,15},{1,2},{2,1},{3,4},{4,3},{5,6},{6,5},{7,8},{8,7},{9,10},{10,... | collective-permute-start | bytes 24584 | tf_op jit(solution)/shard_map/ppermute | solution.py:263
  107.7 2.7 %collective-permute-start.26 = (f32[2,8,128]{2,1,0:T(8,128)S(1)}, f32[2,8,128]{2,1,0:T(8,128)S(1)}, u32[]{:S(2)}, u32[]{:S(2)}) collective-permute-start(f32[2,8,128]{2,1,0:T(8,128)S(1)} %get-tuple-element.206), channel_id=1, source_target_pairs={{0,1},{1,0},{2,3},{3,2},{4,5},{5,4},{6,7},{7,6},{8,9},{9,8},{10,11... | collective-permute-start | bytes 24584 | tf_op jit(solution)/shard_map/ppermute | solution.py:263
  109.1 3.1 %collective-permute-start.27 = (f32[2,8,128]{2,1,0:T(8,128)S(1)}, f32[2,8,128]{2,1,0:T(8,128)S(1)}, u32[]{:S(2)}, u32[]{:S(2)}) collective-permute-start(f32[2,8,128]{2,1,0:T(8,128)S(1)} %get-tuple-element.207), channel_id=1, source_target_pairs={{0,15},{1,2},{2,1},{3,4},{4,3},{5,6},{6,5},{7,8},{8,7},{9,10},{10,... | collective-permute-start | bytes 24584 | tf_op jit(solution)/shard_map/ppermute | solution.py:263
  113.5 2.2 %collective-permute-start.28 = (f32[2,8,128]{2,1,0:T(8,128)S(1)}, f32[2,8,128]{2,1,0:T(8,128)S(1)}, u32[]{:S(2)}, u32[]{:S(2)}) collective-permute-start(f32[2,8,128]{2,1,0:T(8,128)S(1)} %get-tuple-element.224), channel_id=1, source_target_pairs={{0,1},{1,0},{2,3},{3,2},{4,5},{5,4},{6,7},{7,6},{8,9},{9,8},{10,11... | collective-permute-start | bytes 24584 | tf_op jit(solution)/shard_map/ppermute | solution.py:263
  114.9 3.1 %collective-permute-start.29 = (f32[2,8,128]{2,1,0:T(8,128)S(1)}, f32[2,8,128]{2,1,0:T(8,128)S(1)}, u32[]{:S(2)}, u32[]{:S(2)}) collective-permute-start(f32[2,8,128]{2,1,0:T(8,128)S(1)} %get-tuple-element.225), channel_id=1, source_target_pairs={{0,15},{1,2},{2,1},{3,4},{4,3},{5,6},{6,5},{7,8},{8,7},{9,10},{10,... | collective-permute-start | bytes 24584 | tf_op jit(solution)/shard_map/ppermute | solution.py:263
  119.2 2.2 %collective-permute-start.30 = (f32[2,8,128]{2,1,0:T(8,128)S(1)}, f32[2,8,128]{2,1,0:T(8,128)S(1)}, u32[]{:S(2)}, u32[]{:S(2)}) collective-permute-start(f32[2,8,128]{2,1,0:T(8,128)S(1)} %get-tuple-element.228), channel_id=1, source_target_pairs={{0,1},{1,0},{2,3},{3,2},{4,5},{5,4},{6,7},{7,6},{8,9},{9,8},{10,11... | collective-permute-start | bytes 24584 | tf_op jit(solution)/shard_map/ppermute | solution.py:263
  120.6 3.1 %collective-permute-start.31 = (f32[2,8,128]{2,1,0:T(8,128)S(1)}, f32[2,8,128]{2,1,0:T(8,128)S(1)}, u32[]{:S(2)}, u32[]{:S(2)}) collective-permute-start(f32[2,8,128]{2,1,0:T(8,128)S(1)} %get-tuple-element.229), channel_id=1, source_target_pairs={{0,15},{1,2},{2,1},{3,4},{4,3},{5,6},{6,5},{7,8},{8,7},{9,10},{10,... | collective-permute-start | bytes 24584 | tf_op jit(solution)/shard_map/ppermute | solution.py:263
  124.9 2.2 %collective-permute-start.32 = (f32[2,8,128]{2,1,0:T(8,128)S(1)}, f32[2,8,128]{2,1,0:T(8,128)S(1)}, u32[]{:S(2)}, u32[]{:S(2)}) collective-permute-start(f32[2,8,128]{2,1,0:T(8,128)S(1)} %get-tuple-element.232), channel_id=1, source_target_pairs={{0,1},{1,0},{2,3},{3,2},{4,5},{5,4},{6,7},{7,6},{8,9},{9,8},{10,11... | collective-permute-start | bytes 24584 | tf_op jit(solution)/shard_map/ppermute | solution.py:263
  126.3 3.1 %collective-permute-start.33 = (f32[2,8,128]{2,1,0:T(8,128)S(1)}, f32[2,8,128]{2,1,0:T(8,128)S(1)}, u32[]{:S(2)}, u32[]{:S(2)}) collective-permute-start(f32[2,8,128]{2,1,0:T(8,128)S(1)} %get-tuple-element.233), channel_id=1, source_target_pairs={{0,15},{1,2},{2,1},{3,4},{4,3},{5,6},{6,5},{7,8},{8,7},{9,10},{10,... | collective-permute-start | bytes 24584 | tf_op jit(solution)/shard_map/ppermute | solution.py:263
  130.7 2.7 %collective-permute-start.34 = (f32[2,8,128]{2,1,0:T(8,128)S(1)}, f32[2,8,128]{2,1,0:T(8,128)S(1)}, u32[]{:S(2)}, u32[]{:S(2)}) collective-permute-start(f32[2,8,128]{2,1,0:T(8,128)S(1)} %get-tuple-element.235), channel_id=1, source_target_pairs={{0,1},{1,0},{2,3},{3,2},{4,5},{5,4},{6,7},{7,6},{8,9},{9,8},{10,11... | collective-permute-start | bytes 24584 | tf_op jit(solution)/shard_map/ppermute | solution.py:263
  132.1 3.1 %collective-permute-start.35 = (f32[2,8,128]{2,1,0:T(8,128)S(1)}, f32[2,8,128]{2,1,0:T(8,128)S(1)}, u32[]{:S(2)}, u32[]{:S(2)}) collective-permute-start(f32[2,8,128]{2,1,0:T(8,128)S(1)} %get-tuple-element.236), channel_id=1, source_target_pairs={{0,15},{1,2},{2,1},{3,4},{4,3},{5,6},{6,5},{7,8},{8,7},{9,10},{10,... | collective-permute-start | bytes 24584 | tf_op jit(solution)/shard_map/ppermute | solution.py:263
where the time goes:
time: 153 us; the launch traced here: 152 us
  waiting for transfers between devices  56.5 us (37%)
  starting transfers between devices  38.8 us (25%)
  Pallas kernels  28.3 us (18%)
  blocking collectives  14.2 us (9%)
  other arithmetic  10.1 us (7%)
  local copies, waits for them, and re-layouts  2.93 us (2%)
  between operations  1.59 us (1%)
    ppermute x18, waiting for transfers between devices, exchange(): lax.ppermute(z, 'tile', Z_PAIRS)  36.5 us
    ppermute x18, starting transfers between devices, exchange(): lax.ppermute(core, 'tile', CORE_PAIRS)  32 us
    pallas_call x22, Pallas kernels, call(): pl.pallas_call(body, out_shape=outs, in_specs=[SSPEC] * n_smem + [VSPEC]...  27.4 us
    all_to_all x1, blocking collectives, on_device(): lax.all_to_all(packed.reshape(SEC, SH, LANES + GRAD_LANES), 'section', 0,...  14.2 us
    ppermute x18, waiting for transfers between devices, exchange(): lax.ppermute(core, 'tile', CORE_PAIRS)  10.7 us
    all_to_all x1, waiting for transfers between devices, on_device(): marg = lax.all_to_all(sent, 'section', 0, 0, tiled=True)  9.32 us
    all_to_all x1, starting transfers between devices, on_device(): marg = lax.all_to_all(sent, 'section', 0, 0, tiled=True)  6.68 us
  transfers between devices with their start and end apart: 37, of which 31 were waited for; matrix products, arithmetic and copies ran while one was open for 3% of the time, Pallas kernels for 4%

commit v1 on v0

--- a/solution.py
+++ b/solution.py
@@ -65,7 +65,7 @@
     return own
 
 
-def forward_body(ints, floats, marg, by_check, by_var, signs, th_out, u_out, gv_out, sendc, sendz, tb):
+def forward_body(ints, floats, marg, by_check, by_var, signs, labels, fixed, th_out, u_out, gv_out, sendc, sendz, tb):
     zmask = floats[2 * TILES + 1]
     for block in range(EXT):
         th = jnp.tanh(0.5 * marg[:, block * BLK : (block + 1) * BLK])
@@ -89,6 +89,11 @@
             tile = slot * NB + row
             gv_out[ints[tile]] += parts[:, slot * BLK : (slot + 1) * BLK] * floats[TILES + tile]
     send_edges(gv_out, ints, sendc, sendz)
+    even = floats[2 * TILES]
+    for source, row in ((labels[...], 2), (fixed[...], 3)):
+        first, last = source[:, :BLK], source[:, -BLK:]
+        sendc[row] = last * even + first * (1.0 - even)
+        sendz[row] = first * even + last * (1.0 - even)
 
 
 def backward_rows(ints, floats, section, u_ref, signs, by_check, by_var, qs, dz_out, acc_out):
@@ -107,16 +112,21 @@
             acc_out[ints[tile]] += parts[:, slot * BLK : (slot + 1) * BLK] * floats[tile]
 
 
-def first_body(ints, floats, marg, gv, recvc, recvz, ret, prior, labels, u_ref, signs, by_check,
-               by_var, g_out, q_out, dz_out, acc_out, sendc, sendz):
+def first_body(ints, floats, marg, gv, recvc, recvz, fixed, labels, u_ref, signs, by_check,
+               by_var, g_out, q_out, dz_out, acc_out, ret_out, sendc, sendz):
     zmask = floats[2 * TILES + 1]
     for block in range(EXT):
         lanes = slice(block * BLK, (block + 1) * BLK)
-        r = ret[0:1, lanes]
+        if block < NB:
+            y, constants = labels[:, lanes], fixed[:, lanes]
+        else:
+            ref = recvc if block == NB else recvz
+            y, constants = ref[2], ref[3]
+        prior, r = constants[0:1], constants[1:2]
+        ret_out[0:1, lanes] = r
         message = received(gv, block, recvc, recvz, floats)
         level = marg[(SEC - 1) * SH :, lanes]
-        f = r * level + (1.0 - r) * (prior[0:1, lanes] + message)
-        y = labels[:, lanes]
+        f = r * level + (1.0 - r) * (prior + message)
         g = y * jax.nn.sigmoid(f) - (1.0 - y) * jax.nn.sigmoid(-f)
         if block == NB + 1:
             g = g * zmask
@@ -226,16 +236,30 @@
     msg_sum = jnp.sum(msg_rows, axis=1, keepdims=True)
     tile_index = lax.broadcasted_iota(jnp.int32, (TILES, BLK), 0)
     lane_index = lax.broadcasted_iota(jnp.int32, (TILES, BLK), 1)
-    merged = jnp.where(tile_index == lane_index, gate_sum, 0.0) + jnp.where(
-        tile_index + TILES == lane_index, msg_sum, 0.0
-    )
-    high, low = split(jnp.sum(merged, axis=0, keepdims=True))
-    weights = jnp.concatenate([high, low, jnp.zeros((SH - 2, BLK), F32)], axis=0)
+    rows = []
+    for value in (gate_sum, msg_sum):
+        placed = jnp.where(tile_index == lane_index, value, 0.0)
+        rows += split(jnp.sum(placed, axis=0, keepdims=True))
+    weights = jnp.concatenate(rows + [jnp.zeros((SH - 4, BLK), F32)], axis=0)
     for index, value in enumerate(prior_high + prior_low + [weights]):
         doubled = jnp.concatenate([value, value], axis=0).astype(BF16)
         lanes = slice(LANES + index * BLK, LANES + (index + 1) * BLK)
         for pair in range(SEC // 2):
             out[pair * 2 * SH : (pair + 1) * 2 * SH, lanes] = doubled
+
+
+def unpack_body(got, live, out, gate_out, msg_out, prior_out):
+    for block in range(NB):
+        lanes = slice(block * BLK, (block + 1) * BLK)
+        out[:, lanes] = got[:, lanes].astype(F32)
+    grads = []
+    for index in range(GRAD_LANES // BLK):
+        lanes = slice(LANES + index * BLK, LANES + (index + 1) * BLK)
+        grads.append(jnp.sum(got[:, lanes].astype(F32).reshape(SEC, SH, BLK), axis=0))
+    prior_out[:SH] = grads[0] + grads[2]
+    prior_out[SH:] = grads[1] + grads[3]
+    gate_out[...] = (grads[4][0:1] + grads[4][1:2])[:, :TILES] * live[...]
+    msg_out[...] = (grads[4][2:3] + grads[4][3:4])[:, :TILES] * live[...]
 
 
 def on_device(
@@ -265,13 +289,10 @@
     levels = checkpoint[0]
     my_labels = lax.dynamic_slice_in_dim(labels, group * SH, SH, 0).astype(F32)
     my_signs = 1.0 - 2.0 * lax.dynamic_slice_in_dim(syndrome, group * SH, SH, 0).astype(F32)
-    fixed = jnp.stack([prior_llr, retention])
-    edges = [own_edges(x) for x in (levels, my_labels, fixed)]
-    pad = jnp.zeros((SH - 2, BLK), F32)
-    halo_core, halo_z = exchange(
-        jnp.concatenate([e[0] for e in edges] + [pad], axis=0),
-        jnp.concatenate([e[1] for e in edges] + [pad], axis=0),
-    )
+    fixed = jnp.concatenate(
+        [prior_llr[None], retention[None], jnp.zeros((SH - 2, LANES), F32)], axis=0
+    )
+    halo_core, halo_z = exchange(*own_edges(levels))
 
     slots = jnp.arange(TILES, dtype=jnp.int32)
     live = (slots < tile_count[0]).astype(F32)
@@ -286,13 +307,9 @@
     floats = jnp.concatenate(
         [gate_weight * live, msg_weight * live, jnp.stack([even, has_z]).astype(F32)]
     )
-    shots = SEC * SH
-    halo = jnp.concatenate([halo_core, halo_z], axis=1)
-    labels_ext = jnp.concatenate([my_labels, halo[shots : shots + SH]], axis=1)
-    fixed_ext = jnp.concatenate([fixed, halo[shots + SH : shots + SH + 2]], axis=1)
-    prior_ext, ret_ext = fixed_ext[0:1], fixed_ext[1:2]
-    sent = jnp.concatenate([levels, halo[:shots]], axis=1).astype(jnp.float16)
+    sent = jnp.concatenate([levels, halo_core, halo_z], axis=1).astype(jnp.float16)
     sent = sent.reshape(SEC, SH, EXT * BLK)
+    sent, pattern = lax.optimization_barrier((sent, pattern))
     patterns = prepare(pattern)
     marg = lax.all_to_all(sent, "section", 0, 0, tiled=True)
     marg = marg.reshape(SEC * SH, EXT * BLK).astype(F32)
@@ -301,20 +318,21 @@
         return jax.ShapeDtypeStruct(dims, dtype)
 
     edge = shape(2, SH, BLK)
+    wide_edge = shape(4, SH, BLK)
     field = shape(EXT, SH, BLK)
     rows = shape(NB, SH, BLK)
     th, u, gv, core, z = call(
         forward_body,
-        [shape(EXT, SEC * SH, BLK), shape(NB, SEC * SH, BLK), field, edge, edge],
-        [ints, floats, marg, *patterns, my_signs],
+        [shape(EXT, SEC * SH, BLK), shape(NB, SEC * SH, BLK), field, wide_edge, wide_edge],
+        [ints, floats, marg, *patterns, my_signs, my_labels, fixed],
         2,
         scratch=[pltpu.VMEM((EXT, SEC * SH, BLK), BF16)],
     )
     core, z = exchange(core, z)
-    g, q, dz, acc, core, z = call(
+    g, q, dz, acc, ret_ext, core, z = call(
         first_body,
-        [field, field, rows, field, edge, edge],
-        [ints, floats, marg, gv, core, z, ret_ext, prior_ext, labels_ext, u, my_signs, *patterns],
+        [field, field, rows, field, shape(1, EXT * BLK), edge, edge],
+        [ints, floats, marg, gv, core, z, fixed, my_labels, u, my_signs, *patterns],
         2,
     )
     leaving = {SEC - 1: g}
@@ -353,12 +371,13 @@
         1,
     )
     got = lax.all_to_all(packed.reshape(SEC, SH, LANES + GRAD_LANES), "section", 0, 0, tiled=True)
-    grads = jnp.sum(got[:, :, LANES:].astype(F32), axis=0)
-    prior = (grads[:, : 2 * BLK] + grads[:, 2 * BLK : 4 * BLK]).reshape(SH, 2, BLK)
-    prior = prior.transpose(1, 0, 2).reshape(LANES)
-    weights = grads[0, 4 * BLK :] + grads[1, 4 * BLK :]
-    input_grads = got[:, :, :LANES].astype(F32).reshape(1, SEC * SH, LANES)
-    return input_grads, weights[:TILES] * live, weights[TILES : 2 * TILES] * live, prior
+    input_grads, gate, msg, prior = call(
+        unpack_body,
+        [shape(SEC * SH, LANES), shape(1, TILES), shape(1, TILES), shape(NB, BLK)],
+        [got.reshape(SEC * SH, LANES + GRAD_LANES), live[None]],
+        0,
+    )
+    return input_grads[None], gate.reshape(TILES), msg.reshape(TILES), prior.reshape(LANES)
 
 
 def solution(mesh):

time: 153 us -> 150 us (0.980)
  blocking collectives: 14.2 us -> 0 us
  waiting for transfers between devices: 56.5 us -> 66 us
  other arithmetic: 10.1 us -> 6.33 us
  starting transfers between devices: 38.8 us -> 42.4 us
  Pallas kernels: 28.3 us -> 30.6 us
    all_to_all x1 -> x0, blocking collectives: 14.2 us -> none  [on_device(): lax.all_to_all(packed.reshape(SEC, SH, LANES + GRAD_LANES), 'section', 0,...]
    all_to_all x0 -> x1, waiting for transfers between devices: none -> 11.9 us  [on_device(): lax.all_to_all(packed.reshape(SEC, SH, LANES + GRAD_LANES), 'section', 0,...]
    all_to_all x0 -> x1, starting transfers between devices: none -> 3.6 us  [on_device(): lax.all_to_all(packed.reshape(SEC, SH, LANES + GRAD_LANES), 'section', 0,...]
    ppermute x18, starting transfers between devices: 32 us -> 28.8 us  [exchange(): lax.ppermute(core, 'tile', CORE_PAIRS)]
    ppermute x18, starting transfers between devices: 0.05 us -> 3.16 us  [exchange(): lax.ppermute(z, 'tile', Z_PAIRS)]
    all_to_all x1, waiting for transfers between devices: 9.32 us -> 6.88 us  [on_device(): marg = lax.all_to_all(sent, 'section', 0, 0, tiled=True)]
    pallas_call x22 -> x23, Pallas kernels: 27.4 us -> 29.6 us  [call(): pl.pallas_call(body, out_shape=outs, in_specs=[SSPEC] * n_smem + [VSPEC]...]
    reshape x2 -> x0, other arithmetic: 1.68 us -> none  [the longest x1 1.08 us: on_device(): input_grads = got[:, :, :LANES].astype(F32).reshape(1, SEC * SH, LANES)]
  transfers between devices with their start and end apart: 37 -> 38, of which waited for: 31 -> 32; matrix products, arithmetic and copies ran while one was open for 3% -> 2% of each run, Pallas kernels for 4% -> 4%
where the time goes in v1:
time: 150 us; the launch traced here: 149 us
  waiting for transfers between devices  66 us (44%)
  starting transfers between devices  42.4 us (28%)
  Pallas kernels  30.6 us (20%)
  other arithmetic  6.33 us (4%)
  local copies, waits for them, and re-layouts  2.01 us (1%)
  between operations  1.57 us (1%)
    ppermute x18, waiting for transfers between devices, exchange(): lax.ppermute(z, 'tile', Z_PAIRS)  36.5 us
    pallas_call x23, Pallas kernels, call(): pl.pallas_call(body, out_shape=outs, in_specs=[SSPEC] * n_smem + [VSPEC]...  29.6 us
    ppermute x18, starting transfers between devices, exchange(): lax.ppermute(core, 'tile', CORE_PAIRS)  28.8 us
    all_to_all x1, waiting for transfers between devices, on_device(): lax.all_to_all(packed.reshape(SEC, SH, LANES + GRAD_LANES), 'section', 0,...  11.9 us
    ppermute x18, waiting for transfers between devices, exchange(): lax.ppermute(core, 'tile', CORE_PAIRS)  10.8 us
    all_to_all x1, waiting for transfers between devices, on_device(): marg = lax.all_to_all(sent, 'section', 0, 0, tiled=True)  6.88 us
    all_to_all x1, starting transfers between devices, on_device(): marg = lax.all_to_all(sent, 'section', 0, 0, tiled=True)  6.8 us
    all_to_all x1, starting transfers between devices, on_device(): lax.all_to_all(packed.reshape(SEC, SH, LANES + GRAD_LANES), 'section', 0,...  3.6 us
  transfers between devices with their start and end apart: 38, of which 32 were waited for; matrix products, arithmetic and copies ran while one was open for 2% of the time, Pallas kernels for 4%

profile of v1, /device:TPU:1, one launch (start us, length us, event | category | flops | bytes accessed | tf_op | source)
XLA Modules:
  0.0 148.9 jit_solution(2946197089440879011)
XLA Ops:
  1.6 3.1 %collective-permute-start.1 = (f32[128,128]{1,0:T(8,128)S(1)}, f32[128,128]{1,0:T(8,128)S(1)}, u32[]{:S(2)}, u32[]{:S(2)}) collective-permute-start(f32[128,128]{1,0:T(8,128)S(1)} %get-tuple-element.265), channel_id=1, source_target_pairs={{0,15},{1,2},{2,1},{3,4},{4,3},{5,6},{6,5},{7,8},{8,7},{9,10},{10,... | collective-permute-start | bytes 196616 | tf_op jit(solution)/shard_map/ppermute | solution.py:287
  4.7 3.8 %collective-permute-start = (f32[128,128]{1,0:T(8,128)S(1)}, f32[128,128]{1,0:T(8,128)S(1)}, u32[]{:S(2)}, u32[]{:S(2)}) collective-permute-start(f32[128,128]{1,0:T(8,128)S(1)} %get-tuple-element.264), channel_id=1, source_target_pairs={{0,1},{1,0},{2,3},{3,2},{4,5},{5,4},{6,7},{7,6},{8,9},{9,8},{10,11... | collective-permute-start | bytes 196616 | tf_op jit(solution)/shard_map/ppermute | solution.py:287
  8.5 1.3 convert_bitcast_fusion
  12.5 6.8 %all-to-all-start = ((f16[16,8,2304]{2,1,0:T(8,128)(2,1)}), f16[16,8,2304]{2,1,0:T(8,128)(2,1)}, u32[]{:S(2)}, u32[]{:S(2)}) async-start(f16[16,8,2304]{2,1,0:T(8,128)(2,1)} %pad_maximum_fusion), calls=%async_computation | async-start | bytes 1179648 | tf_op jit(solution)/shard_map/all_to_all | solution.py:314
  20.4 1.9 %copy-done = s32[48,128,128]{2,1,0:T(8,128)S(1)} copy-done((s32[48,128,128]{2,1,0:T(8,128)S(1)}, s32[48,128,128]{2,1,0:T(8,128)}, u32[]{:S(2)}) %copy-start) | copy-done | bytes 3145752
  23.3 6.9 %all-to-all-done = f16[16,8,2304]{2,1,0:T(8,128)(2,1)} async-done(((f16[16,8,2304]{2,1,0:T(8,128)(2,1)}), f16[16,8,2304]{2,1,0:T(8,128)(2,1)}, u32[]{:S(2)}, u32[]{:S(2)}) %all-to-all-start) | async-done | bytes 589856 | tf_op jit(solution)/shard_map/all_to_all | solution.py:314
  31.3 1.5 %shard_map.130 = (f32[18,128,128]{2,1,0:T(8,128)S(1)}, f32[16,128,128]{2,1,0:T(8,128)S(1)}, f32[18,8,128]{2,1,0:T(8,128)S(1)}, f32[4,8,128]{2,1,0:T(8,128)S(1)}, f32[4,8,128]{2,1,0:T(8,128)S(1)}) custom-call(s32[50]{0:T(128)S(1)} %pad_add_fusion.ints, f32[98]{0:T(128)S(1)} %pad_maximum_fusion.1.floats, f32[128,2304]{1,0:T(8,128)S(1)} %bitcast_convert_fusion.marg, ...), custom_call_target="tpu_custom_call" | custom-call | tf_op jit(solution)/shard_map/pallas_call | solution.py:35
  32.8 2.5 %collective-permute-start.2 = (f32[4,8,128]{2,1,0:T(8,128)S(1)}, f32[4,8,128]{2,1,0:T(8,128)S(1)}, u32[]{:S(2)}, u32[]{:S(2)}) collective-permute-start(f32[4,8,128]{2,1,0:T(8,128)S(1)} %get-tuple-element.139), channel_id=1, source_target_pairs={{0,1},{1,0},{2,3},{3,2},{4,5},{5,4},{6,7},{7,6},{8,9},{9,8},{10,11... | collective-permute-start | bytes 49160 | tf_op jit(solution)/shard_map/ppermute | solution.py:287
  36.2 2.3 %collective-permute-done.3.recvz = f32[4,8,128]{2,1,0:T(8,128)S(1)} collective-permute-done((f32[4,8,128]{2,1,0:T(8,128)S(1)}, f32[4,8,128]{2,1,0:T(8,128)S(1)}, u32[]{:S(2)}, u32[]{:S(2)}) %collective-permute-start.3) | collective-permute-done | bytes 16416 | tf_op jit(solution)/shard_map/ppermute | solution.py:287
  38.5 1.3 shard_map.131
  39.8 1.4 collective-permute-start.4
  42.0 2.2 %collective-permute-done.5.recvz = f32[2,8,128]{2,1,0:T(8,128)S(1)} collective-permute-done((f32[2,8,128]{2,1,0:T(8,128)S(1)}, f32[2,8,128]{2,1,0:T(8,128)S(1)}, u32[]{:S(2)}, u32[]{:S(2)}) %collective-permute-start.5) | collective-permute-done | bytes 8224 | tf_op jit(solution)/shard_map/ppermute | solution.py:287
  44.3 1.3 shard_map.132
  45.5 1.4 collective-permute-start.6
  47.8 2.2 %collective-permute-done.7.recvz = f32[2,8,128]{2,1,0:T(8,128)S(1)} collective-permute-done((f32[2,8,128]{2,1,0:T(8,128)S(1)}, f32[2,8,128]{2,1,0:T(8,128)S(1)}, u32[]{:S(2)}, u32[]{:S(2)}) %collective-permute-start.7) | collective-permute-done | bytes 8224 | tf_op jit(solution)/shard_map/ppermute | solution.py:287
  50.0 1.3 shard_map.133
  51.3 1.4 collective-permute-start.8
  53.5 2.2 %collective-permute-done.9.recvz = f32[2,8,128]{2,1,0:T(8,128)S(1)} collective-permute-done((f32[2,8,128]{2,1,0:T(8,128)S(1)}, f32[2,8,128]{2,1,0:T(8,128)S(1)}, u32[]{:S(2)}, u32[]{:S(2)}) %collective-permute-start.9) | collective-permute-done | bytes 8224 | tf_op jit(solution)/shard_map/ppermute | solution.py:287
  55.7 1.3 shard_map.134
  57.0 1.4 collective-permute-start.10
  58.4 1.3 shard_map.135
  59.7 1.8 %collective-permute-done.11.recvz = f32[2,8,128]{2,1,0:T(8,128)S(1)} collective-permute-done((f32[2,8,128]{2,1,0:T(8,128)S(1)}, f32[2,8,128]{2,1,0:T(8,128)S(1)}, u32[]{:S(2)}, u32[]{:S(2)}) %collective-permute-start.11) | collective-permute-done | bytes 8224 | tf_op jit(solution)/shard_map/ppermute | solution.py:287
  61.5 1.3 shard_map.136
  62.7 1.6 %collective-permute-start.12 = (f32[2,8,128]{2,1,0:T(8,128)S(1)}, f32[2,8,128]{2,1,0:T(8,128)S(1)}, u32[]{:S(2)}, u32[]{:S(2)}) collective-permute-start(f32[2,8,128]{2,1,0:T(8,128)S(1)} %get-tuple-element.174), channel_id=1, source_target_pairs={{0,1},{1,0},{2,3},{3,2},{4,5},{5,4},{6,7},{7,6},{8,9},{9,8},{10,11... | collective-permute-start | bytes 24584 | tf_op jit(solution)/shard_map/ppermute | solution.py:287
  65.1 2.2 %collective-permute-done.13.recvz = f32[2,8,128]{2,1,0:T(8,128)S(1)} collective-permute-done((f32[2,8,128]{2,1,0:T(8,128)S(1)}, f32[2,8,128]{2,1,0:T(8,128)S(1)}, u32[]{:S(2)}, u32[]{:S(2)}) %collective-permute-start.13) | collective-permute-done | bytes 8224 | tf_op jit(solution)/shard_map/ppermute | solution.py:287
  67.4 1.3 shard_map.137
  68.6 1.4 collective-permute-start.14
  70.9 2.2 %collective-permute-done.15.recvz = f32[2,8,128]{2,1,0:T(8,128)S(1)} collective-permute-done((f32[2,8,128]{2,1,0:T(8,128)S(1)}, f32[2,8,128]{2,1,0:T(8,128)S(1)}, u32[]{:S(2)}, u32[]{:S(2)}) %collective-permute-start.15) | collective-permute-done | bytes 8224 | tf_op jit(solution)/shard_map/ppermute | solution.py:287
  73.1 1.3 shard_map.138
  74.4 1.4 collective-permute-start.16
  76.6 2.2 %collective-permute-done.17.recvz = f32[2,8,128]{2,1,0:T(8,128)S(1)} collective-permute-done((f32[2,8,128]{2,1,0:T(8,128)S(1)}, f32[2,8,128]{2,1,0:T(8,128)S(1)}, u32[]{:S(2)}, u32[]{:S(2)}) %collective-permute-start.17) | collective-permute-done | bytes 8224 | tf_op jit(solution)/shard_map/ppermute | solution.py:287
  78.8 1.3 shard_map.139
  80.1 1.4 collective-permute-start.18
  81.5 1.2 shard_map.140
  82.8 1.8 %collective-permute-done.19.recvz = f32[2,8,128]{2,1,0:T(8,128)S(1)} collective-permute-done((f32[2,8,128]{2,1,0:T(8,128)S(1)}, f32[2,8,128]{2,1,0:T(8,128)S(1)}, u32[]{:S(2)}, u32[]{:S(2)}) %collective-permute-start.19) | collective-permute-done | bytes 8224 | tf_op jit(solution)/shard_map/ppermute | solution.py:287
  84.6 1.3 shard_map.141
  85.8 1.4 collective-permute-start.20
  88.1 2.2 %collective-permute-done.21.recvz = f32[2,8,128]{2,1,0:T(8,128)S(1)} collective-permute-done((f32[2,8,128]{2,1,0:T(8,128)S(1)}, f32[2,8,128]{2,1,0:T(8,128)S(1)}, u32[]{:S(2)}, u32[]{:S(2)}) %collective-permute-start.21) | collective-permute-done | bytes 8224 | tf_op jit(solution)/shard_map/ppermute | solution.py:287
  90.3 1.3 shard_map.142
  91.6 1.4 collective-permute-start.22
  93.8 2.2 %collective-permute-done.23.recvz = f32[2,8,128]{2,1,0:T(8,128)S(1)} collective-permute-done((f32[2,8,128]{2,1,0:T(8,128)S(1)}, f32[2,8,128]{2,1,0:T(8,128)S(1)}, u32[]{:S(2)}, u32[]{:S(2)}) %collective-permute-start.23) | collective-permute-done | bytes 8224 | tf_op jit(solution)/shard_map/ppermute | solution.py:287
  96.0 1.3 shard_map.143
  97.3 1.6 %collective-permute-start.24 = (f32[2,8,128]{2,1,0:T(8,128)S(1)}, f32[2,8,128]{2,1,0:T(8,128)S(1)}, u32[]{:S(2)}, u32[]{:S(2)}) collective-permute-start(f32[2,8,128]{2,1,0:T(8,128)S(1)} %get-tuple-element.212), channel_id=1, source_target_pairs={{0,1},{1,0},{2,3},{3,2},{4,5},{5,4},{6,7},{7,6},{8,9},{9,8},{10,11... | collective-permute-start | bytes 24584 | tf_op jit(solution)/shard_map/ppermute | solution.py:287
  99.7 2.2 %collective-permute-done.25.recvz = f32[2,8,128]{2,1,0:T(8,128)S(1)} collective-permute-done((f32[2,8,128]{2,1,0:T(8,128)S(1)}, f32[2,8,128]{2,1,0:T(8,128)S(1)}, u32[]{:S(2)}, u32[]{:S(2)}) %collective-permute-start.25) | collective-permute-done | bytes 8224 | tf_op jit(solution)/shard_map/ppermute | solution.py:287
  102.0 1.3 shard_map.144
  103.3 1.4 collective-permute-start.26
  104.7 1.2 shard_map.145
  105.9 1.8 %collective-permute-done.27.recvz = f32[2,8,128]{2,1,0:T(8,128)S(1)} collective-permute-done((f32[2,8,128]{2,1,0:T(8,128)S(1)}, f32[2,8,128]{2,1,0:T(8,128)S(1)}, u32[]{:S(2)}, u32[]{:S(2)}) %collective-permute-start.27) | collective-permute-done | bytes 8224 | tf_op jit(solution)/shard_map/ppermute | solution.py:287
  107.7 1.3 shard_map.146
  109.0 1.4 collective-permute-start.28
  111.2 2.2 %collective-permute-done.29.recvz = f32[2,8,128]{2,1,0:T(8,128)S(1)} collective-permute-done((f32[2,8,128]{2,1,0:T(8,128)S(1)}, f32[2,8,128]{2,1,0:T(8,128)S(1)}, u32[]{:S(2)}, u32[]{:S(2)}) %collective-permute-start.29) | collective-permute-done | bytes 8224 | tf_op jit(solution)/shard_map/ppermute | solution.py:287
  113.5 1.3 shard_map.147
  114.7 1.4 collective-permute-start.30
  116.9 2.2 %collective-permute-done.31.recvz = f32[2,8,128]{2,1,0:T(8,128)S(1)} collective-permute-done((f32[2,8,128]{2,1,0:T(8,128)S(1)}, f32[2,8,128]{2,1,0:T(8,128)S(1)}, u32[]{:S(2)}, u32[]{:S(2)}) %collective-permute-start.31) | collective-permute-done | bytes 8224 | tf_op jit(solution)/shard_map/ppermute | solution.py:287
  119.2 1.3 shard_map.148
  120.5 1.4 collective-permute-start.32
  122.7 2.2 %collective-permute-done.33.recvz = f32[2,8,128]{2,1,0:T(8,128)S(1)} collective-permute-done((f32[2,8,128]{2,1,0:T(8,128)S(1)}, f32[2,8,128]{2,1,0:T(8,128)S(1)}, u32[]{:S(2)}, u32[]{:S(2)}) %collective-permute-start.33) | collective-permute-done | bytes 8224 | tf_op jit(solution)/shard_map/ppermute | solution.py:287
  124.9 1.3 shard_map.149
  126.2 1.4 collective-permute-start.34
  127.6 1.2 shard_map.150
  128.8 1.8 %collective-permute-done.35.recvz = f32[2,8,128]{2,1,0:T(8,128)S(1)} collective-permute-done((f32[2,8,128]{2,1,0:T(8,128)S(1)}, f32[2,8,128]{2,1,0:T(8,128)S(1)}, u32[]{:S(2)}, u32[]{:S(2)}) %collective-permute-start.35) | collective-permute-done | bytes 8224 | tf_op jit(solution)/shard_map/ppermute | solution.py:287
  130.7 1.7 %shard_map.151 = bf16[128,2688]{1,0:T(8,128)(2,1)} custom-call(f32[98]{0:T(128)S(1)} %pad_maximum_fusion.1.floats, f32[18,8,128]{2,1,0:T(8,128)S(1)} %get-tuple-element.244.acc_in, f32[2,8,128]{2,1,0:T(8,128)S(1)} %collective-permute-done.34.recvc, f32[2,8,128]{2,1,0:T(8,128)S(1)} %collective-permute-done.35.recvz, f32[1,2304]{1,0:T(1,128)S(1)} %get-tuple-element.146.ret, ...), custom_call_target="tpu_custom_call" | custom-call | tf_op jit(solution)/shard_map/pallas_call | solution.py:35
  132.3 3.6 %all-to-all-start.1 = ((bf16[16,8,2688]{2,1,0:T(8,128)(2,1)}), bf16[16,8,2688]{2,1,0:T(8,128)(2,1)S(1)}, u32[]{:S(2)}, u32[]{:S(2)}) async-start(bf16[16,8,2688]{2,1,0:T(8,128)(2,1)} %bitcast.14), calls=%async_computation.1 | async-start | bytes 1376256 | tf_op jit(solution)/shard_map/all_to_all | solution.py:373
  135.9 11.9 %all-to-all-done.1 = bf16[16,8,2688]{2,1,0:T(8,128)(2,1)S(1)} async-done(((bf16[16,8,2688]{2,1,0:T(8,128)(2,1)}), bf16[16,8,2688]{2,1,0:T(8,128)(2,1)S(1)}, u32[]{:S(2)}, u32[]{:S(2)}) %all-to-all-start.1) | async-done | bytes 688160 | tf_op jit(solution)/shard_map/all_to_all | solution.py:373
  (65 shorter events, 18.0 us)
Async XLA Ops:
  0.6 10.7 %copy-start.3 = (f32[48]{0:T(128)S(1)}, f32[48]{0:T(128)}, u32[]{:S(2)}) copy-start(f32[48]{0:T(128)} %param.19) | copy-start | bytes 580
  0.6 10.7 %copy-start.4 = (f32[48]{0:T(128)S(1)}, f32[48]{0:T(128)}, u32[]{:S(2)}) copy-start(f32[48]{0:T(128)} %param.18) | copy-start | bytes 580
  0.7 10.7 %copy-start.5 = (s32[48]{0:T(128)S(1)}, s32[48]{0:T(128)}, u32[]{:S(2)}) copy-start(s32[48]{0:T(128)} %param.15) | copy-start | bytes 580
  1.6 9.9 %collective-permute-start.1 = (f32[128,128]{1,0:T(8,128)S(1)}, f32[128,128]{1,0:T(8,128)S(1)}, u32[]{:S(2)}, u32[]{:S(2)}) collective-permute-start(f32[128,128]{1,0:T(8,128)S(1)} %get-tuple-element.265), channel_id=1, source_target_pairs={{0,15},{1,2},{2,1},{3,4},{4,3},{5,6},{6,5},{7,8},{8,7},{9,10},{10,... | collective-permute-start | bytes 196616 | tf_op jit(solution)/shard_map/ppermute | solution.py:287
  4.7 6.8 %collective-permute-start = (f32[128,128]{1,0:T(8,128)S(1)}, f32[128,128]{1,0:T(8,128)S(1)}, u32[]{:S(2)}, u32[]{:S(2)}) collective-permute-start(f32[128,128]{1,0:T(8,128)S(1)} %get-tuple-element.264), channel_id=1, source_target_pairs={{0,1},{1,0},{2,3},{3,2},{4,5},{5,4},{6,7},{7,6},{8,9},{9,8},{10,11... | collective-permute-start | bytes 196616 | tf_op jit(solution)/shard_map/ppermute | solution.py:287
  9.7 9.8 %copy-start.1 = (f32[2048]{0:T(1024)S(1)}, f32[2048]{0:T(1024)}, u32[]{:S(2)}) copy-start(f32[2048]{0:T(1024)} %param.12) | copy-start | bytes 24580
  9.8 9.7 %copy-start.2 = (f32[2048]{0:T(1024)S(1)}, f32[2048]{0:T(1024)}, u32[]{:S(2)}) copy-start(f32[2048]{0:T(1024)} %param.11) | copy-start | bytes 24580
  12.5 17.6 %all-to-all-start = ((f16[16,8,2304]{2,1,0:T(8,128)(2,1)}), f16[16,8,2304]{2,1,0:T(8,128)(2,1)}, u32[]{:S(2)}, u32[]{:S(2)}) async-start(f16[16,8,2304]{2,1,0:T(8,128)(2,1)} %pad_maximum_fusion), calls=%async_computation | async-start | bytes 1179648 | tf_op jit(solution)/shard_map/all_to_all | solution.py:314
  20.4 1.9 %copy-start = (s32[48,128,128]{2,1,0:T(8,128)S(1)}, s32[48,128,128]{2,1,0:T(8,128)}, u32[]{:S(2)}) copy-start(s32[48,128,128]{2,1,0:T(8,128)} %param.17) | copy-start | bytes 9437188
  32.8 3.3 %collective-permute-start.2 = (f32[4,8,128]{2,1,0:T(8,128)S(1)}, f32[4,8,128]{2,1,0:T(8,128)S(1)}, u32[]{:S(2)}, u32[]{:S(2)}) collective-permute-start(f32[4,8,128]{2,1,0:T(8,128)S(1)} %get-tuple-element.139), channel_id=1, source_target_pairs={{0,1},{1,0},{2,3},{3,2},{4,5},{5,4},{6,7},{7,6},{8,9},{9,8},{10,11... | collective-permute-start | bytes 49160 | tf_op jit(solution)/shard_map/ppermute | solution.py:287
  35.4 3.2 %collective-permute-start.3 = (f32[4,8,128]{2,1,0:T(8,128)S(1)}, f32[4,8,128]{2,1,0:T(8,128)S(1)}, u32[]{:S(2)}, u32[]{:S(2)}) collective-permute-start(f32[4,8,128]{2,1,0:T(8,128)S(1)} %get-tuple-element.140), channel_id=1, source_target_pairs={{0,15},{1,2},{2,1},{3,4},{4,3},{5,6},{6,5},{7,8},{8,7},{9,10},{10,... | collective-permute-start | bytes 49160 | tf_op jit(solution)/shard_map/ppermute | solution.py:287
  39.8 2.2 %collective-permute-start.4 = (f32[2,8,128]{2,1,0:T(8,128)S(1)}, f32[2,8,128]{2,1,0:T(8,128)S(1)}, u32[]{:S(2)}, u32[]{:S(2)}) collective-permute-start(f32[2,8,128]{2,1,0:T(8,128)S(1)} %get-tuple-element.144), channel_id=1, source_target_pairs={{0,1},{1,0},{2,3},{3,2},{4,5},{5,4},{6,7},{7,6},{8,9},{9,8},{10,11... | collective-permute-start | bytes 24584 | tf_op jit(solution)/shard_map/ppermute | solution.py:287
  41.2 3.1 %collective-permute-start.5 = (f32[2,8,128]{2,1,0:T(8,128)S(1)}, f32[2,8,128]{2,1,0:T(8,128)S(1)}, u32[]{:S(2)}, u32[]{:S(2)}) collective-permute-start(f32[2,8,128]{2,1,0:T(8,128)S(1)} %get-tuple-element.145), channel_id=1, source_target_pairs={{0,15},{1,2},{2,1},{3,4},{4,3},{5,6},{6,5},{7,8},{8,7},{9,10},{10,... | collective-permute-start | bytes 24584 | tf_op jit(solution)/shard_map/ppermute | solution.py:287
  45.5 2.2 %collective-permute-start.6 = (f32[2,8,128]{2,1,0:T(8,128)S(1)}, f32[2,8,128]{2,1,0:T(8,128)S(1)}, u32[]{:S(2)}, u32[]{:S(2)}) collective-permute-start(f32[2,8,128]{2,1,0:T(8,128)S(1)} %get-tuple-element.150), channel_id=1, source_target_pairs={{0,1},{1,0},{2,3},{3,2},{4,5},{5,4},{6,7},{7,6},{8,9},{9,8},{10,11... | collective-permute-start | bytes 24584 | tf_op jit(solution)/shard_map/ppermute | solution.py:287
  46.9 3.1 %collective-permute-start.7 = (f32[2,8,128]{2,1,0:T(8,128)S(1)}, f32[2,8,128]{2,1,0:T(8,128)S(1)}, u32[]{:S(2)}, u32[]{:S(2)}) collective-permute-start(f32[2,8,128]{2,1,0:T(8,128)S(1)} %get-tuple-element.151), channel_id=1, source_target_pairs={{0,15},{1,2},{2,1},{3,4},{4,3},{5,6},{6,5},{7,8},{8,7},{9,10},{10,... | collective-permute-start | bytes 24584 | tf_op jit(solution)/shard_map/ppermute | solution.py:287
  51.3 2.2 %collective-permute-start.8 = (f32[2,8,128]{2,1,0:T(8,128)S(1)}, f32[2,8,128]{2,1,0:T(8,128)S(1)}, u32[]{:S(2)}, u32[]{:S(2)}) collective-permute-start(f32[2,8,128]{2,1,0:T(8,128)S(1)} %get-tuple-element.154), channel_id=1, source_target_pairs={{0,1},{1,0},{2,3},{3,2},{4,5},{5,4},{6,7},{7,6},{8,9},{9,8},{10,11... | collective-permute-start | bytes 24584 | tf_op jit(solution)/shard_map/ppermute | solution.py:287
  52.7 3.1 %collective-permute-start.9 = (f32[2,8,128]{2,1,0:T(8,128)S(1)}, f32[2,8,128]{2,1,0:T(8,128)S(1)}, u32[]{:S(2)}, u32[]{:S(2)}) collective-permute-start(f32[2,8,128]{2,1,0:T(8,128)S(1)} %get-tuple-element.155), channel_id=1, source_target_pairs={{0,15},{1,2},{2,1},{3,4},{4,3},{5,6},{6,5},{7,8},{8,7},{9,10},{10,... | collective-permute-start | bytes 24584 | tf_op jit(solution)/shard_map/ppermute | solution.py:287
  57.0 2.7 %collective-permute-start.10 = (f32[2,8,128]{2,1,0:T(8,128)S(1)}, f32[2,8,128]{2,1,0:T(8,128)S(1)}, u32[]{:S(2)}, u32[]{:S(2)}) collective-permute-start(f32[2,8,128]{2,1,0:T(8,128)S(1)} %get-tuple-element.158), channel_id=1, source_target_pairs={{0,1},{1,0},{2,3},{3,2},{4,5},{5,4},{6,7},{7,6},{8,9},{9,8},{10,11... | collective-permute-start | bytes 24584 | tf_op jit(solution)/shard_map/ppermute | solution.py:287
  58.4 3.1 %collective-permute-start.11 = (f32[2,8,128]{2,1,0:T(8,128)S(1)}, f32[2,8,128]{2,1,0:T(8,128)S(1)}, u32[]{:S(2)}, u32[]{:S(2)}) collective-permute-start(f32[2,8,128]{2,1,0:T(8,128)S(1)} %get-tuple-element.159), channel_id=1, source_target_pairs={{0,15},{1,2},{2,1},{3,4},{4,3},{5,6},{6,5},{7,8},{8,7},{9,10},{10,... | collective-permute-start | bytes 24584 | tf_op jit(solution)/shard_map/ppermute | solution.py:287
  62.7 2.4 %collective-permute-start.12 = (f32[2,8,128]{2,1,0:T(8,128)S(1)}, f32[2,8,128]{2,1,0:T(8,128)S(1)}, u32[]{:S(2)}, u32[]{:S(2)}) collective-permute-start(f32[2,8,128]{2,1,0:T(8,128)S(1)} %get-tuple-element.174), channel_id=1, source_target_pairs={{0,1},{1,0},{2,3},{3,2},{4,5},{5,4},{6,7},{7,6},{8,9},{9,8},{10,11... | collective-permute-start | bytes 24584 | tf_op jit(solution)/shard_map/ppermute | solution.py:287
  64.3 3.1 %collective-permute-start.13 = (f32[2,8,128]{2,1,0:T(8,128)S(1)}, f32[2,8,128]{2,1,0:T(8,128)S(1)}, u32[]{:S(2)}, u32[]{:S(2)}) collective-permute-start(f32[2,8,128]{2,1,0:T(8,128)S(1)} %get-tuple-element.175), channel_id=1, source_target_pairs={{0,15},{1,2},{2,1},{3,4},{4,3},{5,6},{6,5},{7,8},{8,7},{9,10},{10,... | collective-permute-start | bytes 24584 | tf_op jit(solution)/shard_map/ppermute | solution.py:287
  68.6 2.2 %collective-permute-start.14 = (f32[2,8,128]{2,1,0:T(8,128)S(1)}, f32[2,8,128]{2,1,0:T(8,128)S(1)}, u32[]{:S(2)}, u32[]{:S(2)}) collective-permute-start(f32[2,8,128]{2,1,0:T(8,128)S(1)} %get-tuple-element.178), channel_id=1, source_target_pairs={{0,1},{1,0},{2,3},{3,2},{4,5},{5,4},{6,7},{7,6},{8,9},{9,8},{10,11... | collective-permute-start | bytes 24584 | tf_op jit(solution)/shard_map/ppermute | solution.py:287
  70.0 3.1 %collective-permute-start.15 = (f32[2,8,128]{2,1,0:T(8,128)S(1)}, f32[2,8,128]{2,1,0:T(8,128)S(1)}, u32[]{:S(2)}, u32[]{:S(2)}) collective-permute-start(f32[2,8,128]{2,1,0:T(8,128)S(1)} %get-tuple-element.179), channel_id=1, source_target_pairs={{0,15},{1,2},{2,1},{3,4},{4,3},{5,6},{6,5},{7,8},{8,7},{9,10},{10,... | collective-permute-start | bytes 24584 | tf_op jit(solution)/shard_map/ppermute | solution.py:287
  74.4 2.2 %collective-permute-start.16 = (f32[2,8,128]{2,1,0:T(8,128)S(1)}, f32[2,8,128]{2,1,0:T(8,128)S(1)}, u32[]{:S(2)}, u32[]{:S(2)}) collective-permute-start(f32[2,8,128]{2,1,0:T(8,128)S(1)} %get-tuple-element.182), channel_id=1, source_target_pairs={{0,1},{1,0},{2,3},{3,2},{4,5},{5,4},{6,7},{7,6},{8,9},{9,8},{10,11... | collective-permute-start | bytes 24584 | tf_op jit(solution)/shard_map/ppermute | solution.py:287
  75.8 3.1 %collective-permute-start.17 = (f32[2,8,128]{2,1,0:T(8,128)S(1)}, f32[2,8,128]{2,1,0:T(8,128)S(1)}, u32[]{:S(2)}, u32[]{:S(2)}) collective-permute-start(f32[2,8,128]{2,1,0:T(8,128)S(1)} %get-tuple-element.183), channel_id=1, source_target_pairs={{0,15},{1,2},{2,1},{3,4},{4,3},{5,6},{6,5},{7,8},{8,7},{9,10},{10,... | collective-permute-start | bytes 24584 | tf_op jit(solution)/shard_map/ppermute | solution.py:287
  80.1 2.6 %collective-permute-start.18 = (f32[2,8,128]{2,1,0:T(8,128)S(1)}, f32[2,8,128]{2,1,0:T(8,128)S(1)}, u32[]{:S(2)}, u32[]{:S(2)}) collective-permute-start(f32[2,8,128]{2,1,0:T(8,128)S(1)} %get-tuple-element.186), channel_id=1, source_target_pairs={{0,1},{1,0},{2,3},{3,2},{4,5},{5,4},{6,7},{7,6},{8,9},{9,8},{10,11... | collective-permute-start | bytes 24584 | tf_op jit(solution)/shard_map/ppermute | solution.py:287
  81.5 3.1 %collective-permute-start.19 = (f32[2,8,128]{2,1,0:T(8,128)S(1)}, f32[2,8,128]{2,1,0:T(8,128)S(1)}, u32[]{:S(2)}, u32[]{:S(2)}) collective-permute-start(f32[2,8,128]{2,1,0:T(8,128)S(1)} %get-tuple-element.187), channel_id=1, source_target_pairs={{0,15},{1,2},{2,1},{3,4},{4,3},{5,6},{6,5},{7,8},{8,7},{9,10},{10,... | collective-permute-start | bytes 24584 | tf_op jit(solution)/shard_map/ppermute | solution.py:287
  85.8 2.2 %collective-permute-start.20 = (f32[2,8,128]{2,1,0:T(8,128)S(1)}, f32[2,8,128]{2,1,0:T(8,128)S(1)}, u32[]{:S(2)}, u32[]{:S(2)}) collective-permute-start(f32[2,8,128]{2,1,0:T(8,128)S(1)} %get-tuple-element.204), channel_id=1, source_target_pairs={{0,1},{1,0},{2,3},{3,2},{4,5},{5,4},{6,7},{7,6},{8,9},{9,8},{10,11... | collective-permute-start | bytes 24584 | tf_op jit(solution)/shard_map/ppermute | solution.py:287
  87.2 3.1 %collective-permute-start.21 = (f32[2,8,128]{2,1,0:T(8,128)S(1)}, f32[2,8,128]{2,1,0:T(8,128)S(1)}, u32[]{:S(2)}, u32[]{:S(2)}) collective-permute-start(f32[2,8,128]{2,1,0:T(8,128)S(1)} %get-tuple-element.205), channel_id=1, source_target_pairs={{0,15},{1,2},{2,1},{3,4},{4,3},{5,6},{6,5},{7,8},{8,7},{9,10},{10,... | collective-permute-start | bytes 24584 | tf_op jit(solution)/shard_map/ppermute | solution.py:287
  91.6 2.2 %collective-permute-start.22 = (f32[2,8,128]{2,1,0:T(8,128)S(1)}, f32[2,8,128]{2,1,0:T(8,128)S(1)}, u32[]{:S(2)}, u32[]{:S(2)}) collective-permute-start(f32[2,8,128]{2,1,0:T(8,128)S(1)} %get-tuple-element.208), channel_id=1, source_target_pairs={{0,1},{1,0},{2,3},{3,2},{4,5},{5,4},{6,7},{7,6},{8,9},{9,8},{10,11... | collective-permute-start | bytes 24584 | tf_op jit(solution)/shard_map/ppermute | solution.py:287
  93.0 3.1 %collective-permute-start.23 = (f32[2,8,128]{2,1,0:T(8,128)S(1)}, f32[2,8,128]{2,1,0:T(8,128)S(1)}, u32[]{:S(2)}, u32[]{:S(2)}) collective-permute-start(f32[2,8,128]{2,1,0:T(8,128)S(1)} %get-tuple-element.209), channel_id=1, source_target_pairs={{0,15},{1,2},{2,1},{3,4},{4,3},{5,6},{6,5},{7,8},{8,7},{9,10},{10,... | collective-permute-start | bytes 24584 | tf_op jit(solution)/shard_map/ppermute | solution.py:287
  97.3 2.4 %collective-permute-start.24 = (f32[2,8,128]{2,1,0:T(8,128)S(1)}, f32[2,8,128]{2,1,0:T(8,128)S(1)}, u32[]{:S(2)}, u32[]{:S(2)}) collective-permute-start(f32[2,8,128]{2,1,0:T(8,128)S(1)} %get-tuple-element.212), channel_id=1, source_target_pairs={{0,1},{1,0},{2,3},{3,2},{4,5},{5,4},{6,7},{7,6},{8,9},{9,8},{10,11... | collective-permute-start | bytes 24584 | tf_op jit(solution)/shard_map/ppermute | solution.py:287
  98.9 3.1 %collective-permute-start.25 = (f32[2,8,128]{2,1,0:T(8,128)S(1)}, f32[2,8,128]{2,1,0:T(8,128)S(1)}, u32[]{:S(2)}, u32[]{:S(2)}) collective-permute-start(f32[2,8,128]{2,1,0:T(8,128)S(1)} %get-tuple-element.213), channel_id=1, source_target_pairs={{0,15},{1,2},{2,1},{3,4},{4,3},{5,6},{6,5},{7,8},{8,7},{9,10},{10,... | collective-permute-start | bytes 24584 | tf_op jit(solution)/shard_map/ppermute | solution.py:287
  103.3 2.6 %collective-permute-start.26 = (f32[2,8,128]{2,1,0:T(8,128)S(1)}, f32[2,8,128]{2,1,0:T(8,128)S(1)}, u32[]{:S(2)}, u32[]{:S(2)}) collective-permute-start(f32[2,8,128]{2,1,0:T(8,128)S(1)} %get-tuple-element.216), channel_id=1, source_target_pairs={{0,1},{1,0},{2,3},{3,2},{4,5},{5,4},{6,7},{7,6},{8,9},{9,8},{10,11... | collective-permute-start | bytes 24584 | tf_op jit(solution)/shard_map/ppermute | solution.py:287
  104.6 3.1 %collective-permute-start.27 = (f32[2,8,128]{2,1,0:T(8,128)S(1)}, f32[2,8,128]{2,1,0:T(8,128)S(1)}, u32[]{:S(2)}, u32[]{:S(2)}) collective-permute-start(f32[2,8,128]{2,1,0:T(8,128)S(1)} %get-tuple-element.217), channel_id=1, source_target_pairs={{0,15},{1,2},{2,1},{3,4},{4,3},{5,6},{6,5},{7,8},{8,7},{9,10},{10,... | collective-permute-start | bytes 24584 | tf_op jit(solution)/shard_map/ppermute | solution.py:287
  109.0 2.2 %collective-permute-start.28 = (f32[2,8,128]{2,1,0:T(8,128)S(1)}, f32[2,8,128]{2,1,0:T(8,128)S(1)}, u32[]{:S(2)}, u32[]{:S(2)}) collective-permute-start(f32[2,8,128]{2,1,0:T(8,128)S(1)} %get-tuple-element.234), channel_id=1, source_target_pairs={{0,1},{1,0},{2,3},{3,2},{4,5},{5,4},{6,7},{7,6},{8,9},{9,8},{10,11... | collective-permute-start | bytes 24584 | tf_op jit(solution)/shard_map/ppermute | solution.py:287
  110.4 3.1 %collective-permute-start.29 = (f32[2,8,128]{2,1,0:T(8,128)S(1)}, f32[2,8,128]{2,1,0:T(8,128)S(1)}, u32[]{:S(2)}, u32[]{:S(2)}) collective-permute-start(f32[2,8,128]{2,1,0:T(8,128)S(1)} %get-tuple-element.235), channel_id=1, source_target_pairs={{0,15},{1,2},{2,1},{3,4},{4,3},{5,6},{6,5},{7,8},{8,7},{9,10},{10,... | collective-permute-start | bytes 24584 | tf_op jit(solution)/shard_map/ppermute | solution.py:287
  114.7 2.2 %collective-permute-start.30 = (f32[2,8,128]{2,1,0:T(8,128)S(1)}, f32[2,8,128]{2,1,0:T(8,128)S(1)}, u32[]{:S(2)}, u32[]{:S(2)}) collective-permute-start(f32[2,8,128]{2,1,0:T(8,128)S(1)} %get-tuple-element.238), channel_id=1, source_target_pairs={{0,1},{1,0},{2,3},{3,2},{4,5},{5,4},{6,7},{7,6},{8,9},{9,8},{10,11... | collective-permute-start | bytes 24584 | tf_op jit(solution)/shard_map/ppermute | solution.py:287
  116.1 3.1 %collective-permute-start.31 = (f32[2,8,128]{2,1,0:T(8,128)S(1)}, f32[2,8,128]{2,1,0:T(8,128)S(1)}, u32[]{:S(2)}, u32[]{:S(2)}) collective-permute-start(f32[2,8,128]{2,1,0:T(8,128)S(1)} %get-tuple-element.239), channel_id=1, source_target_pairs={{0,15},{1,2},{2,1},{3,4},{4,3},{5,6},{6,5},{7,8},{8,7},{9,10},{10,... | collective-permute-start | bytes 24584 | tf_op jit(solution)/shard_map/ppermute | solution.py:287
  120.5 2.2 %collective-permute-start.32 = (f32[2,8,128]{2,1,0:T(8,128)S(1)}, f32[2,8,128]{2,1,0:T(8,128)S(1)}, u32[]{:S(2)}, u32[]{:S(2)}) collective-permute-start(f32[2,8,128]{2,1,0:T(8,128)S(1)} %get-tuple-element.242), channel_id=1, source_target_pairs={{0,1},{1,0},{2,3},{3,2},{4,5},{5,4},{6,7},{7,6},{8,9},{9,8},{10,11... | collective-permute-start | bytes 24584 | tf_op jit(solution)/shard_map/ppermute | solution.py:287
  121.8 3.1 %collective-permute-start.33 = (f32[2,8,128]{2,1,0:T(8,128)S(1)}, f32[2,8,128]{2,1,0:T(8,128)S(1)}, u32[]{:S(2)}, u32[]{:S(2)}) collective-permute-start(f32[2,8,128]{2,1,0:T(8,128)S(1)} %get-tuple-element.243), channel_id=1, source_target_pairs={{0,15},{1,2},{2,1},{3,4},{4,3},{5,6},{6,5},{7,8},{8,7},{9,10},{10,... | collective-permute-start | bytes 24584 | tf_op jit(solution)/shard_map/ppermute | solution.py:287
  126.2 2.6 %collective-permute-start.34 = (f32[2,8,128]{2,1,0:T(8,128)S(1)}, f32[2,8,128]{2,1,0:T(8,128)S(1)}, u32[]{:S(2)}, u32[]{:S(2)}) collective-permute-start(f32[2,8,128]{2,1,0:T(8,128)S(1)} %get-tuple-element.245), channel_id=1, source_target_pairs={{0,1},{1,0},{2,3},{3,2},{4,5},{5,4},{6,7},{7,6},{8,9},{9,8},{10,11... | collective-permute-start | bytes 24584 | tf_op jit(solution)/shard_map/ppermute | solution.py:287
  127.6 3.1 %collective-permute-start.35 = (f32[2,8,128]{2,1,0:T(8,128)S(1)}, f32[2,8,128]{2,1,0:T(8,128)S(1)}, u32[]{:S(2)}, u32[]{:S(2)}) collective-permute-start(f32[2,8,128]{2,1,0:T(8,128)S(1)} %get-tuple-element.246), channel_id=1, source_target_pairs={{0,15},{1,2},{2,1},{3,4},{4,3},{5,6},{6,5},{7,8},{8,7},{9,10},{10,... | collective-permute-start | bytes 24584 | tf_op jit(solution)/shard_map/ppermute | solution.py:287
  132.3 15.5 %all-to-all-start.1 = ((bf16[16,8,2688]{2,1,0:T(8,128)(2,1)}), bf16[16,8,2688]{2,1,0:T(8,128)(2,1)S(1)}, u32[]{:S(2)}, u32[]{:S(2)}) async-start(bf16[16,8,2688]{2,1,0:T(8,128)(2,1)} %bitcast.14), calls=%async_computation.1 | async-start | bytes 1376256 | tf_op jit(solution)/shard_map/all_to_all | solution.py:373

commit v2 on v1

--- a/solution.py
+++ b/solution.py
@@ -21,7 +21,6 @@
 F32 = jnp.float32
 BF16 = jnp.bfloat16
 VSPEC = pl.BlockSpec(memory_space=pltpu.VMEM)
-SSPEC = pl.BlockSpec(memory_space=pltpu.SMEM)
 
 CORE_PAIRS = [(i, i ^ 1) for i in range(16)]
 Z_PAIRS = [(i, (i + 1) % 16 if i % 2 else (i - 1) % 16) for i in range(16)]
@@ -31,16 +30,28 @@
     return lax.dot_general(a, b, (((1,), (0,)), ((), ())), preferred_element_type=F32)
 
 
-def call(body, outs, args, n_smem, scratch=(), flops=0, bytes_accessed=0):
+def call(body, outs, args, scratch=(), flops=0, bytes_accessed=0):
     return pl.pallas_call(
         body,
         out_shape=outs,
-        in_specs=[SSPEC] * n_smem + [VSPEC] * (len(args) - n_smem),
+        in_specs=[VSPEC] * len(args),
         out_specs=[VSPEC] * len(outs),
         scratch_shapes=list(scratch),
         compiler_params=pltpu.CompilerParams(vmem_limit_bytes=VMEM_LIMIT),
         cost_estimate=pl.CostEstimate(flops=flops, bytes_accessed=bytes_accessed, transcendentals=0),
     )(*args)
+
+
+def scalars(ref):
+    return [ref[index, 0] for index in range(TILES + 2)]
+
+
+class Rows:
+    def __init__(self, ref):
+        self.ref = ref
+
+    def __getitem__(self, index):
+        return self.ref[index : index + 1, :]
 
 
 def send_edges(acc_ref, ints, sendc, sendz):
@@ -66,6 +77,7 @@
 
 
 def forward_body(ints, floats, marg, by_check, by_var, signs, labels, fixed, th_out, u_out, gv_out, sendc, sendz, tb):
+    ints, floats = scalars(ints), Rows(floats)
     zmask = floats[2 * TILES + 1]
     for block in range(EXT):
         th = jnp.tanh(0.5 * marg[:, block * BLK : (block + 1) * BLK])
@@ -114,6 +126,7 @@
 
 def first_body(ints, floats, marg, gv, recvc, recvz, fixed, labels, u_ref, signs, by_check,
                by_var, g_out, q_out, dz_out, acc_out, ret_out, sendc, sendz):
+    ints, floats = scalars(ints), Rows(floats)
     zmask = floats[2 * TILES + 1]
     for block in range(EXT):
         lanes = slice(block * BLK, (block + 1) * BLK)
@@ -145,6 +158,7 @@
 
 def step_body(section, ints, floats, g_in, acc_in, recvc, recvz, ret, th_ref, u_ref, signs, by_check,
               by_var, g_out, q_out, dz_out, acc_out, sendc, sendz):
+    ints, floats = scalars(ints), Rows(floats)
     for block in range(EXT):
         g = next_gradient(section + 1, g_in, acc_in, recvc, recvz, th_ref, ret, floats, block)
         g_out[block] = g
@@ -155,6 +169,7 @@
 
 
 def weights_body(section_high, count, ints, *refs):
+    ints = scalars(ints)
     th_ref, u_ref, by_check, gate_in, msg_in = refs[:5]
     q_refs = refs[5 : 5 + count]
     dz_refs = refs[5 + count : 5 + 2 * count]
@@ -209,6 +224,7 @@
 
 
 def pack_body(floats, acc_in, recvc, recvz, ret, th_ref, gate, msg, *refs):
+    floats = Rows(floats)
     g_refs = refs[:SEC]
     out = refs[SEC]
     for block in range(NB):
@@ -304,9 +320,11 @@
     core_side = jnp.where(even, NB - 1, 0)
     z_side = jnp.where(even, 0, NB - 1)
     ints = jnp.concatenate([columns, core_side[None], z_side[None]]).astype(jnp.int32)
+    ints = jnp.broadcast_to(ints[:, None], (TILES + 2, BLK))
     floats = jnp.concatenate(
         [gate_weight * live, msg_weight * live, jnp.stack([even, has_z]).astype(F32)]
     )
+    floats = jnp.broadcast_to(floats[:, None], (2 * TILES + 2, BLK))
     sent = jnp.concatenate([levels, halo_core, halo_z], axis=1).astype(jnp.float16)
     sent = sent.reshape(SEC, SH, EXT * BLK)
     sent, pattern = lax.optimization_barrier((sent, pattern))
@@ -325,7 +343,6 @@
         forward_body,
         [shape(EXT, SEC * SH, BLK), shape(NB, SEC * SH, BLK), field, wide_edge, wide_edge],
         [ints, floats, marg, *patterns, my_signs, my_labels, fixed],
-        2,
         scratch=[pltpu.VMEM((EXT, SEC * SH, BLK), BF16)],
     )
     core, z = exchange(core, z)
@@ -333,7 +350,6 @@
         first_body,
         [field, field, rows, field, shape(1, EXT * BLK), edge, edge],
         [ints, floats, marg, gv, core, z, fixed, my_labels, u, my_signs, *patterns],
-        2,
     )
     leaving = {SEC - 1: g}
     saved = [(q, dz)]
@@ -348,7 +364,6 @@
             functools.partial(step_body, section),
             [field, field, rows, field, edge, edge],
             [ints, floats, g, acc, core, z, ret_ext, th, u, my_signs, *patterns],
-            2,
         )
         leaving[section] = g
         saved.append((q, dz))
@@ -358,7 +373,6 @@
                 functools.partial(weights_body, section + group_size - 1, group_size),
                 [shape(TILES, SH, BLK)] * 2,
                 [ints, th, u, patterns[0], gate, msg] + [s[0] for s in saved] + [s[1] for s in saved],
-                1,
                 flops=2 * 2 * group_size * SH * TILES * BLK * BLK,
                 bytes_accessed=4 * 2**20,
             )
@@ -368,14 +382,12 @@
         pack_body,
         [shape(SEC * SH, LANES + GRAD_LANES, dtype=BF16)],
         [floats, acc, core, z, ret_ext, th, gate, msg] + [leaving[s] for s in range(SEC)],
-        1,
     )
     got = lax.all_to_all(packed.reshape(SEC, SH, LANES + GRAD_LANES), "section", 0, 0, tiled=True)
     input_grads, gate, msg, prior = call(
         unpack_body,
         [shape(SEC * SH, LANES), shape(1, TILES), shape(1, TILES), shape(NB, BLK)],
         [got.reshape(SEC * SH, LANES + GRAD_LANES), live[None]],
-        0,
     )
     return input_grads[None], gate.reshape(TILES), msg.reshape(TILES), prior.reshape(LANES)
 

time: 150 us -> 141 us (0.940)
  Pallas kernels: 30.6 us -> 19.5 us
  waiting for transfers between devices: 66 us -> 68.2 us
    pallas_call x23, Pallas kernels: 29.6 us -> 18.5 us  [call(): pl.pallas_call(body, out_shape=outs, in_specs=[VSPEC] * len(args), out_sp...]
    ppermute x18, waiting for transfers between devices: 36.5 us -> 38.3 us  [exchange(): lax.ppermute(z, 'tile', Z_PAIRS)]
  transfers between devices with their start and end apart: 38 -> 38, of which waited for: 32 -> 36; matrix products, arithmetic and copies ran while one was open for 2% -> 2% of each run, Pallas kernels for 4% -> 3%
where the time goes in v2:
time: 141 us; the launch traced here: 140 us
  waiting for transfers between devices  68.2 us (48%)
  starting transfers between devices  42.5 us (30%)
  Pallas kernels  19.5 us (14%)
  other arithmetic  6.33 us (4%)
  local copies, waits for them, and re-layouts  2.15 us (2%)
  between operations  1.52 us (1%)
    ppermute x18, waiting for transfers between devices, exchange(): lax.ppermute(z, 'tile', Z_PAIRS)  38.3 us
    ppermute x18, starting transfers between devices, exchange(): lax.ppermute(core, 'tile', CORE_PAIRS)  28.9 us
    pallas_call x23, Pallas kernels, call(): pl.pallas_call(body, out_shape=outs, in_specs=[VSPEC] * len(args), out_sp...  18.5 us
    all_to_all x1, waiting for transfers between devices, on_device(): lax.all_to_all(packed.reshape(SEC, SH, LANES + GRAD_LANES), 'section', 0,...  11.9 us
    ppermute x18, waiting for transfers between devices, exchange(): lax.ppermute(core, 'tile', CORE_PAIRS)  11.1 us
    all_to_all x1, waiting for transfers between devices, on_device(): marg = lax.all_to_all(sent, 'section', 0, 0, tiled=True)  6.88 us
    all_to_all x1, starting transfers between devices, on_device(): marg = lax.all_to_all(sent, 'section', 0, 0, tiled=True)  6.8 us
    all_to_all x1, starting transfers between devices, on_device(): lax.all_to_all(packed.reshape(SEC, SH, LANES + GRAD_LANES), 'section', 0,...  3.6 us
  transfers between devices with their start and end apart: 38, of which 36 were waited for; matrix products, arithmetic and copies ran while one was open for 2% of the time, Pallas kernels for 3%

profile of v2, /device:TPU:1, one launch (start us, length us, event | category | flops | bytes accessed | tf_op | source)
XLA Modules:
  0.0 140.1 jit_solution(15644098989419678347)
XLA Ops:
  0.7 0.9 slice_select_fusion.1
  1.6 3.1 %collective-permute-start.1 = (f32[128,128]{1,0:T(8,128)S(1)}, f32[128,128]{1,0:T(8,128)S(1)}, u32[]{:S(2)}, u32[]{:S(2)}) collective-permute-start(f32[128,128]{1,0:T(8,128)S(1)} %get-tuple-element.265), channel_id=1, source_target_pairs={{0,15},{1,2},{2,1},{3,4},{4,3},{5,6},{6,5},{7,8},{8,7},{9,10},{10,... | collective-permute-start | bytes 196616 | tf_op jit(solution)/shard_map/ppermute | solution.py:303
  4.7 3.8 %collective-permute-start = (f32[128,128]{1,0:T(8,128)S(1)}, f32[128,128]{1,0:T(8,128)S(1)}, u32[]{:S(2)}, u32[]{:S(2)}) collective-permute-start(f32[128,128]{1,0:T(8,128)S(1)} %get-tuple-element.264), channel_id=1, source_target_pairs={{0,1},{1,0},{2,3},{3,2},{4,5},{5,4},{6,7},{7,6},{8,9},{9,8},{10,11... | collective-permute-start | bytes 196616 | tf_op jit(solution)/shard_map/ppermute | solution.py:303
  8.5 1.3 convert_bitcast_fusion
  10.5 0.8 dynamic-slice_convert_fusion.labels
  11.5 1.0 pad_maximum_fusion
  12.5 6.8 %all-to-all-start = ((f16[16,8,2304]{2,1,0:T(8,128)(2,1)}), f16[16,8,2304]{2,1,0:T(8,128)(2,1)}, u32[]{:S(2)}, u32[]{:S(2)}) async-start(f16[16,8,2304]{2,1,0:T(8,128)(2,1)} %pad_maximum_fusion), calls=%async_computation | async-start | bytes 1179648 | tf_op jit(solution)/shard_map/all_to_all | solution.py:332
  19.5 0.9 maximum_maximum_fusion
  20.4 1.9 %copy-done = s32[48,128,128]{2,1,0:T(8,128)S(1)} copy-done((s32[48,128,128]{2,1,0:T(8,128)S(1)}, s32[48,128,128]{2,1,0:T(8,128)}, u32[]{:S(2)}) %copy-start) | copy-done | bytes 3145752
  22.3 1.0 shard_map.129
  23.3 6.9 %all-to-all-done = f16[16,8,2304]{2,1,0:T(8,128)(2,1)} async-done(((f16[16,8,2304]{2,1,0:T(8,128)(2,1)}), f16[16,8,2304]{2,1,0:T(8,128)(2,1)}, u32[]{:S(2)}, u32[]{:S(2)}) %all-to-all-start) | async-done | bytes 589856 | tf_op jit(solution)/shard_map/all_to_all | solution.py:332
  30.2 1.1 bitcast_convert_fusion.marg
  31.4 1.1 shard_map.130
  32.5 2.5 %collective-permute-start.2 = (f32[4,8,128]{2,1,0:T(8,128)S(1)}, f32[4,8,128]{2,1,0:T(8,128)S(1)}, u32[]{:S(2)}, u32[]{:S(2)}) collective-permute-start(f32[4,8,128]{2,1,0:T(8,128)S(1)} %get-tuple-element.139), channel_id=1, source_target_pairs={{0,1},{1,0},{2,3},{3,2},{4,5},{5,4},{6,7},{7,6},{8,9},{9,8},{10,11... | collective-permute-start | bytes 49160 | tf_op jit(solution)/shard_map/ppermute | solution.py:303
  35.0 0.8 collective-permute-done.2.recvc
  35.9 2.3 %collective-permute-done.3.recvz = f32[4,8,128]{2,1,0:T(8,128)S(1)} collective-permute-done((f32[4,8,128]{2,1,0:T(8,128)S(1)}, f32[4,8,128]{2,1,0:T(8,128)S(1)}, u32[]{:S(2)}, u32[]{:S(2)}) %collective-permute-start.3) | collective-permute-done | bytes 16416 | tf_op jit(solution)/shard_map/ppermute | solution.py:303
  39.0 1.4 collective-permute-start.4
  40.4 0.8 collective-permute-done.4.recvc
  41.2 2.2 %collective-permute-done.5.recvz = f32[2,8,128]{2,1,0:T(8,128)S(1)} collective-permute-done((f32[2,8,128]{2,1,0:T(8,128)S(1)}, f32[2,8,128]{2,1,0:T(8,128)S(1)}, u32[]{:S(2)}, u32[]{:S(2)}) %collective-permute-start.5) | collective-permute-done | bytes 8224 | tf_op jit(solution)/shard_map/ppermute | solution.py:303
  44.2 1.4 collective-permute-start.6
  45.6 0.8 collective-permute-done.6.recvc
  46.4 2.2 %collective-permute-done.7.recvz = f32[2,8,128]{2,1,0:T(8,128)S(1)} collective-permute-done((f32[2,8,128]{2,1,0:T(8,128)S(1)}, f32[2,8,128]{2,1,0:T(8,128)S(1)}, u32[]{:S(2)}, u32[]{:S(2)}) %collective-permute-start.7) | collective-permute-done | bytes 8224 | tf_op jit(solution)/shard_map/ppermute | solution.py:303
  49.4 1.4 collective-permute-start.8
  50.8 0.8 collective-permute-done.8.recvc
  51.7 2.2 %collective-permute-done.9.recvz = f32[2,8,128]{2,1,0:T(8,128)S(1)} collective-permute-done((f32[2,8,128]{2,1,0:T(8,128)S(1)}, f32[2,8,128]{2,1,0:T(8,128)S(1)}, u32[]{:S(2)}, u32[]{:S(2)}) %collective-permute-start.9) | collective-permute-done | bytes 8224 | tf_op jit(solution)/shard_map/ppermute | solution.py:303
  54.7 1.4 collective-permute-start.10
  56.9 2.2 %collective-permute-done.11.recvz = f32[2,8,128]{2,1,0:T(8,128)S(1)} collective-permute-done((f32[2,8,128]{2,1,0:T(8,128)S(1)}, f32[2,8,128]{2,1,0:T(8,128)S(1)}, u32[]{:S(2)}, u32[]{:S(2)}) %collective-permute-start.11) | collective-permute-done | bytes 8224 | tf_op jit(solution)/shard_map/ppermute | solution.py:303
  59.9 1.6 %collective-permute-start.12 = (f32[2,8,128]{2,1,0:T(8,128)S(1)}, f32[2,8,128]{2,1,0:T(8,128)S(1)}, u32[]{:S(2)}, u32[]{:S(2)}) collective-permute-start(f32[2,8,128]{2,1,0:T(8,128)S(1)} %get-tuple-element.174), channel_id=1, source_target_pairs={{0,1},{1,0},{2,3},{3,2},{4,5},{5,4},{6,7},{7,6},{8,9},{9,8},{10,11... | collective-permute-start | bytes 24584 | tf_op jit(solution)/shard_map/ppermute | solution.py:303
  61.5 0.8 collective-permute-done.12.recvc
  62.3 2.2 %collective-permute-done.13.recvz = f32[2,8,128]{2,1,0:T(8,128)S(1)} collective-permute-done((f32[2,8,128]{2,1,0:T(8,128)S(1)}, f32[2,8,128]{2,1,0:T(8,128)S(1)}, u32[]{:S(2)}, u32[]{:S(2)}) %collective-permute-start.13) | collective-permute-done | bytes 8224 | tf_op jit(solution)/shard_map/ppermute | solution.py:303
  65.3 1.4 collective-permute-start.14
  66.7 0.8 collective-permute-done.14.recvc
  67.5 2.2 %collective-permute-done.15.recvz = f32[2,8,128]{2,1,0:T(8,128)S(1)} collective-permute-done((f32[2,8,128]{2,1,0:T(8,128)S(1)}, f32[2,8,128]{2,1,0:T(8,128)S(1)}, u32[]{:S(2)}, u32[]{:S(2)}) %collective-permute-start.15) | collective-permute-done | bytes 8224 | tf_op jit(solution)/shard_map/ppermute | solution.py:303
  70.6 1.4 collective-permute-start.16
  72.0 0.8 collective-permute-done.16.recvc
  72.8 2.2 %collective-permute-done.17.recvz = f32[2,8,128]{2,1,0:T(8,128)S(1)} collective-permute-done((f32[2,8,128]{2,1,0:T(8,128)S(1)}, f32[2,8,128]{2,1,0:T(8,128)S(1)}, u32[]{:S(2)}, u32[]{:S(2)}) %collective-permute-start.17) | collective-permute-done | bytes 8224 | tf_op jit(solution)/shard_map/ppermute | solution.py:303
  75.8 1.4 collective-permute-start.18
  78.0 2.2 %collective-permute-done.19.recvz = f32[2,8,128]{2,1,0:T(8,128)S(1)} collective-permute-done((f32[2,8,128]{2,1,0:T(8,128)S(1)}, f32[2,8,128]{2,1,0:T(8,128)S(1)}, u32[]{:S(2)}, u32[]{:S(2)}) %collective-permute-start.19) | collective-permute-done | bytes 8224 | tf_op jit(solution)/shard_map/ppermute | solution.py:303
  81.0 1.4 collective-permute-start.20
  82.4 0.8 collective-permute-done.20.recvc
  83.2 2.2 %collective-permute-done.21.recvz = f32[2,8,128]{2,1,0:T(8,128)S(1)} collective-permute-done((f32[2,8,128]{2,1,0:T(8,128)S(1)}, f32[2,8,128]{2,1,0:T(8,128)S(1)}, u32[]{:S(2)}, u32[]{:S(2)}) %collective-permute-start.21) | collective-permute-done | bytes 8224 | tf_op jit(solution)/shard_map/ppermute | solution.py:303
  86.3 1.4 collective-permute-start.22
  87.7 0.8 collective-permute-done.22.recvc
  88.5 2.2 %collective-permute-done.23.recvz = f32[2,8,128]{2,1,0:T(8,128)S(1)} collective-permute-done((f32[2,8,128]{2,1,0:T(8,128)S(1)}, f32[2,8,128]{2,1,0:T(8,128)S(1)}, u32[]{:S(2)}, u32[]{:S(2)}) %collective-permute-start.23) | collective-permute-done | bytes 8224 | tf_op jit(solution)/shard_map/ppermute | solution.py:303
  91.5 1.6 %collective-permute-start.24 = (f32[2,8,128]{2,1,0:T(8,128)S(1)}, f32[2,8,128]{2,1,0:T(8,128)S(1)}, u32[]{:S(2)}, u32[]{:S(2)}) collective-permute-start(f32[2,8,128]{2,1,0:T(8,128)S(1)} %get-tuple-element.212), channel_id=1, source_target_pairs={{0,1},{1,0},{2,3},{3,2},{4,5},{5,4},{6,7},{7,6},{8,9},{9,8},{10,11... | collective-permute-start | bytes 24584 | tf_op jit(solution)/shard_map/ppermute | solution.py:303
  93.1 0.8 collective-permute-done.24.recvc
  93.9 2.2 %collective-permute-done.25.recvz = f32[2,8,128]{2,1,0:T(8,128)S(1)} collective-permute-done((f32[2,8,128]{2,1,0:T(8,128)S(1)}, f32[2,8,128]{2,1,0:T(8,128)S(1)}, u32[]{:S(2)}, u32[]{:S(2)}) %collective-permute-start.25) | collective-permute-done | bytes 8224 | tf_op jit(solution)/shard_map/ppermute | solution.py:303
  97.0 1.4 collective-permute-start.26
  99.2 2.2 %collective-permute-done.27.recvz = f32[2,8,128]{2,1,0:T(8,128)S(1)} collective-permute-done((f32[2,8,128]{2,1,0:T(8,128)S(1)}, f32[2,8,128]{2,1,0:T(8,128)S(1)}, u32[]{:S(2)}, u32[]{:S(2)}) %collective-permute-start.27) | collective-permute-done | bytes 8224 | tf_op jit(solution)/shard_map/ppermute | solution.py:303
  102.2 1.4 collective-permute-start.28
  103.6 0.8 collective-permute-done.28.recvc
  104.4 2.2 %collective-permute-done.29.recvz = f32[2,8,128]{2,1,0:T(8,128)S(1)} collective-permute-done((f32[2,8,128]{2,1,0:T(8,128)S(1)}, f32[2,8,128]{2,1,0:T(8,128)S(1)}, u32[]{:S(2)}, u32[]{:S(2)}) %collective-permute-start.29) | collective-permute-done | bytes 8224 | tf_op jit(solution)/shard_map/ppermute | solution.py:303
  107.4 1.4 collective-permute-start.30
  108.8 0.8 collective-permute-done.30.recvc
  109.6 2.2 %collective-permute-done.31.recvz = f32[2,8,128]{2,1,0:T(8,128)S(1)} collective-permute-done((f32[2,8,128]{2,1,0:T(8,128)S(1)}, f32[2,8,128]{2,1,0:T(8,128)S(1)}, u32[]{:S(2)}, u32[]{:S(2)}) %collective-permute-start.31) | collective-permute-done | bytes 8224 | tf_op jit(solution)/shard_map/ppermute | solution.py:303
  112.6 1.4 collective-permute-start.32
  114.0 0.8 collective-permute-done.32.recvc
  114.9 2.2 %collective-permute-done.33.recvz = f32[2,8,128]{2,1,0:T(8,128)S(1)} collective-permute-done((f32[2,8,128]{2,1,0:T(8,128)S(1)}, f32[2,8,128]{2,1,0:T(8,128)S(1)}, u32[]{:S(2)}, u32[]{:S(2)}) %collective-permute-start.33) | collective-permute-done | bytes 8224 | tf_op jit(solution)/shard_map/ppermute | solution.py:303
  117.9 1.4 collective-permute-start.34
  120.1 2.2 %collective-permute-done.35.recvz = f32[2,8,128]{2,1,0:T(8,128)S(1)} collective-permute-done((f32[2,8,128]{2,1,0:T(8,128)S(1)}, f32[2,8,128]{2,1,0:T(8,128)S(1)}, u32[]{:S(2)}, u32[]{:S(2)}) %collective-permute-start.35) | collective-permute-done | bytes 8224 | tf_op jit(solution)/shard_map/ppermute | solution.py:303
  122.4 1.1 shard_map.151
  123.5 3.6 %all-to-all-start.1 = ((bf16[16,8,2688]{2,1,0:T(8,128)(2,1)}), bf16[16,8,2688]{2,1,0:T(8,128)(2,1)S(1)}, u32[]{:S(2)}, u32[]{:S(2)}) async-start(bf16[16,8,2688]{2,1,0:T(8,128)(2,1)} %bitcast.14), calls=%async_computation.1 | async-start | bytes 1376256 | tf_op jit(solution)/shard_map/all_to_all | solution.py:386
  127.1 11.9 %all-to-all-done.1 = bf16[16,8,2688]{2,1,0:T(8,128)(2,1)S(1)} async-done(((bf16[16,8,2688]{2,1,0:T(8,128)(2,1)}), bf16[16,8,2688]{2,1,0:T(8,128)(2,1)S(1)}, u32[]{:S(2)}, u32[]{:S(2)}) %all-to-all-start.1) | async-done | bytes 688160 | tf_op jit(solution)/shard_map/all_to_all | solution.py:386
  139.0 1.1 shard_map.152
  (67 shorter events, 16.2 us)
Async XLA Ops:
  0.6 10.7 %copy-start.3 = (f32[48]{0:T(128)S(1)}, f32[48]{0:T(128)}, u32[]{:S(2)}) copy-start(f32[48]{0:T(128)} %param.19) | copy-start | bytes 580
  0.6 10.7 %copy-start.4 = (f32[48]{0:T(128)S(1)}, f32[48]{0:T(128)}, u32[]{:S(2)}) copy-start(f32[48]{0:T(128)} %param.18) | copy-start | bytes 580
  0.7 10.7 %copy-start.5 = (s32[48]{0:T(128)S(1)}, s32[48]{0:T(128)}, u32[]{:S(2)}) copy-start(s32[48]{0:T(128)} %param.15) | copy-start | bytes 580
  1.6 9.9 %collective-permute-start.1 = (f32[128,128]{1,0:T(8,128)S(1)}, f32[128,128]{1,0:T(8,128)S(1)}, u32[]{:S(2)}, u32[]{:S(2)}) collective-permute-start(f32[128,128]{1,0:T(8,128)S(1)} %get-tuple-element.265), channel_id=1, source_target_pairs={{0,15},{1,2},{2,1},{3,4},{4,3},{5,6},{6,5},{7,8},{8,7},{9,10},{10,... | collective-permute-start | bytes 196616 | tf_op jit(solution)/shard_map/ppermute | solution.py:303
  4.7 6.8 %collective-permute-start = (f32[128,128]{1,0:T(8,128)S(1)}, f32[128,128]{1,0:T(8,128)S(1)}, u32[]{:S(2)}, u32[]{:S(2)}) collective-permute-start(f32[128,128]{1,0:T(8,128)S(1)} %get-tuple-element.264), channel_id=1, source_target_pairs={{0,1},{1,0},{2,3},{3,2},{4,5},{5,4},{6,7},{7,6},{8,9},{9,8},{10,11... | collective-permute-start | bytes 196616 | tf_op jit(solution)/shard_map/ppermute | solution.py:303
  9.7 9.8 %copy-start.1 = (f32[2048]{0:T(1024)S(1)}, f32[2048]{0:T(1024)}, u32[]{:S(2)}) copy-start(f32[2048]{0:T(1024)} %param.12) | copy-start | bytes 24580
  9.8 9.7 %copy-start.2 = (f32[2048]{0:T(1024)S(1)}, f32[2048]{0:T(1024)}, u32[]{:S(2)}) copy-start(f32[2048]{0:T(1024)} %param.11) | copy-start | bytes 24580
  12.5 17.6 %all-to-all-start = ((f16[16,8,2304]{2,1,0:T(8,128)(2,1)}), f16[16,8,2304]{2,1,0:T(8,128)(2,1)}, u32[]{:S(2)}, u32[]{:S(2)}) async-start(f16[16,8,2304]{2,1,0:T(8,128)(2,1)} %pad_maximum_fusion), calls=%async_computation | async-start | bytes 1179648 | tf_op jit(solution)/shard_map/all_to_all | solution.py:332
  20.4 1.9 %copy-start = (s32[48,128,128]{2,1,0:T(8,128)S(1)}, s32[48,128,128]{2,1,0:T(8,128)}, u32[]{:S(2)}) copy-start(s32[48,128,128]{2,1,0:T(8,128)} %param.17) | copy-start | bytes 9437188
  32.5 3.3 %collective-permute-start.2 = (f32[4,8,128]{2,1,0:T(8,128)S(1)}, f32[4,8,128]{2,1,0:T(8,128)S(1)}, u32[]{:S(2)}, u32[]{:S(2)}) collective-permute-start(f32[4,8,128]{2,1,0:T(8,128)S(1)} %get-tuple-element.139), channel_id=1, source_target_pairs={{0,1},{1,0},{2,3},{3,2},{4,5},{5,4},{6,7},{7,6},{8,9},{9,8},{10,11... | collective-permute-start | bytes 49160 | tf_op jit(solution)/shard_map/ppermute | solution.py:303
  35.0 3.2 %collective-permute-start.3 = (f32[4,8,128]{2,1,0:T(8,128)S(1)}, f32[4,8,128]{2,1,0:T(8,128)S(1)}, u32[]{:S(2)}, u32[]{:S(2)}) collective-permute-start(f32[4,8,128]{2,1,0:T(8,128)S(1)} %get-tuple-element.140), channel_id=1, source_target_pairs={{0,15},{1,2},{2,1},{3,4},{4,3},{5,6},{6,5},{7,8},{8,7},{9,10},{10,... | collective-permute-start | bytes 49160 | tf_op jit(solution)/shard_map/ppermute | solution.py:303
  39.0 2.2 %collective-permute-start.4 = (f32[2,8,128]{2,1,0:T(8,128)S(1)}, f32[2,8,128]{2,1,0:T(8,128)S(1)}, u32[]{:S(2)}, u32[]{:S(2)}) collective-permute-start(f32[2,8,128]{2,1,0:T(8,128)S(1)} %get-tuple-element.144), channel_id=1, source_target_pairs={{0,1},{1,0},{2,3},{3,2},{4,5},{5,4},{6,7},{7,6},{8,9},{9,8},{10,11... | collective-permute-start | bytes 24584 | tf_op jit(solution)/shard_map/ppermute | solution.py:303
  40.4 3.1 %collective-permute-start.5 = (f32[2,8,128]{2,1,0:T(8,128)S(1)}, f32[2,8,128]{2,1,0:T(8,128)S(1)}, u32[]{:S(2)}, u32[]{:S(2)}) collective-permute-start(f32[2,8,128]{2,1,0:T(8,128)S(1)} %get-tuple-element.145), channel_id=1, source_target_pairs={{0,15},{1,2},{2,1},{3,4},{4,3},{5,6},{6,5},{7,8},{8,7},{9,10},{10,... | collective-permute-start | bytes 24584 | tf_op jit(solution)/shard_map/ppermute | solution.py:303
  44.2 2.2 %collective-permute-start.6 = (f32[2,8,128]{2,1,0:T(8,128)S(1)}, f32[2,8,128]{2,1,0:T(8,128)S(1)}, u32[]{:S(2)}, u32[]{:S(2)}) collective-permute-start(f32[2,8,128]{2,1,0:T(8,128)S(1)} %get-tuple-element.150), channel_id=1, source_target_pairs={{0,1},{1,0},{2,3},{3,2},{4,5},{5,4},{6,7},{7,6},{8,9},{9,8},{10,11... | collective-permute-start | bytes 24584 | tf_op jit(solution)/shard_map/ppermute | solution.py:303
  45.6 3.1 %collective-permute-start.7 = (f32[2,8,128]{2,1,0:T(8,128)S(1)}, f32[2,8,128]{2,1,0:T(8,128)S(1)}, u32[]{:S(2)}, u32[]{:S(2)}) collective-permute-start(f32[2,8,128]{2,1,0:T(8,128)S(1)} %get-tuple-element.151), channel_id=1, source_target_pairs={{0,15},{1,2},{2,1},{3,4},{4,3},{5,6},{6,5},{7,8},{8,7},{9,10},{10,... | collective-permute-start | bytes 24584 | tf_op jit(solution)/shard_map/ppermute | solution.py:303
  49.4 2.2 %collective-permute-start.8 = (f32[2,8,128]{2,1,0:T(8,128)S(1)}, f32[2,8,128]{2,1,0:T(8,128)S(1)}, u32[]{:S(2)}, u32[]{:S(2)}) collective-permute-start(f32[2,8,128]{2,1,0:T(8,128)S(1)} %get-tuple-element.154), channel_id=1, source_target_pairs={{0,1},{1,0},{2,3},{3,2},{4,5},{5,4},{6,7},{7,6},{8,9},{9,8},{10,11... | collective-permute-start | bytes 24584 | tf_op jit(solution)/shard_map/ppermute | solution.py:303
  50.8 3.1 %collective-permute-start.9 = (f32[2,8,128]{2,1,0:T(8,128)S(1)}, f32[2,8,128]{2,1,0:T(8,128)S(1)}, u32[]{:S(2)}, u32[]{:S(2)}) collective-permute-start(f32[2,8,128]{2,1,0:T(8,128)S(1)} %get-tuple-element.155), channel_id=1, source_target_pairs={{0,15},{1,2},{2,1},{3,4},{4,3},{5,6},{6,5},{7,8},{8,7},{9,10},{10,... | collective-permute-start | bytes 24584 | tf_op jit(solution)/shard_map/ppermute | solution.py:303
  54.7 2.2 %collective-permute-start.10 = (f32[2,8,128]{2,1,0:T(8,128)S(1)}, f32[2,8,128]{2,1,0:T(8,128)S(1)}, u32[]{:S(2)}, u32[]{:S(2)}) collective-permute-start(f32[2,8,128]{2,1,0:T(8,128)S(1)} %get-tuple-element.158), channel_id=1, source_target_pairs={{0,1},{1,0},{2,3},{3,2},{4,5},{5,4},{6,7},{7,6},{8,9},{9,8},{10,11... | collective-permute-start | bytes 24584 | tf_op jit(solution)/shard_map/ppermute | solution.py:303
  56.1 3.1 %collective-permute-start.11 = (f32[2,8,128]{2,1,0:T(8,128)S(1)}, f32[2,8,128]{2,1,0:T(8,128)S(1)}, u32[]{:S(2)}, u32[]{:S(2)}) collective-permute-start(f32[2,8,128]{2,1,0:T(8,128)S(1)} %get-tuple-element.159), channel_id=1, source_target_pairs={{0,15},{1,2},{2,1},{3,4},{4,3},{5,6},{6,5},{7,8},{8,7},{9,10},{10,... | collective-permute-start | bytes 24584 | tf_op jit(solution)/shard_map/ppermute | solution.py:303
  59.9 2.4 %collective-permute-start.12 = (f32[2,8,128]{2,1,0:T(8,128)S(1)}, f32[2,8,128]{2,1,0:T(8,128)S(1)}, u32[]{:S(2)}, u32[]{:S(2)}) collective-permute-start(f32[2,8,128]{2,1,0:T(8,128)S(1)} %get-tuple-element.174), channel_id=1, source_target_pairs={{0,1},{1,0},{2,3},{3,2},{4,5},{5,4},{6,7},{7,6},{8,9},{9,8},{10,11... | collective-permute-start | bytes 24584 | tf_op jit(solution)/shard_map/ppermute | solution.py:303
  61.5 3.1 %collective-permute-start.13 = (f32[2,8,128]{2,1,0:T(8,128)S(1)}, f32[2,8,128]{2,1,0:T(8,128)S(1)}, u32[]{:S(2)}, u32[]{:S(2)}) collective-permute-start(f32[2,8,128]{2,1,0:T(8,128)S(1)} %get-tuple-element.175), channel_id=1, source_target_pairs={{0,15},{1,2},{2,1},{3,4},{4,3},{5,6},{6,5},{7,8},{8,7},{9,10},{10,... | collective-permute-start | bytes 24584 | tf_op jit(solution)/shard_map/ppermute | solution.py:303
  65.3 2.2 %collective-permute-start.14 = (f32[2,8,128]{2,1,0:T(8,128)S(1)}, f32[2,8,128]{2,1,0:T(8,128)S(1)}, u32[]{:S(2)}, u32[]{:S(2)}) collective-permute-start(f32[2,8,128]{2,1,0:T(8,128)S(1)} %get-tuple-element.178), channel_id=1, source_target_pairs={{0,1},{1,0},{2,3},{3,2},{4,5},{5,4},{6,7},{7,6},{8,9},{9,8},{10,11... | collective-permute-start | bytes 24584 | tf_op jit(solution)/shard_map/ppermute | solution.py:303
  66.7 3.1 %collective-permute-start.15 = (f32[2,8,128]{2,1,0:T(8,128)S(1)}, f32[2,8,128]{2,1,0:T(8,128)S(1)}, u32[]{:S(2)}, u32[]{:S(2)}) collective-permute-start(f32[2,8,128]{2,1,0:T(8,128)S(1)} %get-tuple-element.179), channel_id=1, source_target_pairs={{0,15},{1,2},{2,1},{3,4},{4,3},{5,6},{6,5},{7,8},{8,7},{9,10},{10,... | collective-permute-start | bytes 24584 | tf_op jit(solution)/shard_map/ppermute | solution.py:303
  70.6 2.2 %collective-permute-start.16 = (f32[2,8,128]{2,1,0:T(8,128)S(1)}, f32[2,8,128]{2,1,0:T(8,128)S(1)}, u32[]{:S(2)}, u32[]{:S(2)}) collective-permute-start(f32[2,8,128]{2,1,0:T(8,128)S(1)} %get-tuple-element.182), channel_id=1, source_target_pairs={{0,1},{1,0},{2,3},{3,2},{4,5},{5,4},{6,7},{7,6},{8,9},{9,8},{10,11... | collective-permute-start | bytes 24584 | tf_op jit(solution)/shard_map/ppermute | solution.py:303
  71.9 3.1 %collective-permute-start.17 = (f32[2,8,128]{2,1,0:T(8,128)S(1)}, f32[2,8,128]{2,1,0:T(8,128)S(1)}, u32[]{:S(2)}, u32[]{:S(2)}) collective-permute-start(f32[2,8,128]{2,1,0:T(8,128)S(1)} %get-tuple-element.183), channel_id=1, source_target_pairs={{0,15},{1,2},{2,1},{3,4},{4,3},{5,6},{6,5},{7,8},{8,7},{9,10},{10,... | collective-permute-start | bytes 24584 | tf_op jit(solution)/shard_map/ppermute | solution.py:303
  75.8 2.2 %collective-permute-start.18 = (f32[2,8,128]{2,1,0:T(8,128)S(1)}, f32[2,8,128]{2,1,0:T(8,128)S(1)}, u32[]{:S(2)}, u32[]{:S(2)}) collective-permute-start(f32[2,8,128]{2,1,0:T(8,128)S(1)} %get-tuple-element.186), channel_id=1, source_target_pairs={{0,1},{1,0},{2,3},{3,2},{4,5},{5,4},{6,7},{7,6},{8,9},{9,8},{10,11... | collective-permute-start | bytes 24584 | tf_op jit(solution)/shard_map/ppermute | solution.py:303
  77.2 3.1 %collective-permute-start.19 = (f32[2,8,128]{2,1,0:T(8,128)S(1)}, f32[2,8,128]{2,1,0:T(8,128)S(1)}, u32[]{:S(2)}, u32[]{:S(2)}) collective-permute-start(f32[2,8,128]{2,1,0:T(8,128)S(1)} %get-tuple-element.187), channel_id=1, source_target_pairs={{0,15},{1,2},{2,1},{3,4},{4,3},{5,6},{6,5},{7,8},{8,7},{9,10},{10,... | collective-permute-start | bytes 24584 | tf_op jit(solution)/shard_map/ppermute | solution.py:303
  81.0 2.2 %collective-permute-start.20 = (f32[2,8,128]{2,1,0:T(8,128)S(1)}, f32[2,8,128]{2,1,0:T(8,128)S(1)}, u32[]{:S(2)}, u32[]{:S(2)}) collective-permute-start(f32[2,8,128]{2,1,0:T(8,128)S(1)} %get-tuple-element.204), channel_id=1, source_target_pairs={{0,1},{1,0},{2,3},{3,2},{4,5},{5,4},{6,7},{7,6},{8,9},{9,8},{10,11... | collective-permute-start | bytes 24584 | tf_op jit(solution)/shard_map/ppermute | solution.py:303
  82.4 3.1 %collective-permute-start.21 = (f32[2,8,128]{2,1,0:T(8,128)S(1)}, f32[2,8,128]{2,1,0:T(8,128)S(1)}, u32[]{:S(2)}, u32[]{:S(2)}) collective-permute-start(f32[2,8,128]{2,1,0:T(8,128)S(1)} %get-tuple-element.205), channel_id=1, source_target_pairs={{0,15},{1,2},{2,1},{3,4},{4,3},{5,6},{6,5},{7,8},{8,7},{9,10},{10,... | collective-permute-start | bytes 24584 | tf_op jit(solution)/shard_map/ppermute | solution.py:303
  86.3 2.2 %collective-permute-start.22 = (f32[2,8,128]{2,1,0:T(8,128)S(1)}, f32[2,8,128]{2,1,0:T(8,128)S(1)}, u32[]{:S(2)}, u32[]{:S(2)}) collective-permute-start(f32[2,8,128]{2,1,0:T(8,128)S(1)} %get-tuple-element.208), channel_id=1, source_target_pairs={{0,1},{1,0},{2,3},{3,2},{4,5},{5,4},{6,7},{7,6},{8,9},{9,8},{10,11... | collective-permute-start | bytes 24584 | tf_op jit(solution)/shard_map/ppermute | solution.py:303
  87.7 3.1 %collective-permute-start.23 = (f32[2,8,128]{2,1,0:T(8,128)S(1)}, f32[2,8,128]{2,1,0:T(8,128)S(1)}, u32[]{:S(2)}, u32[]{:S(2)}) collective-permute-start(f32[2,8,128]{2,1,0:T(8,128)S(1)} %get-tuple-element.209), channel_id=1, source_target_pairs={{0,15},{1,2},{2,1},{3,4},{4,3},{5,6},{6,5},{7,8},{8,7},{9,10},{10,... | collective-permute-start | bytes 24584 | tf_op jit(solution)/shard_map/ppermute | solution.py:303
  91.5 2.4 %collective-permute-start.24 = (f32[2,8,128]{2,1,0:T(8,128)S(1)}, f32[2,8,128]{2,1,0:T(8,128)S(1)}, u32[]{:S(2)}, u32[]{:S(2)}) collective-permute-start(f32[2,8,128]{2,1,0:T(8,128)S(1)} %get-tuple-element.212), channel_id=1, source_target_pairs={{0,1},{1,0},{2,3},{3,2},{4,5},{5,4},{6,7},{7,6},{8,9},{9,8},{10,11... | collective-permute-start | bytes 24584 | tf_op jit(solution)/shard_map/ppermute | solution.py:303
  93.1 3.1 %collective-permute-start.25 = (f32[2,8,128]{2,1,0:T(8,128)S(1)}, f32[2,8,128]{2,1,0:T(8,128)S(1)}, u32[]{:S(2)}, u32[]{:S(2)}) collective-permute-start(f32[2,8,128]{2,1,0:T(8,128)S(1)} %get-tuple-element.213), channel_id=1, source_target_pairs={{0,15},{1,2},{2,1},{3,4},{4,3},{5,6},{6,5},{7,8},{8,7},{9,10},{10,... | collective-permute-start | bytes 24584 | tf_op jit(solution)/shard_map/ppermute | solution.py:303
  97.0 2.2 %collective-permute-start.26 = (f32[2,8,128]{2,1,0:T(8,128)S(1)}, f32[2,8,128]{2,1,0:T(8,128)S(1)}, u32[]{:S(2)}, u32[]{:S(2)}) collective-permute-start(f32[2,8,128]{2,1,0:T(8,128)S(1)} %get-tuple-element.216), channel_id=1, source_target_pairs={{0,1},{1,0},{2,3},{3,2},{4,5},{5,4},{6,7},{7,6},{8,9},{9,8},{10,11... | collective-permute-start | bytes 24584 | tf_op jit(solution)/shard_map/ppermute | solution.py:303
  98.3 3.1 %collective-permute-start.27 = (f32[2,8,128]{2,1,0:T(8,128)S(1)}, f32[2,8,128]{2,1,0:T(8,128)S(1)}, u32[]{:S(2)}, u32[]{:S(2)}) collective-permute-start(f32[2,8,128]{2,1,0:T(8,128)S(1)} %get-tuple-element.217), channel_id=1, source_target_pairs={{0,15},{1,2},{2,1},{3,4},{4,3},{5,6},{6,5},{7,8},{8,7},{9,10},{10,... | collective-permute-start | bytes 24584 | tf_op jit(solution)/shard_map/ppermute | solution.py:303
  102.2 2.2 %collective-permute-start.28 = (f32[2,8,128]{2,1,0:T(8,128)S(1)}, f32[2,8,128]{2,1,0:T(8,128)S(1)}, u32[]{:S(2)}, u32[]{:S(2)}) collective-permute-start(f32[2,8,128]{2,1,0:T(8,128)S(1)} %get-tuple-element.234), channel_id=1, source_target_pairs={{0,1},{1,0},{2,3},{3,2},{4,5},{5,4},{6,7},{7,6},{8,9},{9,8},{10,11... | collective-permute-start | bytes 24584 | tf_op jit(solution)/shard_map/ppermute | solution.py:303
  103.6 3.1 %collective-permute-start.29 = (f32[2,8,128]{2,1,0:T(8,128)S(1)}, f32[2,8,128]{2,1,0:T(8,128)S(1)}, u32[]{:S(2)}, u32[]{:S(2)}) collective-permute-start(f32[2,8,128]{2,1,0:T(8,128)S(1)} %get-tuple-element.235), channel_id=1, source_target_pairs={{0,15},{1,2},{2,1},{3,4},{4,3},{5,6},{6,5},{7,8},{8,7},{9,10},{10,... | collective-permute-start | bytes 24584 | tf_op jit(solution)/shard_map/ppermute | solution.py:303
  107.4 2.2 %collective-permute-start.30 = (f32[2,8,128]{2,1,0:T(8,128)S(1)}, f32[2,8,128]{2,1,0:T(8,128)S(1)}, u32[]{:S(2)}, u32[]{:S(2)}) collective-permute-start(f32[2,8,128]{2,1,0:T(8,128)S(1)} %get-tuple-element.238), channel_id=1, source_target_pairs={{0,1},{1,0},{2,3},{3,2},{4,5},{5,4},{6,7},{7,6},{8,9},{9,8},{10,11... | collective-permute-start | bytes 24584 | tf_op jit(solution)/shard_map/ppermute | solution.py:303
  108.8 3.1 %collective-permute-start.31 = (f32[2,8,128]{2,1,0:T(8,128)S(1)}, f32[2,8,128]{2,1,0:T(8,128)S(1)}, u32[]{:S(2)}, u32[]{:S(2)}) collective-permute-start(f32[2,8,128]{2,1,0:T(8,128)S(1)} %get-tuple-element.239), channel_id=1, source_target_pairs={{0,15},{1,2},{2,1},{3,4},{4,3},{5,6},{6,5},{7,8},{8,7},{9,10},{10,... | collective-permute-start | bytes 24584 | tf_op jit(solution)/shard_map/ppermute | solution.py:303
  112.6 2.2 %collective-permute-start.32 = (f32[2,8,128]{2,1,0:T(8,128)S(1)}, f32[2,8,128]{2,1,0:T(8,128)S(1)}, u32[]{:S(2)}, u32[]{:S(2)}) collective-permute-start(f32[2,8,128]{2,1,0:T(8,128)S(1)} %get-tuple-element.242), channel_id=1, source_target_pairs={{0,1},{1,0},{2,3},{3,2},{4,5},{5,4},{6,7},{7,6},{8,9},{9,8},{10,11... | collective-permute-start | bytes 24584 | tf_op jit(solution)/shard_map/ppermute | solution.py:303
  114.0 3.1 %collective-permute-start.33 = (f32[2,8,128]{2,1,0:T(8,128)S(1)}, f32[2,8,128]{2,1,0:T(8,128)S(1)}, u32[]{:S(2)}, u32[]{:S(2)}) collective-permute-start(f32[2,8,128]{2,1,0:T(8,128)S(1)} %get-tuple-element.243), channel_id=1, source_target_pairs={{0,15},{1,2},{2,1},{3,4},{4,3},{5,6},{6,5},{7,8},{8,7},{9,10},{10,... | collective-permute-start | bytes 24584 | tf_op jit(solution)/shard_map/ppermute | solution.py:303
  117.9 2.2 %collective-permute-start.34 = (f32[2,8,128]{2,1,0:T(8,128)S(1)}, f32[2,8,128]{2,1,0:T(8,128)S(1)}, u32[]{:S(2)}, u32[]{:S(2)}) collective-permute-start(f32[2,8,128]{2,1,0:T(8,128)S(1)} %get-tuple-element.245), channel_id=1, source_target_pairs={{0,1},{1,0},{2,3},{3,2},{4,5},{5,4},{6,7},{7,6},{8,9},{9,8},{10,11... | collective-permute-start | bytes 24584 | tf_op jit(solution)/shard_map/ppermute | solution.py:303
  119.3 3.1 %collective-permute-start.35 = (f32[2,8,128]{2,1,0:T(8,128)S(1)}, f32[2,8,128]{2,1,0:T(8,128)S(1)}, u32[]{:S(2)}, u32[]{:S(2)}) collective-permute-start(f32[2,8,128]{2,1,0:T(8,128)S(1)} %get-tuple-element.246), channel_id=1, source_target_pairs={{0,15},{1,2},{2,1},{3,4},{4,3},{5,6},{6,5},{7,8},{8,7},{9,10},{10,... | collective-permute-start | bytes 24584 | tf_op jit(solution)/shard_map/ppermute | solution.py:303
  123.5 15.5 %all-to-all-start.1 = ((bf16[16,8,2688]{2,1,0:T(8,128)(2,1)}), bf16[16,8,2688]{2,1,0:T(8,128)(2,1)S(1)}, u32[]{:S(2)}, u32[]{:S(2)}) async-start(bf16[16,8,2688]{2,1,0:T(8,128)(2,1)} %bitcast.14), calls=%async_computation.1 | async-start | bytes 1376256 | tf_op jit(solution)/shard_map/all_to_all | solution.py:386

commit v3 on v2

--- a/solution.py
+++ b/solution.py
@@ -76,7 +76,7 @@
     return own
 
 
-def forward_body(ints, floats, marg, by_check, by_var, signs, labels, fixed, th_out, u_out, gv_out, sendc, sendz, tb):
+def forward_body(ints, floats, marg, by_var, signs, th_out, u_out, tb):
     ints, floats = scalars(ints), Rows(floats)
     zmask = floats[2 * TILES + 1]
     for block in range(EXT):
@@ -85,7 +85,6 @@
             th = th * zmask
         th_out[block] = th
         tb[block] = th.astype(BF16)
-    gv_out[...] = jnp.zeros_like(gv_out)
     for row in range(NB):
         total = None
         for slot in range(TPC):
@@ -95,8 +94,27 @@
         sign = signs[:, row * BLK : (row + 1) * BLK]
         soft = jnp.tanh(total).reshape(SEC, SH, BLK) * sign[None]
         u_out[row] = soft.reshape(SEC * SH, BLK)
-    for row in range(NB):
-        parts = nn(u_out[row, (SEC - 1) * SH :, :].astype(BF16), by_check[row])
+
+
+def message_body(ints, floats, marg, by_check, by_var, signs, labels, fixed, gv_out, sendc, sendz, th, us):
+    ints, floats = scalars(ints), Rows(floats)
+    zmask = floats[2 * TILES + 1]
+    for block in range(EXT):
+        value = jnp.tanh(0.5 * marg[:, block * BLK : (block + 1) * BLK])
+        if block == NB + 1:
+            value = value * zmask
+        th[block] = value
+    gv_out[...] = jnp.zeros_like(gv_out)
+    for row in range(NB):
+        total = None
+        for slot in range(TPC):
+            tile = slot * NB + row
+            chosen = th[ints[tile]].astype(BF16)
+            part = nn(chosen, by_var[row, slot * BLK : (slot + 1) * BLK, :]) * floats[tile]
+            total = part if total is None else total + part
+        us[row] = jnp.tanh(total) * signs[:, row * BLK : (row + 1) * BLK]
+    for row in range(NB):
+        parts = nn(us[row].astype(BF16), by_check[row])
         for slot in range(TPC):
             tile = slot * NB + row
             gv_out[ints[tile]] += parts[:, slot * BLK : (slot + 1) * BLK] * floats[TILES + tile]
@@ -138,7 +156,7 @@
         prior, r = constants[0:1], constants[1:2]
         ret_out[0:1, lanes] = r
         message = received(gv, block, recvc, recvz, floats)
-        level = marg[(SEC - 1) * SH :, lanes]
+        level = marg[:, lanes]
         f = r * level + (1.0 - r) * (prior + message)
         g = y * jax.nn.sigmoid(f) - (1.0 - y) * jax.nn.sigmoid(-f)
         if block == NB + 1:
@@ -303,8 +321,6 @@
         return lax.ppermute(core, "tile", CORE_PAIRS), lax.ppermute(z, "tile", Z_PAIRS)
 
     levels = checkpoint[0]
-    my_labels = lax.dynamic_slice_in_dim(labels, group * SH, SH, 0).astype(F32)
-    my_signs = 1.0 - 2.0 * lax.dynamic_slice_in_dim(syndrome, group * SH, SH, 0).astype(F32)
     fixed = jnp.concatenate(
         [prior_llr[None], retention[None], jnp.zeros((SH - 2, LANES), F32)], axis=0
     )
@@ -327,10 +343,12 @@
     floats = jnp.broadcast_to(floats[:, None], (2 * TILES + 2, BLK))
     sent = jnp.concatenate([levels, halo_core, halo_z], axis=1).astype(jnp.float16)
     sent = sent.reshape(SEC, SH, EXT * BLK)
-    sent, pattern = lax.optimization_barrier((sent, pattern))
+    sent, pattern, labels, syndrome = lax.optimization_barrier((sent, pattern, labels, syndrome))
+    my_labels = lax.dynamic_slice_in_dim(labels, group * SH, SH, 0).astype(F32)
+    my_signs = 1.0 - 2.0 * lax.dynamic_slice_in_dim(syndrome, group * SH, SH, 0).astype(F32)
     patterns = prepare(pattern)
     marg = lax.all_to_all(sent, "section", 0, 0, tiled=True)
-    marg = marg.reshape(SEC * SH, EXT * BLK).astype(F32)
+    last_marg = marg[SEC - 1].astype(F32)
 
     def shape(*dims, dtype=F32):
         return jax.ShapeDtypeStruct(dims, dtype)
@@ -339,17 +357,26 @@
     wide_edge = shape(4, SH, BLK)
     field = shape(EXT, SH, BLK)
     rows = shape(NB, SH, BLK)
-    th, u, gv, core, z = call(
+    gv, core, z = call(
+        message_body,
+        [field, wide_edge, wide_edge],
+        [ints, floats, last_marg, *patterns, my_signs, my_labels, fixed],
+        scratch=[pltpu.VMEM((EXT, SH, BLK), F32), pltpu.VMEM((NB, SH, BLK), F32)],
+    )
+    core, z, marg = lax.optimization_barrier((core, z, marg))
+    th, u = call(
         forward_body,
-        [shape(EXT, SEC * SH, BLK), shape(NB, SEC * SH, BLK), field, wide_edge, wide_edge],
-        [ints, floats, marg, *patterns, my_signs, my_labels, fixed],
+        [shape(EXT, SEC * SH, BLK), shape(NB, SEC * SH, BLK)],
+        [ints, floats, marg.reshape(SEC * SH, EXT * BLK).astype(F32), patterns[1], my_signs],
         scratch=[pltpu.VMEM((EXT, SEC * SH, BLK), BF16)],
+        flops=2 * SEC * SH * TILES * BLK * BLK,
+        bytes_accessed=4 * 2**20,
     )
     core, z = exchange(core, z)
     g, q, dz, acc, ret_ext, core, z = call(
         first_body,
         [field, field, rows, field, shape(1, EXT * BLK), edge, edge],
-        [ints, floats, marg, gv, core, z, fixed, my_labels, u, my_signs, *patterns],
+        [ints, floats, last_marg, gv, core, z, fixed, my_labels, u, my_signs, *patterns],
     )
     leaving = {SEC - 1: g}
     saved = [(q, dz)]

time: 141 us -> 139 us (0.986)
  waiting for transfers between devices: 68.2 us -> 65.5 us
    pallas_call x23 -> x24, Pallas kernels: 18.5 us -> 19.2 us  [call(): pl.pallas_call(body, out_shape=outs, in_specs=[VSPEC] * len(args), out_sp...]
  transfers between devices with their start and end apart: 38 -> 38, of which waited for: 36 -> 35; matrix products, arithmetic and copies ran while one was open for 2% -> 3% of each run, Pallas kernels for 3% -> 3%
where the time goes in v3:
time: 139 us
  waiting for transfers between devices  65.5 us (47%)
  starting transfers between devices  42.4 us (31%)
  Pallas kernels  20.2 us (15%)
  other arithmetic  7.11 us (5%)
  local copies, waits for them, and re-layouts  2.14 us (2%)
  between operations  1.49 us (1%)
    ppermute x18, waiting for transfers between devices, exchange(): lax.ppermute(z, 'tile', Z_PAIRS)  37.2 us
    ppermute x18, starting transfers between devices, exchange(): lax.ppermute(core, 'tile', CORE_PAIRS)  28.9 us
    pallas_call x24, Pallas kernels, call(): pl.pallas_call(body, out_shape=outs, in_specs=[VSPEC] * len(args), out_sp...  19.2 us
    all_to_all x1, waiting for transfers between devices, on_device(): lax.all_to_all(packed.reshape(SEC, SH, LANES + GRAD_LANES), 'section', 0,...  11.9 us
    ppermute x18, waiting for transfers between devices, exchange(): lax.ppermute(core, 'tile', CORE_PAIRS)  10.3 us
    all_to_all x1, starting transfers between devices, on_device(): marg = lax.all_to_all(sent, 'section', 0, 0, tiled=True)  6.8 us
    all_to_all x1, waiting for transfers between devices, on_device(): marg = lax.all_to_all(sent, 'section', 0, 0, tiled=True)  6.16 us
    all_to_all x1, starting transfers between devices, on_device(): lax.all_to_all(packed.reshape(SEC, SH, LANES + GRAD_LANES), 'section', 0,...  3.6 us
  transfers between devices with their start and end apart: 38, of which 35 were waited for; matrix products, arithmetic and copies ran while one was open for 3% of the time, Pallas kernels for 3%

profile of v3, /device:TPU:1, one launch (start us, length us, event | category | flops | bytes accessed | tf_op | source)
XLA Modules:
  0.0 138.8 jit_solution(9523025550008775362)
XLA Ops:
  0.7 0.9 slice_select_fusion.1
  1.6 3.1 %collective-permute-start.1 = (f32[128,128]{1,0:T(8,128)S(1)}, f32[128,128]{1,0:T(8,128)S(1)}, u32[]{:S(2)}, u32[]{:S(2)}) collective-permute-start(f32[128,128]{1,0:T(8,128)S(1)} %get-tuple-element.275), channel_id=1, source_target_pairs={{0,15},{1,2},{2,1},{3,4},{4,3},{5,6},{6,5},{7,8},{8,7},{9,10},{10,... | collective-permute-start | bytes 196616 | tf_op jit(solution)/shard_map/ppermute | solution.py:321
  4.7 3.8 %collective-permute-start = (f32[128,128]{1,0:T(8,128)S(1)}, f32[128,128]{1,0:T(8,128)S(1)}, u32[]{:S(2)}, u32[]{:S(2)}) collective-permute-start(f32[128,128]{1,0:T(8,128)S(1)} %get-tuple-element.274), channel_id=1, source_target_pairs={{0,1},{1,0},{2,3},{3,2},{4,5},{5,4},{6,7},{7,6},{8,9},{9,8},{10,11... | collective-permute-start | bytes 196616 | tf_op jit(solution)/shard_map/ppermute | solution.py:321
  8.5 1.3 convert_bitcast_fusion
  10.8 1.0 pad_maximum_fusion
  11.8 6.8 %all-to-all-start = ((f16[16,8,2304]{2,1,0:T(8,128)(2,1)}), f16[16,8,2304]{2,1,0:T(8,128)(2,1)}, u32[]{:S(2)}, u32[]{:S(2)}) async-start(f16[16,8,2304]{2,1,0:T(8,128)(2,1)} %pad_maximum_fusion), calls=%async_computation | async-start | bytes 1179648 | tf_op jit(solution)/shard_map/all_to_all | solution.py:350
  18.6 0.9 dynamic-slice_convert_fusion.labels
  19.4 1.9 %copy-done = s32[48,128,128]{2,1,0:T(8,128)S(1)} copy-done((s32[48,128,128]{2,1,0:T(8,128)S(1)}, s32[48,128,128]{2,1,0:T(8,128)}, u32[]{:S(2)}) %copy-start) | copy-done | bytes 3145752
  21.3 1.0 shard_map.129
  22.3 0.9 maximum_maximum_fusion
  23.2 6.2 %all-to-all-done = f16[16,8,2304]{2,1,0:T(8,128)(2,1)} async-done(((f16[16,8,2304]{2,1,0:T(8,128)(2,1)}), f16[16,8,2304]{2,1,0:T(8,128)(2,1)}, u32[]{:S(2)}, u32[]{:S(2)}) %all-to-all-start) | async-done | bytes 589856 | tf_op jit(solution)/shard_map/all_to_all | solution.py:350
  30.3 0.9 shard_map.130
  31.2 2.5 %collective-permute-start.2 = (f32[4,8,128]{2,1,0:T(8,128)S(1)}, f32[4,8,128]{2,1,0:T(8,128)S(1)}, u32[]{:S(2)}, u32[]{:S(2)}) collective-permute-start(f32[4,8,128]{2,1,0:T(8,128)S(1)} %get-tuple-element.148), channel_id=1, source_target_pairs={{0,1},{1,0},{2,3},{3,2},{4,5},{5,4},{6,7},{7,6},{8,9},{9,8},{10,11... | collective-permute-start | bytes 49160 | tf_op jit(solution)/shard_map/ppermute | solution.py:321
  33.7 1.1 bitcast_convert_fusion.marg
  35.7 1.2 collective-permute-done.3.recvz
  36.9 0.8 shard_map.132
  37.7 1.5 %collective-permute-start.4 = (f32[2,8,128]{2,1,0:T(8,128)S(1)}, f32[2,8,128]{2,1,0:T(8,128)S(1)}, u32[]{:S(2)}, u32[]{:S(2)}) collective-permute-start(f32[2,8,128]{2,1,0:T(8,128)S(1)} %get-tuple-element.154), channel_id=1, source_target_pairs={{0,1},{1,0},{2,3},{3,2},{4,5},{5,4},{6,7},{7,6},{8,9},{9,8},{10,11... | collective-permute-start | bytes 24584 | tf_op jit(solution)/shard_map/ppermute | solution.py:321
  39.2 0.8 collective-permute-done.4.recvc
  40.0 2.2 %collective-permute-done.5.recvz = f32[2,8,128]{2,1,0:T(8,128)S(1)} collective-permute-done((f32[2,8,128]{2,1,0:T(8,128)S(1)}, f32[2,8,128]{2,1,0:T(8,128)S(1)}, u32[]{:S(2)}, u32[]{:S(2)}) %collective-permute-start.5) | collective-permute-done | bytes 8224 | tf_op jit(solution)/shard_map/ppermute | solution.py:321
  43.0 1.4 collective-permute-start.6
  44.4 0.8 collective-permute-done.6.recvc
  45.2 2.2 %collective-permute-done.7.recvz = f32[2,8,128]{2,1,0:T(8,128)S(1)} collective-permute-done((f32[2,8,128]{2,1,0:T(8,128)S(1)}, f32[2,8,128]{2,1,0:T(8,128)S(1)}, u32[]{:S(2)}, u32[]{:S(2)}) %collective-permute-start.7) | collective-permute-done | bytes 8224 | tf_op jit(solution)/shard_map/ppermute | solution.py:321
  48.3 1.4 collective-permute-start.8
  49.6 0.8 collective-permute-done.8.recvc
  50.5 2.2 %collective-permute-done.9.recvz = f32[2,8,128]{2,1,0:T(8,128)S(1)} collective-permute-done((f32[2,8,128]{2,1,0:T(8,128)S(1)}, f32[2,8,128]{2,1,0:T(8,128)S(1)}, u32[]{:S(2)}, u32[]{:S(2)}) %collective-permute-start.9) | collective-permute-done | bytes 8224 | tf_op jit(solution)/shard_map/ppermute | solution.py:321
  53.5 1.4 collective-permute-start.10
  55.7 2.2 %collective-permute-done.11.recvz = f32[2,8,128]{2,1,0:T(8,128)S(1)} collective-permute-done((f32[2,8,128]{2,1,0:T(8,128)S(1)}, f32[2,8,128]{2,1,0:T(8,128)S(1)}, u32[]{:S(2)}, u32[]{:S(2)}) %collective-permute-start.11) | collective-permute-done | bytes 8224 | tf_op jit(solution)/shard_map/ppermute | solution.py:321
  58.7 1.6 %collective-permute-start.12 = (f32[2,8,128]{2,1,0:T(8,128)S(1)}, f32[2,8,128]{2,1,0:T(8,128)S(1)}, u32[]{:S(2)}, u32[]{:S(2)}) collective-permute-start(f32[2,8,128]{2,1,0:T(8,128)S(1)} %get-tuple-element.184), channel_id=1, source_target_pairs={{0,1},{1,0},{2,3},{3,2},{4,5},{5,4},{6,7},{7,6},{8,9},{9,8},{10,11... | collective-permute-start | bytes 24584 | tf_op jit(solution)/shard_map/ppermute | solution.py:321
  60.3 0.8 collective-permute-done.12.recvc
  61.1 2.2 %collective-permute-done.13.recvz = f32[2,8,128]{2,1,0:T(8,128)S(1)} collective-permute-done((f32[2,8,128]{2,1,0:T(8,128)S(1)}, f32[2,8,128]{2,1,0:T(8,128)S(1)}, u32[]{:S(2)}, u32[]{:S(2)}) %collective-permute-start.13) | collective-permute-done | bytes 8224 | tf_op jit(solution)/shard_map/ppermute | solution.py:321
  64.1 1.4 collective-permute-start.14
  65.5 0.8 collective-permute-done.14.recvc
  66.3 2.2 %collective-permute-done.15.recvz = f32[2,8,128]{2,1,0:T(8,128)S(1)} collective-permute-done((f32[2,8,128]{2,1,0:T(8,128)S(1)}, f32[2,8,128]{2,1,0:T(8,128)S(1)}, u32[]{:S(2)}, u32[]{:S(2)}) %collective-permute-start.15) | collective-permute-done | bytes 8224 | tf_op jit(solution)/shard_map/ppermute | solution.py:321
  69.4 1.4 collective-permute-start.16
  70.7 0.8 collective-permute-done.16.recvc
  71.6 2.2 %collective-permute-done.17.recvz = f32[2,8,128]{2,1,0:T(8,128)S(1)} collective-permute-done((f32[2,8,128]{2,1,0:T(8,128)S(1)}, f32[2,8,128]{2,1,0:T(8,128)S(1)}, u32[]{:S(2)}, u32[]{:S(2)}) %collective-permute-start.17) | collective-permute-done | bytes 8224 | tf_op jit(solution)/shard_map/ppermute | solution.py:321
  74.6 1.4 collective-permute-start.18
  76.8 2.2 %collective-permute-done.19.recvz = f32[2,8,128]{2,1,0:T(8,128)S(1)} collective-permute-done((f32[2,8,128]{2,1,0:T(8,128)S(1)}, f32[2,8,128]{2,1,0:T(8,128)S(1)}, u32[]{:S(2)}, u32[]{:S(2)}) %collective-permute-start.19) | collective-permute-done | bytes 8224 | tf_op jit(solution)/shard_map/ppermute | solution.py:321
  79.8 1.4 collective-permute-start.20
  81.2 0.8 collective-permute-done.20.recvc
  82.0 2.2 %collective-permute-done.21.recvz = f32[2,8,128]{2,1,0:T(8,128)S(1)} collective-permute-done((f32[2,8,128]{2,1,0:T(8,128)S(1)}, f32[2,8,128]{2,1,0:T(8,128)S(1)}, u32[]{:S(2)}, u32[]{:S(2)}) %collective-permute-start.21) | collective-permute-done | bytes 8224 | tf_op jit(solution)/shard_map/ppermute | solution.py:321
  85.0 1.4 collective-permute-start.22
  86.4 0.8 collective-permute-done.22.recvc
  87.3 2.2 %collective-permute-done.23.recvz = f32[2,8,128]{2,1,0:T(8,128)S(1)} collective-permute-done((f32[2,8,128]{2,1,0:T(8,128)S(1)}, f32[2,8,128]{2,1,0:T(8,128)S(1)}, u32[]{:S(2)}, u32[]{:S(2)}) %collective-permute-start.23) | collective-permute-done | bytes 8224 | tf_op jit(solution)/shard_map/ppermute | solution.py:321
  90.3 1.6 %collective-permute-start.24 = (f32[2,8,128]{2,1,0:T(8,128)S(1)}, f32[2,8,128]{2,1,0:T(8,128)S(1)}, u32[]{:S(2)}, u32[]{:S(2)}) collective-permute-start(f32[2,8,128]{2,1,0:T(8,128)S(1)} %get-tuple-element.222), channel_id=1, source_target_pairs={{0,1},{1,0},{2,3},{3,2},{4,5},{5,4},{6,7},{7,6},{8,9},{9,8},{10,11... | collective-permute-start | bytes 24584 | tf_op jit(solution)/shard_map/ppermute | solution.py:321
  91.9 0.8 collective-permute-done.24.recvc
  92.7 2.2 %collective-permute-done.25.recvz = f32[2,8,128]{2,1,0:T(8,128)S(1)} collective-permute-done((f32[2,8,128]{2,1,0:T(8,128)S(1)}, f32[2,8,128]{2,1,0:T(8,128)S(1)}, u32[]{:S(2)}, u32[]{:S(2)}) %collective-permute-start.25) | collective-permute-done | bytes 8224 | tf_op jit(solution)/shard_map/ppermute | solution.py:321
  95.7 1.4 collective-permute-start.26
  97.9 2.2 %collective-permute-done.27.recvz = f32[2,8,128]{2,1,0:T(8,128)S(1)} collective-permute-done((f32[2,8,128]{2,1,0:T(8,128)S(1)}, f32[2,8,128]{2,1,0:T(8,128)S(1)}, u32[]{:S(2)}, u32[]{:S(2)}) %collective-permute-start.27) | collective-permute-done | bytes 8224 | tf_op jit(solution)/shard_map/ppermute | solution.py:321
  101.0 1.4 collective-permute-start.28
  102.3 0.8 collective-permute-done.28.recvc
  103.2 2.2 %collective-permute-done.29.recvz = f32[2,8,128]{2,1,0:T(8,128)S(1)} collective-permute-done((f32[2,8,128]{2,1,0:T(8,128)S(1)}, f32[2,8,128]{2,1,0:T(8,128)S(1)}, u32[]{:S(2)}, u32[]{:S(2)}) %collective-permute-start.29) | collective-permute-done | bytes 8224 | tf_op jit(solution)/shard_map/ppermute | solution.py:321
  106.2 1.4 collective-permute-start.30
  107.6 0.8 collective-permute-done.30.recvc
  108.4 2.2 %collective-permute-done.31.recvz = f32[2,8,128]{2,1,0:T(8,128)S(1)} collective-permute-done((f32[2,8,128]{2,1,0:T(8,128)S(1)}, f32[2,8,128]{2,1,0:T(8,128)S(1)}, u32[]{:S(2)}, u32[]{:S(2)}) %collective-permute-start.31) | collective-permute-done | bytes 8224 | tf_op jit(solution)/shard_map/ppermute | solution.py:321
  111.4 1.4 collective-permute-start.32
  112.8 0.8 collective-permute-done.32.recvc
  113.6 2.2 %collective-permute-done.33.recvz = f32[2,8,128]{2,1,0:T(8,128)S(1)} collective-permute-done((f32[2,8,128]{2,1,0:T(8,128)S(1)}, f32[2,8,128]{2,1,0:T(8,128)S(1)}, u32[]{:S(2)}, u32[]{:S(2)}) %collective-permute-start.33) | collective-permute-done | bytes 8224 | tf_op jit(solution)/shard_map/ppermute | solution.py:321
  116.6 1.4 collective-permute-start.34
  118.9 2.2 %collective-permute-done.35.recvz = f32[2,8,128]{2,1,0:T(8,128)S(1)} collective-permute-done((f32[2,8,128]{2,1,0:T(8,128)S(1)}, f32[2,8,128]{2,1,0:T(8,128)S(1)}, u32[]{:S(2)}, u32[]{:S(2)}) %collective-permute-start.35) | collective-permute-done | bytes 8224 | tf_op jit(solution)/shard_map/ppermute | solution.py:321
  121.1 1.1 shard_map.152
  122.2 3.6 %all-to-all-start.1 = ((bf16[16,8,2688]{2,1,0:T(8,128)(2,1)}), bf16[16,8,2688]{2,1,0:T(8,128)(2,1)S(1)}, u32[]{:S(2)}, u32[]{:S(2)}) async-start(bf16[16,8,2688]{2,1,0:T(8,128)(2,1)} %bitcast.15), calls=%async_computation.1 | async-start | bytes 1376256 | tf_op jit(solution)/shard_map/all_to_all | solution.py:413
  125.9 11.9 %all-to-all-done.1 = bf16[16,8,2688]{2,1,0:T(8,128)(2,1)S(1)} async-done(((bf16[16,8,2688]{2,1,0:T(8,128)(2,1)}), bf16[16,8,2688]{2,1,0:T(8,128)(2,1)S(1)}, u32[]{:S(2)}, u32[]{:S(2)}) %all-to-all-start.1) | async-done | bytes 688160 | tf_op jit(solution)/shard_map/all_to_all | solution.py:413
  137.8 1.1 shard_map.153
  (69 shorter events, 17.0 us)
Async XLA Ops:
  0.6 9.9 %copy-start.3 = (f32[48]{0:T(128)S(1)}, f32[48]{0:T(128)}, u32[]{:S(2)}) copy-start(f32[48]{0:T(128)} %param.19) | copy-start | bytes 580
  0.6 9.9 %copy-start.4 = (f32[48]{0:T(128)S(1)}, f32[48]{0:T(128)}, u32[]{:S(2)}) copy-start(f32[48]{0:T(128)} %param.18) | copy-start | bytes 580
  0.7 10.0 %copy-start.5 = (s32[48]{0:T(128)S(1)}, s32[48]{0:T(128)}, u32[]{:S(2)}) copy-start(s32[48]{0:T(128)} %param.15) | copy-start | bytes 580
  1.6 9.2 %collective-permute-start.1 = (f32[128,128]{1,0:T(8,128)S(1)}, f32[128,128]{1,0:T(8,128)S(1)}, u32[]{:S(2)}, u32[]{:S(2)}) collective-permute-start(f32[128,128]{1,0:T(8,128)S(1)} %get-tuple-element.275), channel_id=1, source_target_pairs={{0,15},{1,2},{2,1},{3,4},{4,3},{5,6},{6,5},{7,8},{8,7},{9,10},{10,... | collective-permute-start | bytes 196616 | tf_op jit(solution)/shard_map/ppermute | solution.py:321
  4.7 6.1 %collective-permute-start = (f32[128,128]{1,0:T(8,128)S(1)}, f32[128,128]{1,0:T(8,128)S(1)}, u32[]{:S(2)}, u32[]{:S(2)}) collective-permute-start(f32[128,128]{1,0:T(8,128)S(1)} %get-tuple-element.274), channel_id=1, source_target_pairs={{0,1},{1,0},{2,3},{3,2},{4,5},{5,4},{6,7},{7,6},{8,9},{9,8},{10,11... | collective-permute-start | bytes 196616 | tf_op jit(solution)/shard_map/ppermute | solution.py:321
  11.8 17.6 %all-to-all-start = ((f16[16,8,2304]{2,1,0:T(8,128)(2,1)}), f16[16,8,2304]{2,1,0:T(8,128)(2,1)}, u32[]{:S(2)}, u32[]{:S(2)}) async-start(f16[16,8,2304]{2,1,0:T(8,128)(2,1)} %pad_maximum_fusion), calls=%async_computation | async-start | bytes 1179648 | tf_op jit(solution)/shard_map/all_to_all | solution.py:350
  19.4 1.9 %copy-start = (s32[48,128,128]{2,1,0:T(8,128)S(1)}, s32[48,128,128]{2,1,0:T(8,128)}, u32[]{:S(2)}) copy-start(s32[48,128,128]{2,1,0:T(8,128)} %param.17) | copy-start | bytes 9437188
  21.3 1.0 copy-start.1
  21.3 1.0 copy-start.2
  31.2 4.4 %collective-permute-start.2 = (f32[4,8,128]{2,1,0:T(8,128)S(1)}, f32[4,8,128]{2,1,0:T(8,128)S(1)}, u32[]{:S(2)}, u32[]{:S(2)}) collective-permute-start(f32[4,8,128]{2,1,0:T(8,128)S(1)} %get-tuple-element.148), channel_id=1, source_target_pairs={{0,1},{1,0},{2,3},{3,2},{4,5},{5,4},{6,7},{7,6},{8,9},{9,8},{10,11... | collective-permute-start | bytes 49160 | tf_op jit(solution)/shard_map/ppermute | solution.py:321
  33.7 3.2 %collective-permute-start.3 = (f32[4,8,128]{2,1,0:T(8,128)S(1)}, f32[4,8,128]{2,1,0:T(8,128)S(1)}, u32[]{:S(2)}, u32[]{:S(2)}) collective-permute-start(f32[4,8,128]{2,1,0:T(8,128)S(1)} %get-tuple-element.149), channel_id=1, source_target_pairs={{0,15},{1,2},{2,1},{3,4},{4,3},{5,6},{6,5},{7,8},{8,7},{9,10},{10,... | collective-permute-start | bytes 49160 | tf_op jit(solution)/shard_map/ppermute | solution.py:321
  37.7 2.3 %collective-permute-start.4 = (f32[2,8,128]{2,1,0:T(8,128)S(1)}, f32[2,8,128]{2,1,0:T(8,128)S(1)}, u32[]{:S(2)}, u32[]{:S(2)}) collective-permute-start(f32[2,8,128]{2,1,0:T(8,128)S(1)} %get-tuple-element.154), channel_id=1, source_target_pairs={{0,1},{1,0},{2,3},{3,2},{4,5},{5,4},{6,7},{7,6},{8,9},{9,8},{10,11... | collective-permute-start | bytes 24584 | tf_op jit(solution)/shard_map/ppermute | solution.py:321
  39.2 3.1 %collective-permute-start.5 = (f32[2,8,128]{2,1,0:T(8,128)S(1)}, f32[2,8,128]{2,1,0:T(8,128)S(1)}, u32[]{:S(2)}, u32[]{:S(2)}) collective-permute-start(f32[2,8,128]{2,1,0:T(8,128)S(1)} %get-tuple-element.155), channel_id=1, source_target_pairs={{0,15},{1,2},{2,1},{3,4},{4,3},{5,6},{6,5},{7,8},{8,7},{9,10},{10,... | collective-permute-start | bytes 24584 | tf_op jit(solution)/shard_map/ppermute | solution.py:321
  43.0 2.2 %collective-permute-start.6 = (f32[2,8,128]{2,1,0:T(8,128)S(1)}, f32[2,8,128]{2,1,0:T(8,128)S(1)}, u32[]{:S(2)}, u32[]{:S(2)}) collective-permute-start(f32[2,8,128]{2,1,0:T(8,128)S(1)} %get-tuple-element.160), channel_id=1, source_target_pairs={{0,1},{1,0},{2,3},{3,2},{4,5},{5,4},{6,7},{7,6},{8,9},{9,8},{10,11... | collective-permute-start | bytes 24584 | tf_op jit(solution)/shard_map/ppermute | solution.py:321
  44.4 3.1 %collective-permute-start.7 = (f32[2,8,128]{2,1,0:T(8,128)S(1)}, f32[2,8,128]{2,1,0:T(8,128)S(1)}, u32[]{:S(2)}, u32[]{:S(2)}) collective-permute-start(f32[2,8,128]{2,1,0:T(8,128)S(1)} %get-tuple-element.161), channel_id=1, source_target_pairs={{0,15},{1,2},{2,1},{3,4},{4,3},{5,6},{6,5},{7,8},{8,7},{9,10},{10,... | collective-permute-start | bytes 24584 | tf_op jit(solution)/shard_map/ppermute | solution.py:321
  48.3 2.2 %collective-permute-start.8 = (f32[2,8,128]{2,1,0:T(8,128)S(1)}, f32[2,8,128]{2,1,0:T(8,128)S(1)}, u32[]{:S(2)}, u32[]{:S(2)}) collective-permute-start(f32[2,8,128]{2,1,0:T(8,128)S(1)} %get-tuple-element.164), channel_id=1, source_target_pairs={{0,1},{1,0},{2,3},{3,2},{4,5},{5,4},{6,7},{7,6},{8,9},{9,8},{10,11... | collective-permute-start | bytes 24584 | tf_op jit(solution)/shard_map/ppermute | solution.py:321
  49.6 3.1 %collective-permute-start.9 = (f32[2,8,128]{2,1,0:T(8,128)S(1)}, f32[2,8,128]{2,1,0:T(8,128)S(1)}, u32[]{:S(2)}, u32[]{:S(2)}) collective-permute-start(f32[2,8,128]{2,1,0:T(8,128)S(1)} %get-tuple-element.165), channel_id=1, source_target_pairs={{0,15},{1,2},{2,1},{3,4},{4,3},{5,6},{6,5},{7,8},{8,7},{9,10},{10,... | collective-permute-start | bytes 24584 | tf_op jit(solution)/shard_map/ppermute | solution.py:321
  53.5 2.2 %collective-permute-start.10 = (f32[2,8,128]{2,1,0:T(8,128)S(1)}, f32[2,8,128]{2,1,0:T(8,128)S(1)}, u32[]{:S(2)}, u32[]{:S(2)}) collective-permute-start(f32[2,8,128]{2,1,0:T(8,128)S(1)} %get-tuple-element.168), channel_id=1, source_target_pairs={{0,1},{1,0},{2,3},{3,2},{4,5},{5,4},{6,7},{7,6},{8,9},{9,8},{10,11... | collective-permute-start | bytes 24584 | tf_op jit(solution)/shard_map/ppermute | solution.py:321
  54.9 3.1 %collective-permute-start.11 = (f32[2,8,128]{2,1,0:T(8,128)S(1)}, f32[2,8,128]{2,1,0:T(8,128)S(1)}, u32[]{:S(2)}, u32[]{:S(2)}) collective-permute-start(f32[2,8,128]{2,1,0:T(8,128)S(1)} %get-tuple-element.169), channel_id=1, source_target_pairs={{0,15},{1,2},{2,1},{3,4},{4,3},{5,6},{6,5},{7,8},{8,7},{9,10},{10,... | collective-permute-start | bytes 24584 | tf_op jit(solution)/shard_map/ppermute | solution.py:321
  58.7 2.4 %collective-permute-start.12 = (f32[2,8,128]{2,1,0:T(8,128)S(1)}, f32[2,8,128]{2,1,0:T(8,128)S(1)}, u32[]{:S(2)}, u32[]{:S(2)}) collective-permute-start(f32[2,8,128]{2,1,0:T(8,128)S(1)} %get-tuple-element.184), channel_id=1, source_target_pairs={{0,1},{1,0},{2,3},{3,2},{4,5},{5,4},{6,7},{7,6},{8,9},{9,8},{10,11... | collective-permute-start | bytes 24584 | tf_op jit(solution)/shard_map/ppermute | solution.py:321
  60.3 3.1 %collective-permute-start.13 = (f32[2,8,128]{2,1,0:T(8,128)S(1)}, f32[2,8,128]{2,1,0:T(8,128)S(1)}, u32[]{:S(2)}, u32[]{:S(2)}) collective-permute-start(f32[2,8,128]{2,1,0:T(8,128)S(1)} %get-tuple-element.185), channel_id=1, source_target_pairs={{0,15},{1,2},{2,1},{3,4},{4,3},{5,6},{6,5},{7,8},{8,7},{9,10},{10,... | collective-permute-start | bytes 24584 | tf_op jit(solution)/shard_map/ppermute | solution.py:321
  64.1 2.2 %collective-permute-start.14 = (f32[2,8,128]{2,1,0:T(8,128)S(1)}, f32[2,8,128]{2,1,0:T(8,128)S(1)}, u32[]{:S(2)}, u32[]{:S(2)}) collective-permute-start(f32[2,8,128]{2,1,0:T(8,128)S(1)} %get-tuple-element.188), channel_id=1, source_target_pairs={{0,1},{1,0},{2,3},{3,2},{4,5},{5,4},{6,7},{7,6},{8,9},{9,8},{10,11... | collective-permute-start | bytes 24584 | tf_op jit(solution)/shard_map/ppermute | solution.py:321
  65.5 3.1 %collective-permute-start.15 = (f32[2,8,128]{2,1,0:T(8,128)S(1)}, f32[2,8,128]{2,1,0:T(8,128)S(1)}, u32[]{:S(2)}, u32[]{:S(2)}) collective-permute-start(f32[2,8,128]{2,1,0:T(8,128)S(1)} %get-tuple-element.189), channel_id=1, source_target_pairs={{0,15},{1,2},{2,1},{3,4},{4,3},{5,6},{6,5},{7,8},{8,7},{9,10},{10,... | collective-permute-start | bytes 24584 | tf_op jit(solution)/shard_map/ppermute | solution.py:321
  69.4 2.2 %collective-permute-start.16 = (f32[2,8,128]{2,1,0:T(8,128)S(1)}, f32[2,8,128]{2,1,0:T(8,128)S(1)}, u32[]{:S(2)}, u32[]{:S(2)}) collective-permute-start(f32[2,8,128]{2,1,0:T(8,128)S(1)} %get-tuple-element.192), channel_id=1, source_target_pairs={{0,1},{1,0},{2,3},{3,2},{4,5},{5,4},{6,7},{7,6},{8,9},{9,8},{10,11... | collective-permute-start | bytes 24584 | tf_op jit(solution)/shard_map/ppermute | solution.py:321
  70.7 3.1 %collective-permute-start.17 = (f32[2,8,128]{2,1,0:T(8,128)S(1)}, f32[2,8,128]{2,1,0:T(8,128)S(1)}, u32[]{:S(2)}, u32[]{:S(2)}) collective-permute-start(f32[2,8,128]{2,1,0:T(8,128)S(1)} %get-tuple-element.193), channel_id=1, source_target_pairs={{0,15},{1,2},{2,1},{3,4},{4,3},{5,6},{6,5},{7,8},{8,7},{9,10},{10,... | collective-permute-start | bytes 24584 | tf_op jit(solution)/shard_map/ppermute | solution.py:321
  74.6 2.2 %collective-permute-start.18 = (f32[2,8,128]{2,1,0:T(8,128)S(1)}, f32[2,8,128]{2,1,0:T(8,128)S(1)}, u32[]{:S(2)}, u32[]{:S(2)}) collective-permute-start(f32[2,8,128]{2,1,0:T(8,128)S(1)} %get-tuple-element.196), channel_id=1, source_target_pairs={{0,1},{1,0},{2,3},{3,2},{4,5},{5,4},{6,7},{7,6},{8,9},{9,8},{10,11... | collective-permute-start | bytes 24584 | tf_op jit(solution)/shard_map/ppermute | solution.py:321
  76.0 3.1 %collective-permute-start.19 = (f32[2,8,128]{2,1,0:T(8,128)S(1)}, f32[2,8,128]{2,1,0:T(8,128)S(1)}, u32[]{:S(2)}, u32[]{:S(2)}) collective-permute-start(f32[2,8,128]{2,1,0:T(8,128)S(1)} %get-tuple-element.197), channel_id=1, source_target_pairs={{0,15},{1,2},{2,1},{3,4},{4,3},{5,6},{6,5},{7,8},{8,7},{9,10},{10,... | collective-permute-start | bytes 24584 | tf_op jit(solution)/shard_map/ppermute | solution.py:321
  79.8 2.2 %collective-permute-start.20 = (f32[2,8,128]{2,1,0:T(8,128)S(1)}, f32[2,8,128]{2,1,0:T(8,128)S(1)}, u32[]{:S(2)}, u32[]{:S(2)}) collective-permute-start(f32[2,8,128]{2,1,0:T(8,128)S(1)} %get-tuple-element.214), channel_id=1, source_target_pairs={{0,1},{1,0},{2,3},{3,2},{4,5},{5,4},{6,7},{7,6},{8,9},{9,8},{10,11... | collective-permute-start | bytes 24584 | tf_op jit(solution)/shard_map/ppermute | solution.py:321
  81.2 3.1 %collective-permute-start.21 = (f32[2,8,128]{2,1,0:T(8,128)S(1)}, f32[2,8,128]{2,1,0:T(8,128)S(1)}, u32[]{:S(2)}, u32[]{:S(2)}) collective-permute-start(f32[2,8,128]{2,1,0:T(8,128)S(1)} %get-tuple-element.215), channel_id=1, source_target_pairs={{0,15},{1,2},{2,1},{3,4},{4,3},{5,6},{6,5},{7,8},{8,7},{9,10},{10,... | collective-permute-start | bytes 24584 | tf_op jit(solution)/shard_map/ppermute | solution.py:321
  85.0 2.2 %collective-permute-start.22 = (f32[2,8,128]{2,1,0:T(8,128)S(1)}, f32[2,8,128]{2,1,0:T(8,128)S(1)}, u32[]{:S(2)}, u32[]{:S(2)}) collective-permute-start(f32[2,8,128]{2,1,0:T(8,128)S(1)} %get-tuple-element.218), channel_id=1, source_target_pairs={{0,1},{1,0},{2,3},{3,2},{4,5},{5,4},{6,7},{7,6},{8,9},{9,8},{10,11... | collective-permute-start | bytes 24584 | tf_op jit(solution)/shard_map/ppermute | solution.py:321
  86.4 3.1 %collective-permute-start.23 = (f32[2,8,128]{2,1,0:T(8,128)S(1)}, f32[2,8,128]{2,1,0:T(8,128)S(1)}, u32[]{:S(2)}, u32[]{:S(2)}) collective-permute-start(f32[2,8,128]{2,1,0:T(8,128)S(1)} %get-tuple-element.219), channel_id=1, source_target_pairs={{0,15},{1,2},{2,1},{3,4},{4,3},{5,6},{6,5},{7,8},{8,7},{9,10},{10,... | collective-permute-start | bytes 24584 | tf_op jit(solution)/shard_map/ppermute | solution.py:321
  90.3 2.4 %collective-permute-start.24 = (f32[2,8,128]{2,1,0:T(8,128)S(1)}, f32[2,8,128]{2,1,0:T(8,128)S(1)}, u32[]{:S(2)}, u32[]{:S(2)}) collective-permute-start(f32[2,8,128]{2,1,0:T(8,128)S(1)} %get-tuple-element.222), channel_id=1, source_target_pairs={{0,1},{1,0},{2,3},{3,2},{4,5},{5,4},{6,7},{7,6},{8,9},{9,8},{10,11... | collective-permute-start | bytes 24584 | tf_op jit(solution)/shard_map/ppermute | solution.py:321
  91.9 3.1 %collective-permute-start.25 = (f32[2,8,128]{2,1,0:T(8,128)S(1)}, f32[2,8,128]{2,1,0:T(8,128)S(1)}, u32[]{:S(2)}, u32[]{:S(2)}) collective-permute-start(f32[2,8,128]{2,1,0:T(8,128)S(1)} %get-tuple-element.223), channel_id=1, source_target_pairs={{0,15},{1,2},{2,1},{3,4},{4,3},{5,6},{6,5},{7,8},{8,7},{9,10},{10,... | collective-permute-start | bytes 24584 | tf_op jit(solution)/shard_map/ppermute | solution.py:321
  95.7 2.2 %collective-permute-start.26 = (f32[2,8,128]{2,1,0:T(8,128)S(1)}, f32[2,8,128]{2,1,0:T(8,128)S(1)}, u32[]{:S(2)}, u32[]{:S(2)}) collective-permute-start(f32[2,8,128]{2,1,0:T(8,128)S(1)} %get-tuple-element.226), channel_id=1, source_target_pairs={{0,1},{1,0},{2,3},{3,2},{4,5},{5,4},{6,7},{7,6},{8,9},{9,8},{10,11... | collective-permute-start | bytes 24584 | tf_op jit(solution)/shard_map/ppermute | solution.py:321
  97.1 3.1 %collective-permute-start.27 = (f32[2,8,128]{2,1,0:T(8,128)S(1)}, f32[2,8,128]{2,1,0:T(8,128)S(1)}, u32[]{:S(2)}, u32[]{:S(2)}) collective-permute-start(f32[2,8,128]{2,1,0:T(8,128)S(1)} %get-tuple-element.227), channel_id=1, source_target_pairs={{0,15},{1,2},{2,1},{3,4},{4,3},{5,6},{6,5},{7,8},{8,7},{9,10},{10,... | collective-permute-start | bytes 24584 | tf_op jit(solution)/shard_map/ppermute | solution.py:321
  101.0 2.2 %collective-permute-start.28 = (f32[2,8,128]{2,1,0:T(8,128)S(1)}, f32[2,8,128]{2,1,0:T(8,128)S(1)}, u32[]{:S(2)}, u32[]{:S(2)}) collective-permute-start(f32[2,8,128]{2,1,0:T(8,128)S(1)} %get-tuple-element.244), channel_id=1, source_target_pairs={{0,1},{1,0},{2,3},{3,2},{4,5},{5,4},{6,7},{7,6},{8,9},{9,8},{10,11... | collective-permute-start | bytes 24584 | tf_op jit(solution)/shard_map/ppermute | solution.py:321
  102.3 3.1 %collective-permute-start.29 = (f32[2,8,128]{2,1,0:T(8,128)S(1)}, f32[2,8,128]{2,1,0:T(8,128)S(1)}, u32[]{:S(2)}, u32[]{:S(2)}) collective-permute-start(f32[2,8,128]{2,1,0:T(8,128)S(1)} %get-tuple-element.245), channel_id=1, source_target_pairs={{0,15},{1,2},{2,1},{3,4},{4,3},{5,6},{6,5},{7,8},{8,7},{9,10},{10,... | collective-permute-start | bytes 24584 | tf_op jit(solution)/shard_map/ppermute | solution.py:321
  106.2 2.2 %collective-permute-start.30 = (f32[2,8,128]{2,1,0:T(8,128)S(1)}, f32[2,8,128]{2,1,0:T(8,128)S(1)}, u32[]{:S(2)}, u32[]{:S(2)}) collective-permute-start(f32[2,8,128]{2,1,0:T(8,128)S(1)} %get-tuple-element.248), channel_id=1, source_target_pairs={{0,1},{1,0},{2,3},{3,2},{4,5},{5,4},{6,7},{7,6},{8,9},{9,8},{10,11... | collective-permute-start | bytes 24584 | tf_op jit(solution)/shard_map/ppermute | solution.py:321
  107.6 3.1 %collective-permute-start.31 = (f32[2,8,128]{2,1,0:T(8,128)S(1)}, f32[2,8,128]{2,1,0:T(8,128)S(1)}, u32[]{:S(2)}, u32[]{:S(2)}) collective-permute-start(f32[2,8,128]{2,1,0:T(8,128)S(1)} %get-tuple-element.249), channel_id=1, source_target_pairs={{0,15},{1,2},{2,1},{3,4},{4,3},{5,6},{6,5},{7,8},{8,7},{9,10},{10,... | collective-permute-start | bytes 24584 | tf_op jit(solution)/shard_map/ppermute | solution.py:321
  111.4 2.2 %collective-permute-start.32 = (f32[2,8,128]{2,1,0:T(8,128)S(1)}, f32[2,8,128]{2,1,0:T(8,128)S(1)}, u32[]{:S(2)}, u32[]{:S(2)}) collective-permute-start(f32[2,8,128]{2,1,0:T(8,128)S(1)} %get-tuple-element.252), channel_id=1, source_target_pairs={{0,1},{1,0},{2,3},{3,2},{4,5},{5,4},{6,7},{7,6},{8,9},{9,8},{10,11... | collective-permute-start | bytes 24584 | tf_op jit(solution)/shard_map/ppermute | solution.py:321
  112.8 3.1 %collective-permute-start.33 = (f32[2,8,128]{2,1,0:T(8,128)S(1)}, f32[2,8,128]{2,1,0:T(8,128)S(1)}, u32[]{:S(2)}, u32[]{:S(2)}) collective-permute-start(f32[2,8,128]{2,1,0:T(8,128)S(1)} %get-tuple-element.253), channel_id=1, source_target_pairs={{0,15},{1,2},{2,1},{3,4},{4,3},{5,6},{6,5},{7,8},{8,7},{9,10},{10,... | collective-permute-start | bytes 24584 | tf_op jit(solution)/shard_map/ppermute | solution.py:321
  116.6 2.2 %collective-permute-start.34 = (f32[2,8,128]{2,1,0:T(8,128)S(1)}, f32[2,8,128]{2,1,0:T(8,128)S(1)}, u32[]{:S(2)}, u32[]{:S(2)}) collective-permute-start(f32[2,8,128]{2,1,0:T(8,128)S(1)} %get-tuple-element.255), channel_id=1, source_target_pairs={{0,1},{1,0},{2,3},{3,2},{4,5},{5,4},{6,7},{7,6},{8,9},{9,8},{10,11... | collective-permute-start | bytes 24584 | tf_op jit(solution)/shard_map/ppermute | solution.py:321
  118.0 3.1 %collective-permute-start.35 = (f32[2,8,128]{2,1,0:T(8,128)S(1)}, f32[2,8,128]{2,1,0:T(8,128)S(1)}, u32[]{:S(2)}, u32[]{:S(2)}) collective-permute-start(f32[2,8,128]{2,1,0:T(8,128)S(1)} %get-tuple-element.256), channel_id=1, source_target_pairs={{0,15},{1,2},{2,1},{3,4},{4,3},{5,6},{6,5},{7,8},{8,7},{9,10},{10,... | collective-permute-start | bytes 24584 | tf_op jit(solution)/shard_map/ppermute | solution.py:321
  122.2 15.5 %all-to-all-start.1 = ((bf16[16,8,2688]{2,1,0:T(8,128)(2,1)}), bf16[16,8,2688]{2,1,0:T(8,128)(2,1)S(1)}, u32[]{:S(2)}, u32[]{:S(2)}) async-start(bf16[16,8,2688]{2,1,0:T(8,128)(2,1)} %bitcast.15), calls=%async_computation.1 | async-start | bytes 1376256 | tf_op jit(solution)/shard_map/all_to_all | solution.py:413

commit v4 on v3

--- a/solution.py
+++ b/solution.py
@@ -320,7 +320,7 @@
     def exchange(core, z):
         return lax.ppermute(core, "tile", CORE_PAIRS), lax.ppermute(z, "tile", Z_PAIRS)
 
-    levels = checkpoint[0]
+    levels = lax.optimization_barrier(checkpoint[0].astype(jnp.float16))
     fixed = jnp.concatenate(
         [prior_llr[None], retention[None], jnp.zeros((SH - 2, LANES), F32)], axis=0
     )
@@ -341,7 +341,7 @@
         [gate_weight * live, msg_weight * live, jnp.stack([even, has_z]).astype(F32)]
     )
     floats = jnp.broadcast_to(floats[:, None], (2 * TILES + 2, BLK))
-    sent = jnp.concatenate([levels, halo_core, halo_z], axis=1).astype(jnp.float16)
+    sent = jnp.concatenate([levels, halo_core, halo_z], axis=1)
     sent = sent.reshape(SEC, SH, EXT * BLK)
     sent, pattern, labels, syndrome = lax.optimization_barrier((sent, pattern, labels, syndrome))
     my_labels = lax.dynamic_slice_in_dim(labels, group * SH, SH, 0).astype(F32)

time: 139 us -> 140 us (level)
    concatenate x4 -> x0, other arithmetic: 2.29 us -> none  [on_device(): jnp.concatenate([levels, halo_core, halo_z], axis=1).astype(jnp.float16)]
  transfers between devices with their start and end apart: 38 -> 38, of which waited for: 35 -> 35; matrix products, arithmetic and copies ran while one was open for 3% -> 2% of each run, Pallas kernels for 3% -> 3%
where the time goes in v4:
time: 140 us; the launch traced here: 139 us
  waiting for transfers between devices  65.7 us (47%)
  starting transfers between devices  43.6 us (31%)
  Pallas kernels  20 us (14%)
  other arithmetic  6.24 us (4%)
  local copies, waits for them, and re-layouts  2.14 us (2%)
  between operations  1.47 us (1%)
    ppermute x18, waiting for transfers between devices, exchange(): lax.ppermute(z, 'tile', Z_PAIRS)  37.2 us
    ppermute x18, starting transfers between devices, exchange(): lax.ppermute(core, 'tile', CORE_PAIRS)  30 us
    pallas_call x24, Pallas kernels, call(): pl.pallas_call(body, out_shape=outs, in_specs=[VSPEC] * len(args), out_sp...  19 us
    all_to_all x1, waiting for transfers between devices, on_device(): lax.all_to_all(packed.reshape(SEC, SH, LANES + GRAD_LANES), 'section', 0,...  11.9 us
    ppermute x18, waiting for transfers between devices, exchange(): lax.ppermute(core, 'tile', CORE_PAIRS)  10.3 us
    all_to_all x1, starting transfers between devices, on_device(): marg = lax.all_to_all(sent, 'section', 0, 0, tiled=True)  6.8 us
    all_to_all x1, waiting for transfers between devices, on_device(): marg = lax.all_to_all(sent, 'section', 0, 0, tiled=True)  6.38 us
    all_to_all x1, starting transfers between devices, on_device(): lax.all_to_all(packed.reshape(SEC, SH, LANES + GRAD_LANES), 'section', 0,...  3.6 us
  transfers between devices with their start and end apart: 38, of which 35 were waited for; matrix products, arithmetic and copies ran while one was open for 2% of the time, Pallas kernels for 3%

profile of v4, /device:TPU:1, one launch (start us, length us, event | category | flops | bytes accessed | tf_op | source)
XLA Modules:
  0.0 139.1 jit_solution(9234217043247290977)
XLA Ops:
  0.7 1.3 convert_bitcast_fusion
  2.0 3.1 %collective-permute-start.1 = (f16[128,128]{1,0:T(8,128)(2,1)S(1)}, f16[128,128]{1,0:T(8,128)(2,1)S(1)}, u32[]{:S(2)}, u32[]{:S(2)}) collective-permute-start(f16[128,128]{1,0:T(8,128)(2,1)S(1)} %get-tuple-element.275), channel_id=1, source_target_pairs={{0,15},{1,2},{2,1},{3,4},{4,3},{5,6},{6,5},{7,8},{8,7},{9,10},{10,... | collective-permute-start | bytes 98312 | tf_op jit(solution)/shard_map/ppermute | solution.py:321
  5.1 3.8 %collective-permute-start = (f16[128,128]{1,0:T(8,128)(2,1)S(1)}, f16[128,128]{1,0:T(8,128)(2,1)S(1)}, u32[]{:S(2)}, u32[]{:S(2)}) collective-permute-start(f16[128,128]{1,0:T(8,128)(2,1)S(1)} %get-tuple-element.274), channel_id=1, source_target_pairs={{0,1},{1,0},{2,3},{3,2},{4,5},{5,4},{6,7},{7,6},{8,9},{9,8},{10,11... | collective-permute-start | bytes 98312 | tf_op jit(solution)/shard_map/ppermute | solution.py:321
  9.9 1.0 maximum_bitcast_fusion
  10.9 6.8 %all-to-all-start = ((f16[16,8,2304]{2,1,0:T(8,128)(2,1)}), f16[16,8,2304]{2,1,0:T(8,128)(2,1)}, u32[]{:S(2)}, u32[]{:S(2)}) async-start(f16[16,8,2304]{2,1,0:T(8,128)(2,1)} %maximum_bitcast_fusion), calls=%async_computation | async-start | bytes 1179648 | tf_op jit(solution)/shard_map/all_to_all | solution.py:350
  17.7 0.9 dynamic-slice_convert_fusion.labels
  18.5 1.9 %copy-done = s32[48,128,128]{2,1,0:T(8,128)S(1)} copy-done((s32[48,128,128]{2,1,0:T(8,128)S(1)}, s32[48,128,128]{2,1,0:T(8,128)}, u32[]{:S(2)}) %copy-start) | copy-done | bytes 3145752
  20.4 1.0 shard_map.129
  21.4 0.9 maximum_maximum_fusion
  22.3 6.4 %all-to-all-done = f16[16,8,2304]{2,1,0:T(8,128)(2,1)} async-done(((f16[16,8,2304]{2,1,0:T(8,128)(2,1)}), f16[16,8,2304]{2,1,0:T(8,128)(2,1)}, u32[]{:S(2)}, u32[]{:S(2)}) %all-to-all-start) | async-done | bytes 589856 | tf_op jit(solution)/shard_map/all_to_all | solution.py:350
  29.6 0.9 shard_map.130
  30.5 2.3 %collective-permute-start.2 = (f32[4,8,128]{2,1,0:T(8,128)S(1)}, f32[4,8,128]{2,1,0:T(8,128)S(1)}, u32[]{:S(2)}, u32[]{:S(2)}) collective-permute-start(f32[4,8,128]{2,1,0:T(8,128)S(1)} %get-tuple-element.148), channel_id=1, source_target_pairs={{0,1},{1,0},{2,3},{3,2},{4,5},{5,4},{6,7},{7,6},{8,9},{9,8},{10,11... | collective-permute-start | bytes 49160 | tf_op jit(solution)/shard_map/ppermute | solution.py:321
  32.8 1.1 bitcast_convert_fusion.marg
  33.9 0.8 shard_map.131
  34.7 1.2 collective-permute-done.3.recvz
  35.9 0.8 shard_map.132
  36.7 2.5 %collective-permute-start.4 = (f32[2,8,128]{2,1,0:T(8,128)S(1)}, f32[2,8,128]{2,1,0:T(8,128)S(1)}, u32[]{:S(2)}, u32[]{:S(2)}) collective-permute-start(f32[2,8,128]{2,1,0:T(8,128)S(1)} %get-tuple-element.154), channel_id=1, source_target_pairs={{0,1},{1,0},{2,3},{3,2},{4,5},{5,4},{6,7},{7,6},{8,9},{9,8},{10,11... | collective-permute-start | bytes 24584 | tf_op jit(solution)/shard_map/ppermute | solution.py:321
  39.3 0.8 collective-permute-done.4.recvc
  40.1 2.2 %collective-permute-done.5.recvz = f32[2,8,128]{2,1,0:T(8,128)S(1)} collective-permute-done((f32[2,8,128]{2,1,0:T(8,128)S(1)}, f32[2,8,128]{2,1,0:T(8,128)S(1)}, u32[]{:S(2)}, u32[]{:S(2)}) %collective-permute-start.5) | collective-permute-done | bytes 8224 | tf_op jit(solution)/shard_map/ppermute | solution.py:321
  43.1 1.4 %collective-permute-start.6 = (f32[2,8,128]{2,1,0:T(8,128)S(1)}, f32[2,8,128]{2,1,0:T(8,128)S(1)}, u32[]{:S(2)}, u32[]{:S(2)}) collective-permute-start(f32[2,8,128]{2,1,0:T(8,128)S(1)} %get-tuple-element.160), channel_id=1, source_target_pairs={{0,1},{1,0},{2,3},{3,2},{4,5},{5,4},{6,7},{7,6},{8,9},{9,8},{10,11... | collective-permute-start | bytes 24584 | tf_op jit(solution)/shard_map/ppermute | solution.py:321
  44.5 0.8 collective-permute-done.6.recvc
  45.3 2.2 %collective-permute-done.7.recvz = f32[2,8,128]{2,1,0:T(8,128)S(1)} collective-permute-done((f32[2,8,128]{2,1,0:T(8,128)S(1)}, f32[2,8,128]{2,1,0:T(8,128)S(1)}, u32[]{:S(2)}, u32[]{:S(2)}) %collective-permute-start.7) | collective-permute-done | bytes 8224 | tf_op jit(solution)/shard_map/ppermute | solution.py:321
  48.3 1.4 %collective-permute-start.8 = (f32[2,8,128]{2,1,0:T(8,128)S(1)}, f32[2,8,128]{2,1,0:T(8,128)S(1)}, u32[]{:S(2)}, u32[]{:S(2)}) collective-permute-start(f32[2,8,128]{2,1,0:T(8,128)S(1)} %get-tuple-element.164), channel_id=1, source_target_pairs={{0,1},{1,0},{2,3},{3,2},{4,5},{5,4},{6,7},{7,6},{8,9},{9,8},{10,11... | collective-permute-start | bytes 24584 | tf_op jit(solution)/shard_map/ppermute | solution.py:321
  49.7 0.8 collective-permute-done.8.recvc
  50.6 2.2 %collective-permute-done.9.recvz = f32[2,8,128]{2,1,0:T(8,128)S(1)} collective-permute-done((f32[2,8,128]{2,1,0:T(8,128)S(1)}, f32[2,8,128]{2,1,0:T(8,128)S(1)}, u32[]{:S(2)}, u32[]{:S(2)}) %collective-permute-start.9) | collective-permute-done | bytes 8224 | tf_op jit(solution)/shard_map/ppermute | solution.py:321
  53.6 1.4 %collective-permute-start.10 = (f32[2,8,128]{2,1,0:T(8,128)S(1)}, f32[2,8,128]{2,1,0:T(8,128)S(1)}, u32[]{:S(2)}, u32[]{:S(2)}) collective-permute-start(f32[2,8,128]{2,1,0:T(8,128)S(1)} %get-tuple-element.168), channel_id=1, source_target_pairs={{0,1},{1,0},{2,3},{3,2},{4,5},{5,4},{6,7},{7,6},{8,9},{9,8},{10,11... | collective-permute-start | bytes 24584 | tf_op jit(solution)/shard_map/ppermute | solution.py:321
  55.8 2.2 %collective-permute-done.11.recvz = f32[2,8,128]{2,1,0:T(8,128)S(1)} collective-permute-done((f32[2,8,128]{2,1,0:T(8,128)S(1)}, f32[2,8,128]{2,1,0:T(8,128)S(1)}, u32[]{:S(2)}, u32[]{:S(2)}) %collective-permute-start.11) | collective-permute-done | bytes 8224 | tf_op jit(solution)/shard_map/ppermute | solution.py:321
  58.8 1.6 %collective-permute-start.12 = (f32[2,8,128]{2,1,0:T(8,128)S(1)}, f32[2,8,128]{2,1,0:T(8,128)S(1)}, u32[]{:S(2)}, u32[]{:S(2)}) collective-permute-start(f32[2,8,128]{2,1,0:T(8,128)S(1)} %get-tuple-element.184), channel_id=1, source_target_pairs={{0,1},{1,0},{2,3},{3,2},{4,5},{5,4},{6,7},{7,6},{8,9},{9,8},{10,11... | collective-permute-start | bytes 24584 | tf_op jit(solution)/shard_map/ppermute | solution.py:321
  60.4 0.8 collective-permute-done.12.recvc
  61.2 2.2 %collective-permute-done.13.recvz = f32[2,8,128]{2,1,0:T(8,128)S(1)} collective-permute-done((f32[2,8,128]{2,1,0:T(8,128)S(1)}, f32[2,8,128]{2,1,0:T(8,128)S(1)}, u32[]{:S(2)}, u32[]{:S(2)}) %collective-permute-start.13) | collective-permute-done | bytes 8224 | tf_op jit(solution)/shard_map/ppermute | solution.py:321
  64.2 1.4 %collective-permute-start.14 = (f32[2,8,128]{2,1,0:T(8,128)S(1)}, f32[2,8,128]{2,1,0:T(8,128)S(1)}, u32[]{:S(2)}, u32[]{:S(2)}) collective-permute-start(f32[2,8,128]{2,1,0:T(8,128)S(1)} %get-tuple-element.188), channel_id=1, source_target_pairs={{0,1},{1,0},{2,3},{3,2},{4,5},{5,4},{6,7},{7,6},{8,9},{9,8},{10,11... | collective-permute-start | bytes 24584 | tf_op jit(solution)/shard_map/ppermute | solution.py:321
  65.6 0.8 collective-permute-done.14.recvc
  66.5 2.2 %collective-permute-done.15.recvz = f32[2,8,128]{2,1,0:T(8,128)S(1)} collective-permute-done((f32[2,8,128]{2,1,0:T(8,128)S(1)}, f32[2,8,128]{2,1,0:T(8,128)S(1)}, u32[]{:S(2)}, u32[]{:S(2)}) %collective-permute-start.15) | collective-permute-done | bytes 8224 | tf_op jit(solution)/shard_map/ppermute | solution.py:321
  69.5 1.4 %collective-permute-start.16 = (f32[2,8,128]{2,1,0:T(8,128)S(1)}, f32[2,8,128]{2,1,0:T(8,128)S(1)}, u32[]{:S(2)}, u32[]{:S(2)}) collective-permute-start(f32[2,8,128]{2,1,0:T(8,128)S(1)} %get-tuple-element.192), channel_id=1, source_target_pairs={{0,1},{1,0},{2,3},{3,2},{4,5},{5,4},{6,7},{7,6},{8,9},{9,8},{10,11... | collective-permute-start | bytes 24584 | tf_op jit(solution)/shard_map/ppermute | solution.py:321
  70.9 0.8 collective-permute-done.16.recvc
  71.7 2.2 %collective-permute-done.17.recvz = f32[2,8,128]{2,1,0:T(8,128)S(1)} collective-permute-done((f32[2,8,128]{2,1,0:T(8,128)S(1)}, f32[2,8,128]{2,1,0:T(8,128)S(1)}, u32[]{:S(2)}, u32[]{:S(2)}) %collective-permute-start.17) | collective-permute-done | bytes 8224 | tf_op jit(solution)/shard_map/ppermute | solution.py:321
  74.7 1.4 %collective-permute-start.18 = (f32[2,8,128]{2,1,0:T(8,128)S(1)}, f32[2,8,128]{2,1,0:T(8,128)S(1)}, u32[]{:S(2)}, u32[]{:S(2)}) collective-permute-start(f32[2,8,128]{2,1,0:T(8,128)S(1)} %get-tuple-element.196), channel_id=1, source_target_pairs={{0,1},{1,0},{2,3},{3,2},{4,5},{5,4},{6,7},{7,6},{8,9},{9,8},{10,11... | collective-permute-start | bytes 24584 | tf_op jit(solution)/shard_map/ppermute | solution.py:321
  77.0 2.2 %collective-permute-done.19.recvz = f32[2,8,128]{2,1,0:T(8,128)S(1)} collective-permute-done((f32[2,8,128]{2,1,0:T(8,128)S(1)}, f32[2,8,128]{2,1,0:T(8,128)S(1)}, u32[]{:S(2)}, u32[]{:S(2)}) %collective-permute-start.19) | collective-permute-done | bytes 8224 | tf_op jit(solution)/shard_map/ppermute | solution.py:321
  80.0 1.4 %collective-permute-start.20 = (f32[2,8,128]{2,1,0:T(8,128)S(1)}, f32[2,8,128]{2,1,0:T(8,128)S(1)}, u32[]{:S(2)}, u32[]{:S(2)}) collective-permute-start(f32[2,8,128]{2,1,0:T(8,128)S(1)} %get-tuple-element.214), channel_id=1, source_target_pairs={{0,1},{1,0},{2,3},{3,2},{4,5},{5,4},{6,7},{7,6},{8,9},{9,8},{10,11... | collective-permute-start | bytes 24584 | tf_op jit(solution)/shard_map/ppermute | solution.py:321
  81.4 0.8 collective-permute-done.20.recvc
  82.2 2.2 %collective-permute-done.21.recvz = f32[2,8,128]{2,1,0:T(8,128)S(1)} collective-permute-done((f32[2,8,128]{2,1,0:T(8,128)S(1)}, f32[2,8,128]{2,1,0:T(8,128)S(1)}, u32[]{:S(2)}, u32[]{:S(2)}) %collective-permute-start.21) | collective-permute-done | bytes 8224 | tf_op jit(solution)/shard_map/ppermute | solution.py:321
  85.2 1.4 %collective-permute-start.22 = (f32[2,8,128]{2,1,0:T(8,128)S(1)}, f32[2,8,128]{2,1,0:T(8,128)S(1)}, u32[]{:S(2)}, u32[]{:S(2)}) collective-permute-start(f32[2,8,128]{2,1,0:T(8,128)S(1)} %get-tuple-element.218), channel_id=1, source_target_pairs={{0,1},{1,0},{2,3},{3,2},{4,5},{5,4},{6,7},{7,6},{8,9},{9,8},{10,11... | collective-permute-start | bytes 24584 | tf_op jit(solution)/shard_map/ppermute | solution.py:321
  86.6 0.8 collective-permute-done.22.recvc
  87.4 2.2 %collective-permute-done.23.recvz = f32[2,8,128]{2,1,0:T(8,128)S(1)} collective-permute-done((f32[2,8,128]{2,1,0:T(8,128)S(1)}, f32[2,8,128]{2,1,0:T(8,128)S(1)}, u32[]{:S(2)}, u32[]{:S(2)}) %collective-permute-start.23) | collective-permute-done | bytes 8224 | tf_op jit(solution)/shard_map/ppermute | solution.py:321
  90.5 1.6 %collective-permute-start.24 = (f32[2,8,128]{2,1,0:T(8,128)S(1)}, f32[2,8,128]{2,1,0:T(8,128)S(1)}, u32[]{:S(2)}, u32[]{:S(2)}) collective-permute-start(f32[2,8,128]{2,1,0:T(8,128)S(1)} %get-tuple-element.222), channel_id=1, source_target_pairs={{0,1},{1,0},{2,3},{3,2},{4,5},{5,4},{6,7},{7,6},{8,9},{9,8},{10,11... | collective-permute-start | bytes 24584 | tf_op jit(solution)/shard_map/ppermute | solution.py:321
  92.1 0.8 collective-permute-done.24.recvc
  92.9 2.2 %collective-permute-done.25.recvz = f32[2,8,128]{2,1,0:T(8,128)S(1)} collective-permute-done((f32[2,8,128]{2,1,0:T(8,128)S(1)}, f32[2,8,128]{2,1,0:T(8,128)S(1)}, u32[]{:S(2)}, u32[]{:S(2)}) %collective-permute-start.25) | collective-permute-done | bytes 8224 | tf_op jit(solution)/shard_map/ppermute | solution.py:321
  95.9 1.4 %collective-permute-start.26 = (f32[2,8,128]{2,1,0:T(8,128)S(1)}, f32[2,8,128]{2,1,0:T(8,128)S(1)}, u32[]{:S(2)}, u32[]{:S(2)}) collective-permute-start(f32[2,8,128]{2,1,0:T(8,128)S(1)} %get-tuple-element.226), channel_id=1, source_target_pairs={{0,1},{1,0},{2,3},{3,2},{4,5},{5,4},{6,7},{7,6},{8,9},{9,8},{10,11... | collective-permute-start | bytes 24584 | tf_op jit(solution)/shard_map/ppermute | solution.py:321
  98.2 2.2 %collective-permute-done.27.recvz = f32[2,8,128]{2,1,0:T(8,128)S(1)} collective-permute-done((f32[2,8,128]{2,1,0:T(8,128)S(1)}, f32[2,8,128]{2,1,0:T(8,128)S(1)}, u32[]{:S(2)}, u32[]{:S(2)}) %collective-permute-start.27) | collective-permute-done | bytes 8224 | tf_op jit(solution)/shard_map/ppermute | solution.py:321
  101.2 1.4 %collective-permute-start.28 = (f32[2,8,128]{2,1,0:T(8,128)S(1)}, f32[2,8,128]{2,1,0:T(8,128)S(1)}, u32[]{:S(2)}, u32[]{:S(2)}) collective-permute-start(f32[2,8,128]{2,1,0:T(8,128)S(1)} %get-tuple-element.244), channel_id=1, source_target_pairs={{0,1},{1,0},{2,3},{3,2},{4,5},{5,4},{6,7},{7,6},{8,9},{9,8},{10,11... | collective-permute-start | bytes 24584 | tf_op jit(solution)/shard_map/ppermute | solution.py:321
  102.6 0.8 collective-permute-done.28.recvc
  103.4 2.2 %collective-permute-done.29.recvz = f32[2,8,128]{2,1,0:T(8,128)S(1)} collective-permute-done((f32[2,8,128]{2,1,0:T(8,128)S(1)}, f32[2,8,128]{2,1,0:T(8,128)S(1)}, u32[]{:S(2)}, u32[]{:S(2)}) %collective-permute-start.29) | collective-permute-done | bytes 8224 | tf_op jit(solution)/shard_map/ppermute | solution.py:321
  106.4 1.4 %collective-permute-start.30 = (f32[2,8,128]{2,1,0:T(8,128)S(1)}, f32[2,8,128]{2,1,0:T(8,128)S(1)}, u32[]{:S(2)}, u32[]{:S(2)}) collective-permute-start(f32[2,8,128]{2,1,0:T(8,128)S(1)} %get-tuple-element.248), channel_id=1, source_target_pairs={{0,1},{1,0},{2,3},{3,2},{4,5},{5,4},{6,7},{7,6},{8,9},{9,8},{10,11... | collective-permute-start | bytes 24584 | tf_op jit(solution)/shard_map/ppermute | solution.py:321
  107.8 0.8 collective-permute-done.30.recvc
  108.6 2.2 %collective-permute-done.31.recvz = f32[2,8,128]{2,1,0:T(8,128)S(1)} collective-permute-done((f32[2,8,128]{2,1,0:T(8,128)S(1)}, f32[2,8,128]{2,1,0:T(8,128)S(1)}, u32[]{:S(2)}, u32[]{:S(2)}) %collective-permute-start.31) | collective-permute-done | bytes 8224 | tf_op jit(solution)/shard_map/ppermute | solution.py:321
  111.6 1.4 %collective-permute-start.32 = (f32[2,8,128]{2,1,0:T(8,128)S(1)}, f32[2,8,128]{2,1,0:T(8,128)S(1)}, u32[]{:S(2)}, u32[]{:S(2)}) collective-permute-start(f32[2,8,128]{2,1,0:T(8,128)S(1)} %get-tuple-element.252), channel_id=1, source_target_pairs={{0,1},{1,0},{2,3},{3,2},{4,5},{5,4},{6,7},{7,6},{8,9},{9,8},{10,11... | collective-permute-start | bytes 24584 | tf_op jit(solution)/shard_map/ppermute | solution.py:321
  113.1 0.8 collective-permute-done.32.recvc
  113.9 2.2 %collective-permute-done.33.recvz = f32[2,8,128]{2,1,0:T(8,128)S(1)} collective-permute-done((f32[2,8,128]{2,1,0:T(8,128)S(1)}, f32[2,8,128]{2,1,0:T(8,128)S(1)}, u32[]{:S(2)}, u32[]{:S(2)}) %collective-permute-start.33) | collective-permute-done | bytes 8224 | tf_op jit(solution)/shard_map/ppermute | solution.py:321
  116.9 1.4 %collective-permute-start.34 = (f32[2,8,128]{2,1,0:T(8,128)S(1)}, f32[2,8,128]{2,1,0:T(8,128)S(1)}, u32[]{:S(2)}, u32[]{:S(2)}) collective-permute-start(f32[2,8,128]{2,1,0:T(8,128)S(1)} %get-tuple-element.255), channel_id=1, source_target_pairs={{0,1},{1,0},{2,3},{3,2},{4,5},{5,4},{6,7},{7,6},{8,9},{9,8},{10,11... | collective-permute-start | bytes 24584 | tf_op jit(solution)/shard_map/ppermute | solution.py:321
  119.1 2.2 %collective-permute-done.35.recvz = f32[2,8,128]{2,1,0:T(8,128)S(1)} collective-permute-done((f32[2,8,128]{2,1,0:T(8,128)S(1)}, f32[2,8,128]{2,1,0:T(8,128)S(1)}, u32[]{:S(2)}, u32[]{:S(2)}) %collective-permute-start.35) | collective-permute-done | bytes 8224 | tf_op jit(solution)/shard_map/ppermute | solution.py:321
  121.4 1.1 shard_map.152
  122.5 3.6 %all-to-all-start.1 = ((bf16[16,8,2688]{2,1,0:T(8,128)(2,1)}), bf16[16,8,2688]{2,1,0:T(8,128)(2,1)S(1)}, u32[]{:S(2)}, u32[]{:S(2)}) async-start(bf16[16,8,2688]{2,1,0:T(8,128)(2,1)} %bitcast.13), calls=%async_computation.1 | async-start | bytes 1376256 | tf_op jit(solution)/shard_map/all_to_all | solution.py:413
  126.1 11.9 %all-to-all-done.1 = bf16[16,8,2688]{2,1,0:T(8,128)(2,1)S(1)} async-done(((bf16[16,8,2688]{2,1,0:T(8,128)(2,1)}), bf16[16,8,2688]{2,1,0:T(8,128)(2,1)S(1)}, u32[]{:S(2)}, u32[]{:S(2)}) %all-to-all-start.1) | async-done | bytes 688160 | tf_op jit(solution)/shard_map/all_to_all | solution.py:413
  138.0 1.1 shard_map.153
  (67 shorter events, 16.0 us)
Async XLA Ops:
  0.6 9.0 %copy-start.3 = (f32[48]{0:T(128)S(1)}, f32[48]{0:T(128)}, u32[]{:S(2)}) copy-start(f32[48]{0:T(128)} %param.19) | copy-start | bytes 580
  0.6 9.0 %copy-start.4 = (f32[48]{0:T(128)S(1)}, f32[48]{0:T(128)}, u32[]{:S(2)}) copy-start(f32[48]{0:T(128)} %param.18) | copy-start | bytes 580
  0.7 9.1 %copy-start.5 = (s32[48]{0:T(128)S(1)}, s32[48]{0:T(128)}, u32[]{:S(2)}) copy-start(s32[48]{0:T(128)} %param.15) | copy-start | bytes 580
  2.0 7.9 %collective-permute-start.1 = (f16[128,128]{1,0:T(8,128)(2,1)S(1)}, f16[128,128]{1,0:T(8,128)(2,1)S(1)}, u32[]{:S(2)}, u32[]{:S(2)}) collective-permute-start(f16[128,128]{1,0:T(8,128)(2,1)S(1)} %get-tuple-element.275), channel_id=1, source_target_pairs={{0,15},{1,2},{2,1},{3,4},{4,3},{5,6},{6,5},{7,8},{8,7},{9,10},{10,... | collective-permute-start | bytes 98312 | tf_op jit(solution)/shard_map/ppermute | solution.py:321
  5.1 4.8 %collective-permute-start = (f16[128,128]{1,0:T(8,128)(2,1)S(1)}, f16[128,128]{1,0:T(8,128)(2,1)S(1)}, u32[]{:S(2)}, u32[]{:S(2)}) collective-permute-start(f16[128,128]{1,0:T(8,128)(2,1)S(1)} %get-tuple-element.274), channel_id=1, source_target_pairs={{0,1},{1,0},{2,3},{3,2},{4,5},{5,4},{6,7},{7,6},{8,9},{9,8},{10,11... | collective-permute-start | bytes 98312 | tf_op jit(solution)/shard_map/ppermute | solution.py:321
  10.9 17.9 %all-to-all-start = ((f16[16,8,2304]{2,1,0:T(8,128)(2,1)}), f16[16,8,2304]{2,1,0:T(8,128)(2,1)}, u32[]{:S(2)}, u32[]{:S(2)}) async-start(f16[16,8,2304]{2,1,0:T(8,128)(2,1)} %maximum_bitcast_fusion), calls=%async_computation | async-start | bytes 1179648 | tf_op jit(solution)/shard_map/all_to_all | solution.py:350
  18.5 1.9 %copy-start = (s32[48,128,128]{2,1,0:T(8,128)S(1)}, s32[48,128,128]{2,1,0:T(8,128)}, u32[]{:S(2)}) copy-start(s32[48,128,128]{2,1,0:T(8,128)} %param.17) | copy-start | bytes 9437188
  20.4 1.0 copy-start.1
  20.4 1.0 copy-start.2
  30.5 4.2 %collective-permute-start.2 = (f32[4,8,128]{2,1,0:T(8,128)S(1)}, f32[4,8,128]{2,1,0:T(8,128)S(1)}, u32[]{:S(2)}, u32[]{:S(2)}) collective-permute-start(f32[4,8,128]{2,1,0:T(8,128)S(1)} %get-tuple-element.148), channel_id=1, source_target_pairs={{0,1},{1,0},{2,3},{3,2},{4,5},{5,4},{6,7},{7,6},{8,9},{9,8},{10,11... | collective-permute-start | bytes 49160 | tf_op jit(solution)/shard_map/ppermute | solution.py:321
  32.8 3.2 %collective-permute-start.3 = (f32[4,8,128]{2,1,0:T(8,128)S(1)}, f32[4,8,128]{2,1,0:T(8,128)S(1)}, u32[]{:S(2)}, u32[]{:S(2)}) collective-permute-start(f32[4,8,128]{2,1,0:T(8,128)S(1)} %get-tuple-element.149), channel_id=1, source_target_pairs={{0,15},{1,2},{2,1},{3,4},{4,3},{5,6},{6,5},{7,8},{8,7},{9,10},{10,... | collective-permute-start | bytes 49160 | tf_op jit(solution)/shard_map/ppermute | solution.py:321
  36.7 3.3 %collective-permute-start.4 = (f32[2,8,128]{2,1,0:T(8,128)S(1)}, f32[2,8,128]{2,1,0:T(8,128)S(1)}, u32[]{:S(2)}, u32[]{:S(2)}) collective-permute-start(f32[2,8,128]{2,1,0:T(8,128)S(1)} %get-tuple-element.154), channel_id=1, source_target_pairs={{0,1},{1,0},{2,3},{3,2},{4,5},{5,4},{6,7},{7,6},{8,9},{9,8},{10,11... | collective-permute-start | bytes 24584 | tf_op jit(solution)/shard_map/ppermute | solution.py:321
  39.2 3.1 %collective-permute-start.5 = (f32[2,8,128]{2,1,0:T(8,128)S(1)}, f32[2,8,128]{2,1,0:T(8,128)S(1)}, u32[]{:S(2)}, u32[]{:S(2)}) collective-permute-start(f32[2,8,128]{2,1,0:T(8,128)S(1)} %get-tuple-element.155), channel_id=1, source_target_pairs={{0,15},{1,2},{2,1},{3,4},{4,3},{5,6},{6,5},{7,8},{8,7},{9,10},{10,... | collective-permute-start | bytes 24584 | tf_op jit(solution)/shard_map/ppermute | solution.py:321
  43.1 2.2 %collective-permute-start.6 = (f32[2,8,128]{2,1,0:T(8,128)S(1)}, f32[2,8,128]{2,1,0:T(8,128)S(1)}, u32[]{:S(2)}, u32[]{:S(2)}) collective-permute-start(f32[2,8,128]{2,1,0:T(8,128)S(1)} %get-tuple-element.160), channel_id=1, source_target_pairs={{0,1},{1,0},{2,3},{3,2},{4,5},{5,4},{6,7},{7,6},{8,9},{9,8},{10,11... | collective-permute-start | bytes 24584 | tf_op jit(solution)/shard_map/ppermute | solution.py:321
  44.5 3.1 %collective-permute-start.7 = (f32[2,8,128]{2,1,0:T(8,128)S(1)}, f32[2,8,128]{2,1,0:T(8,128)S(1)}, u32[]{:S(2)}, u32[]{:S(2)}) collective-permute-start(f32[2,8,128]{2,1,0:T(8,128)S(1)} %get-tuple-element.161), channel_id=1, source_target_pairs={{0,15},{1,2},{2,1},{3,4},{4,3},{5,6},{6,5},{7,8},{8,7},{9,10},{10,... | collective-permute-start | bytes 24584 | tf_op jit(solution)/shard_map/ppermute | solution.py:321
  48.3 2.2 %collective-permute-start.8 = (f32[2,8,128]{2,1,0:T(8,128)S(1)}, f32[2,8,128]{2,1,0:T(8,128)S(1)}, u32[]{:S(2)}, u32[]{:S(2)}) collective-permute-start(f32[2,8,128]{2,1,0:T(8,128)S(1)} %get-tuple-element.164), channel_id=1, source_target_pairs={{0,1},{1,0},{2,3},{3,2},{4,5},{5,4},{6,7},{7,6},{8,9},{9,8},{10,11... | collective-permute-start | bytes 24584 | tf_op jit(solution)/shard_map/ppermute | solution.py:321
  49.7 3.1 %collective-permute-start.9 = (f32[2,8,128]{2,1,0:T(8,128)S(1)}, f32[2,8,128]{2,1,0:T(8,128)S(1)}, u32[]{:S(2)}, u32[]{:S(2)}) collective-permute-start(f32[2,8,128]{2,1,0:T(8,128)S(1)} %get-tuple-element.165), channel_id=1, source_target_pairs={{0,15},{1,2},{2,1},{3,4},{4,3},{5,6},{6,5},{7,8},{8,7},{9,10},{10,... | collective-permute-start | bytes 24584 | tf_op jit(solution)/shard_map/ppermute | solution.py:321
  53.6 2.2 %collective-permute-start.10 = (f32[2,8,128]{2,1,0:T(8,128)S(1)}, f32[2,8,128]{2,1,0:T(8,128)S(1)}, u32[]{:S(2)}, u32[]{:S(2)}) collective-permute-start(f32[2,8,128]{2,1,0:T(8,128)S(1)} %get-tuple-element.168), channel_id=1, source_target_pairs={{0,1},{1,0},{2,3},{3,2},{4,5},{5,4},{6,7},{7,6},{8,9},{9,8},{10,11... | collective-permute-start | bytes 24584 | tf_op jit(solution)/shard_map/ppermute | solution.py:321
  55.0 3.1 %collective-permute-start.11 = (f32[2,8,128]{2,1,0:T(8,128)S(1)}, f32[2,8,128]{2,1,0:T(8,128)S(1)}, u32[]{:S(2)}, u32[]{:S(2)}) collective-permute-start(f32[2,8,128]{2,1,0:T(8,128)S(1)} %get-tuple-element.169), channel_id=1, source_target_pairs={{0,15},{1,2},{2,1},{3,4},{4,3},{5,6},{6,5},{7,8},{8,7},{9,10},{10,... | collective-permute-start | bytes 24584 | tf_op jit(solution)/shard_map/ppermute | solution.py:321
  58.8 2.4 %collective-permute-start.12 = (f32[2,8,128]{2,1,0:T(8,128)S(1)}, f32[2,8,128]{2,1,0:T(8,128)S(1)}, u32[]{:S(2)}, u32[]{:S(2)}) collective-permute-start(f32[2,8,128]{2,1,0:T(8,128)S(1)} %get-tuple-element.184), channel_id=1, source_target_pairs={{0,1},{1,0},{2,3},{3,2},{4,5},{5,4},{6,7},{7,6},{8,9},{9,8},{10,11... | collective-permute-start | bytes 24584 | tf_op jit(solution)/shard_map/ppermute | solution.py:321
  60.4 3.1 %collective-permute-start.13 = (f32[2,8,128]{2,1,0:T(8,128)S(1)}, f32[2,8,128]{2,1,0:T(8,128)S(1)}, u32[]{:S(2)}, u32[]{:S(2)}) collective-permute-start(f32[2,8,128]{2,1,0:T(8,128)S(1)} %get-tuple-element.185), channel_id=1, source_target_pairs={{0,15},{1,2},{2,1},{3,4},{4,3},{5,6},{6,5},{7,8},{8,7},{9,10},{10,... | collective-permute-start | bytes 24584 | tf_op jit(solution)/shard_map/ppermute | solution.py:321
  64.2 2.2 %collective-permute-start.14 = (f32[2,8,128]{2,1,0:T(8,128)S(1)}, f32[2,8,128]{2,1,0:T(8,128)S(1)}, u32[]{:S(2)}, u32[]{:S(2)}) collective-permute-start(f32[2,8,128]{2,1,0:T(8,128)S(1)} %get-tuple-element.188), channel_id=1, source_target_pairs={{0,1},{1,0},{2,3},{3,2},{4,5},{5,4},{6,7},{7,6},{8,9},{9,8},{10,11... | collective-permute-start | bytes 24584 | tf_op jit(solution)/shard_map/ppermute | solution.py:321
  65.6 3.1 %collective-permute-start.15 = (f32[2,8,128]{2,1,0:T(8,128)S(1)}, f32[2,8,128]{2,1,0:T(8,128)S(1)}, u32[]{:S(2)}, u32[]{:S(2)}) collective-permute-start(f32[2,8,128]{2,1,0:T(8,128)S(1)} %get-tuple-element.189), channel_id=1, source_target_pairs={{0,15},{1,2},{2,1},{3,4},{4,3},{5,6},{6,5},{7,8},{8,7},{9,10},{10,... | collective-permute-start | bytes 24584 | tf_op jit(solution)/shard_map/ppermute | solution.py:321
  69.5 2.2 %collective-permute-start.16 = (f32[2,8,128]{2,1,0:T(8,128)S(1)}, f32[2,8,128]{2,1,0:T(8,128)S(1)}, u32[]{:S(2)}, u32[]{:S(2)}) collective-permute-start(f32[2,8,128]{2,1,0:T(8,128)S(1)} %get-tuple-element.192), channel_id=1, source_target_pairs={{0,1},{1,0},{2,3},{3,2},{4,5},{5,4},{6,7},{7,6},{8,9},{9,8},{10,11... | collective-permute-start | bytes 24584 | tf_op jit(solution)/shard_map/ppermute | solution.py:321
  70.9 3.1 %collective-permute-start.17 = (f32[2,8,128]{2,1,0:T(8,128)S(1)}, f32[2,8,128]{2,1,0:T(8,128)S(1)}, u32[]{:S(2)}, u32[]{:S(2)}) collective-permute-start(f32[2,8,128]{2,1,0:T(8,128)S(1)} %get-tuple-element.193), channel_id=1, source_target_pairs={{0,15},{1,2},{2,1},{3,4},{4,3},{5,6},{6,5},{7,8},{8,7},{9,10},{10,... | collective-permute-start | bytes 24584 | tf_op jit(solution)/shard_map/ppermute | solution.py:321
  74.7 2.2 %collective-permute-start.18 = (f32[2,8,128]{2,1,0:T(8,128)S(1)}, f32[2,8,128]{2,1,0:T(8,128)S(1)}, u32[]{:S(2)}, u32[]{:S(2)}) collective-permute-start(f32[2,8,128]{2,1,0:T(8,128)S(1)} %get-tuple-element.196), channel_id=1, source_target_pairs={{0,1},{1,0},{2,3},{3,2},{4,5},{5,4},{6,7},{7,6},{8,9},{9,8},{10,11... | collective-permute-start | bytes 24584 | tf_op jit(solution)/shard_map/ppermute | solution.py:321
  76.1 3.1 %collective-permute-start.19 = (f32[2,8,128]{2,1,0:T(8,128)S(1)}, f32[2,8,128]{2,1,0:T(8,128)S(1)}, u32[]{:S(2)}, u32[]{:S(2)}) collective-permute-start(f32[2,8,128]{2,1,0:T(8,128)S(1)} %get-tuple-element.197), channel_id=1, source_target_pairs={{0,15},{1,2},{2,1},{3,4},{4,3},{5,6},{6,5},{7,8},{8,7},{9,10},{10,... | collective-permute-start | bytes 24584 | tf_op jit(solution)/shard_map/ppermute | solution.py:321
  80.0 2.2 %collective-permute-start.20 = (f32[2,8,128]{2,1,0:T(8,128)S(1)}, f32[2,8,128]{2,1,0:T(8,128)S(1)}, u32[]{:S(2)}, u32[]{:S(2)}) collective-permute-start(f32[2,8,128]{2,1,0:T(8,128)S(1)} %get-tuple-element.214), channel_id=1, source_target_pairs={{0,1},{1,0},{2,3},{3,2},{4,5},{5,4},{6,7},{7,6},{8,9},{9,8},{10,11... | collective-permute-start | bytes 24584 | tf_op jit(solution)/shard_map/ppermute | solution.py:321
  81.4 3.1 %collective-permute-start.21 = (f32[2,8,128]{2,1,0:T(8,128)S(1)}, f32[2,8,128]{2,1,0:T(8,128)S(1)}, u32[]{:S(2)}, u32[]{:S(2)}) collective-permute-start(f32[2,8,128]{2,1,0:T(8,128)S(1)} %get-tuple-element.215), channel_id=1, source_target_pairs={{0,15},{1,2},{2,1},{3,4},{4,3},{5,6},{6,5},{7,8},{8,7},{9,10},{10,... | collective-permute-start | bytes 24584 | tf_op jit(solution)/shard_map/ppermute | solution.py:321
  85.2 2.2 %collective-permute-start.22 = (f32[2,8,128]{2,1,0:T(8,128)S(1)}, f32[2,8,128]{2,1,0:T(8,128)S(1)}, u32[]{:S(2)}, u32[]{:S(2)}) collective-permute-start(f32[2,8,128]{2,1,0:T(8,128)S(1)} %get-tuple-element.218), channel_id=1, source_target_pairs={{0,1},{1,0},{2,3},{3,2},{4,5},{5,4},{6,7},{7,6},{8,9},{9,8},{10,11... | collective-permute-start | bytes 24584 | tf_op jit(solution)/shard_map/ppermute | solution.py:321
  86.6 3.1 %collective-permute-start.23 = (f32[2,8,128]{2,1,0:T(8,128)S(1)}, f32[2,8,128]{2,1,0:T(8,128)S(1)}, u32[]{:S(2)}, u32[]{:S(2)}) collective-permute-start(f32[2,8,128]{2,1,0:T(8,128)S(1)} %get-tuple-element.219), channel_id=1, source_target_pairs={{0,15},{1,2},{2,1},{3,4},{4,3},{5,6},{6,5},{7,8},{8,7},{9,10},{10,... | collective-permute-start | bytes 24584 | tf_op jit(solution)/shard_map/ppermute | solution.py:321
  90.5 2.5 %collective-permute-start.24 = (f32[2,8,128]{2,1,0:T(8,128)S(1)}, f32[2,8,128]{2,1,0:T(8,128)S(1)}, u32[]{:S(2)}, u32[]{:S(2)}) collective-permute-start(f32[2,8,128]{2,1,0:T(8,128)S(1)} %get-tuple-element.222), channel_id=1, source_target_pairs={{0,1},{1,0},{2,3},{3,2},{4,5},{5,4},{6,7},{7,6},{8,9},{9,8},{10,11... | collective-permute-start | bytes 24584 | tf_op jit(solution)/shard_map/ppermute | solution.py:321
  92.1 3.1 %collective-permute-start.25 = (f32[2,8,128]{2,1,0:T(8,128)S(1)}, f32[2,8,128]{2,1,0:T(8,128)S(1)}, u32[]{:S(2)}, u32[]{:S(2)}) collective-permute-start(f32[2,8,128]{2,1,0:T(8,128)S(1)} %get-tuple-element.223), channel_id=1, source_target_pairs={{0,15},{1,2},{2,1},{3,4},{4,3},{5,6},{6,5},{7,8},{8,7},{9,10},{10,... | collective-permute-start | bytes 24584 | tf_op jit(solution)/shard_map/ppermute | solution.py:321
  95.9 2.2 %collective-permute-start.26 = (f32[2,8,128]{2,1,0:T(8,128)S(1)}, f32[2,8,128]{2,1,0:T(8,128)S(1)}, u32[]{:S(2)}, u32[]{:S(2)}) collective-permute-start(f32[2,8,128]{2,1,0:T(8,128)S(1)} %get-tuple-element.226), channel_id=1, source_target_pairs={{0,1},{1,0},{2,3},{3,2},{4,5},{5,4},{6,7},{7,6},{8,9},{9,8},{10,11... | collective-permute-start | bytes 24584 | tf_op jit(solution)/shard_map/ppermute | solution.py:321
  97.3 3.1 %collective-permute-start.27 = (f32[2,8,128]{2,1,0:T(8,128)S(1)}, f32[2,8,128]{2,1,0:T(8,128)S(1)}, u32[]{:S(2)}, u32[]{:S(2)}) collective-permute-start(f32[2,8,128]{2,1,0:T(8,128)S(1)} %get-tuple-element.227), channel_id=1, source_target_pairs={{0,15},{1,2},{2,1},{3,4},{4,3},{5,6},{6,5},{7,8},{8,7},{9,10},{10,... | collective-permute-start | bytes 24584 | tf_op jit(solution)/shard_map/ppermute | solution.py:321
  101.2 2.2 %collective-permute-start.28 = (f32[2,8,128]{2,1,0:T(8,128)S(1)}, f32[2,8,128]{2,1,0:T(8,128)S(1)}, u32[]{:S(2)}, u32[]{:S(2)}) collective-permute-start(f32[2,8,128]{2,1,0:T(8,128)S(1)} %get-tuple-element.244), channel_id=1, source_target_pairs={{0,1},{1,0},{2,3},{3,2},{4,5},{5,4},{6,7},{7,6},{8,9},{9,8},{10,11... | collective-permute-start | bytes 24584 | tf_op jit(solution)/shard_map/ppermute | solution.py:321
  102.6 3.1 %collective-permute-start.29 = (f32[2,8,128]{2,1,0:T(8,128)S(1)}, f32[2,8,128]{2,1,0:T(8,128)S(1)}, u32[]{:S(2)}, u32[]{:S(2)}) collective-permute-start(f32[2,8,128]{2,1,0:T(8,128)S(1)} %get-tuple-element.245), channel_id=1, source_target_pairs={{0,15},{1,2},{2,1},{3,4},{4,3},{5,6},{6,5},{7,8},{8,7},{9,10},{10,... | collective-permute-start | bytes 24584 | tf_op jit(solution)/shard_map/ppermute | solution.py:321
  106.4 2.2 %collective-permute-start.30 = (f32[2,8,128]{2,1,0:T(8,128)S(1)}, f32[2,8,128]{2,1,0:T(8,128)S(1)}, u32[]{:S(2)}, u32[]{:S(2)}) collective-permute-start(f32[2,8,128]{2,1,0:T(8,128)S(1)} %get-tuple-element.248), channel_id=1, source_target_pairs={{0,1},{1,0},{2,3},{3,2},{4,5},{5,4},{6,7},{7,6},{8,9},{9,8},{10,11... | collective-permute-start | bytes 24584 | tf_op jit(solution)/shard_map/ppermute | solution.py:321
  107.8 3.1 %collective-permute-start.31 = (f32[2,8,128]{2,1,0:T(8,128)S(1)}, f32[2,8,128]{2,1,0:T(8,128)S(1)}, u32[]{:S(2)}, u32[]{:S(2)}) collective-permute-start(f32[2,8,128]{2,1,0:T(8,128)S(1)} %get-tuple-element.249), channel_id=1, source_target_pairs={{0,15},{1,2},{2,1},{3,4},{4,3},{5,6},{6,5},{7,8},{8,7},{9,10},{10,... | collective-permute-start | bytes 24584 | tf_op jit(solution)/shard_map/ppermute | solution.py:321
  111.6 2.2 %collective-permute-start.32 = (f32[2,8,128]{2,1,0:T(8,128)S(1)}, f32[2,8,128]{2,1,0:T(8,128)S(1)}, u32[]{:S(2)}, u32[]{:S(2)}) collective-permute-start(f32[2,8,128]{2,1,0:T(8,128)S(1)} %get-tuple-element.252), channel_id=1, source_target_pairs={{0,1},{1,0},{2,3},{3,2},{4,5},{5,4},{6,7},{7,6},{8,9},{9,8},{10,11... | collective-permute-start | bytes 24584 | tf_op jit(solution)/shard_map/ppermute | solution.py:321
  113.1 3.1 %collective-permute-start.33 = (f32[2,8,128]{2,1,0:T(8,128)S(1)}, f32[2,8,128]{2,1,0:T(8,128)S(1)}, u32[]{:S(2)}, u32[]{:S(2)}) collective-permute-start(f32[2,8,128]{2,1,0:T(8,128)S(1)} %get-tuple-element.253), channel_id=1, source_target_pairs={{0,15},{1,2},{2,1},{3,4},{4,3},{5,6},{6,5},{7,8},{8,7},{9,10},{10,... | collective-permute-start | bytes 24584 | tf_op jit(solution)/shard_map/ppermute | solution.py:321
  116.9 2.2 %collective-permute-start.34 = (f32[2,8,128]{2,1,0:T(8,128)S(1)}, f32[2,8,128]{2,1,0:T(8,128)S(1)}, u32[]{:S(2)}, u32[]{:S(2)}) collective-permute-start(f32[2,8,128]{2,1,0:T(8,128)S(1)} %get-tuple-element.255), channel_id=1, source_target_pairs={{0,1},{1,0},{2,3},{3,2},{4,5},{5,4},{6,7},{7,6},{8,9},{9,8},{10,11... | collective-permute-start | bytes 24584 | tf_op jit(solution)/shard_map/ppermute | solution.py:321
  118.3 3.1 %collective-permute-start.35 = (f32[2,8,128]{2,1,0:T(8,128)S(1)}, f32[2,8,128]{2,1,0:T(8,128)S(1)}, u32[]{:S(2)}, u32[]{:S(2)}) collective-permute-start(f32[2,8,128]{2,1,0:T(8,128)S(1)} %get-tuple-element.256), channel_id=1, source_target_pairs={{0,15},{1,2},{2,1},{3,4},{4,3},{5,6},{6,5},{7,8},{8,7},{9,10},{10,... | collective-permute-start | bytes 24584 | tf_op jit(solution)/shard_map/ppermute | solution.py:321
  122.5 15.5 %all-to-all-start.1 = ((bf16[16,8,2688]{2,1,0:T(8,128)(2,1)}), bf16[16,8,2688]{2,1,0:T(8,128)(2,1)S(1)}, u32[]{:S(2)}, u32[]{:S(2)}) async-start(bf16[16,8,2688]{2,1,0:T(8,128)(2,1)} %bitcast.13), calls=%async_computation.1 | async-start | bytes 1376256 | tf_op jit(solution)/shard_map/all_to_all | solution.py:413
